TPU v7x, 128 devices: a whole 4x4x4 slice. The times are simulated.
128 devices in a mesh: dp: 16 (over x_lo, z, core), expert: 8 (over x_hi, y).
Axes of the slice: x: 4 (x_hi: 2, x_lo: 2; x = x_hi * 2 + x_lo), y: 4, z: 4, core: 2. Of those that a mesh axis runs over, the one named last changes fastest.
Arguments:
- value_input: bfloat16 [16384, 4096], P(('dp', 'expert')), may hold values from -2.5 to 2.5
- value_grad: bfloat16 [16384, 512], P(('dp', 'expert')), may hold values from -0.625 to 0.625
- value_weight: bfloat16 [4096, 512], P('dp'), may hold values from -0.75 to 0.75
- out_grad: bfloat16 [16384, 4096], P(('dp', 'expert')), may hold values from -6 to 6
- route_ids: int32 [16384, 8], P(('dp', 'expert')), may hold values from 0 to 127, as said below
- route_slots: int32 [16384, 8], P(('dp', 'expert')), may hold values from 0 to 7, as said below
- seq_lengths: int32 [128], P(('dp', 'expert')), may hold values from 16 to 128, as said below
- route_weights: bfloat16 [16384, 8], P(('dp', 'expert')), may hold values from 0.019897461 to 0.5
- gate_act: bfloat16 [128, 128, 8, 768], P(('dp', 'expert')), may hold values from -8 to 8
- up_act: bfloat16 [128, 128, 8, 768], P(('dp', 'expert')), may hold values from -6 to 6
- w_gate: bfloat16 [128, 4096, 768], P(('dp', 'expert')), may hold values from -0.09375 to 0.09375
- w_up: bfloat16 [128, 4096, 768], P(('dp', 'expert')), may hold values from -0.09375 to 0.09375
- w_down: bfloat16 [128, 768, 4096], P(('dp', 'expert')), may hold values from -0.21875 to 0.21875
Outputs:
- moe_input_grad: bfloat16 [16384, 4096], P(('dp', 'expert'))
- weight_grad: bfloat16 [16384, 8], P(('dp', 'expert'))
- value_input_grad: bfloat16 [16384, 4096], P(('dp', 'expert'))
- value_weight_grad: float32 [4096, 512], P(('dp', 'expert'))
Inputs may be any that keep to these rules, and one draw needn't show every extreme that they name: `route_ids`: each token names 8 different experts; the 128 tokens of one device name every expert exactly 8 times. `route_slots`: among the tokens of one device, the choices that name one expert hold the slots 0 to 7 once each, in order of token and then of choice. `seq_lengths`: some sequence has all 128 tokens live.
All inputs are finite; a program needn't handle non-finite values.
Results may differ from a plain program's by a relative error of at most 0.0057.
Values may be sent and summed in bfloat16 or wider, within the bound.
No kernel may reach another device: no remote copies, remote signals or barrier semaphores. Data moves between devices by JAX's collectives and lax.ppermute only.
A program may use at most 192 MiB of HBM per device.

v0:
```python
import jax
import jax.numpy as jnp
from jax import lax
from jax.sharding import PartitionSpec as P


def expert_grads(routed_rows, routed_weights, gate_saved, up_saved, gate_proj, up_proj, down_proj):
    back_proj = jnp.einsum(
        "erd,efd->erf", routed_rows, down_proj, preferred_element_type=jnp.float32
    )
    gate_pre = gate_saved.astype(jnp.float32)
    up_pre = up_saved.astype(jnp.float32)
    gate_sigmoid = jax.nn.sigmoid(gate_pre)
    gate_silu = gate_pre * gate_sigmoid
    weight_grads = jnp.sum(back_proj * gate_silu * up_pre, axis=2).astype(jnp.bfloat16)
    scaled = routed_weights.astype(jnp.float32)[:, :, None] * back_proj
    up_grad = (scaled * gate_silu).astype(jnp.bfloat16)
    gate_grad = (scaled * up_pre * gate_sigmoid * (1.0 + gate_pre * (1.0 - gate_sigmoid))).astype(
        jnp.bfloat16
    )
    input_grads = jnp.einsum(
        "erf,edf->erd", gate_grad, gate_proj, preferred_element_type=jnp.float32
    )
    input_grads = input_grads + jnp.einsum(
        "erf,edf->erd", up_grad, up_proj, preferred_element_type=jnp.float32
    )
    return (input_grads.astype(jnp.bfloat16), weight_grads)


def body(
    value_input,
    value_grad,
    value_weight,
    out_grad,
    route_ids,
    route_slots,
    seq_lengths,
    route_weights,
    gate_act,
    up_act,
    w_gate,
    w_up,
    w_down,
):
    tok_count, model_width = out_grad.shape
    top_count = route_ids.shape[1]
    local_experts = w_gate.shape[0]
    dp_count = lax.axis_size("dp")
    expert_count = lax.axis_size("expert")
    all_experts = local_experts * dp_count * expert_count
    source_count = gate_act.shape[1]
    capacity = gate_act.shape[2]
    ffw_width = gate_act.shape[3]
    live_mask = jnp.arange(tok_count, dtype=jnp.int32) < seq_lengths[0]
    target = jnp.where(live_mask[:, None], route_ids, all_experts)
    spread_rows = jnp.broadcast_to(out_grad[:, None, :], (tok_count, top_count, model_width))
    send_rows = (
        jnp.zeros((all_experts, capacity, model_width), jnp.bfloat16)
        .at[target, route_slots]
        .set(spread_rows, mode="drop")
    )
    send_weights = (
        jnp.zeros((all_experts, capacity), jnp.bfloat16)
        .at[target, route_slots]
        .set(route_weights, mode="drop")
    )
    routed_rows, routed_weights = (
        lax.all_to_all(send_rows, ("dp", "expert"), split_axis=0, concat_axis=1, tiled=True),
        lax.all_to_all(send_weights, ("dp", "expert"), split_axis=0, concat_axis=1, tiled=True),
    )
    gate_saved = gate_act.reshape(local_experts, source_count * capacity, ffw_width)
    up_saved = up_act.reshape(local_experts, source_count * capacity, ffw_width)
    input_grads, weight_grads = expert_grads(
        routed_rows, routed_weights, gate_saved, up_saved, w_gate, w_up, w_down
    )
    slot_inputs, slot_weights = (
        lax.all_to_all(input_grads, ("dp", "expert"), split_axis=1, concat_axis=0, tiled=True),
        lax.all_to_all(weight_grads, ("dp", "expert"), split_axis=1, concat_axis=0, tiled=True),
    )
    safe_ids = jnp.where(live_mask[:, None], route_ids, 0)
    picked = slot_inputs[safe_ids, route_slots]
    live_weights = jnp.broadcast_to(live_mask[:, None], (tok_count, top_count)).astype(jnp.bfloat16)
    moe_input_grad = jnp.einsum(
        "tk,tkd->td", live_weights, picked, preferred_element_type=jnp.float32
    ).astype(jnp.bfloat16)
    chosen = slot_weights[safe_ids, route_slots]
    weight_grad = jnp.where(live_mask[:, None], chosen, jnp.zeros((), chosen.dtype))
    value_input_grad = jnp.einsum(
        "tk,rk->tr",
        value_grad,
        lax.all_gather(value_weight, "dp", axis=0, tiled=True),
        preferred_element_type=jnp.float32,
    ).astype(jnp.bfloat16)
    value_weight_grad = lax.psum_scatter(
        jnp.einsum("tr,tk->rk", value_input, value_grad, preferred_element_type=jnp.float32),
        ("dp", "expert"),
        scatter_dimension=0,
        tiled=True,
    )
    return (moe_input_grad, weight_grad, value_input_grad, value_weight_grad)


def solution(mesh):
    return jax.shard_map(
        body,
        mesh=mesh,
        in_specs=(
            P(("dp", "expert"), None),
            P(("dp", "expert"), None),
            P("dp", None),
            P(("dp", "expert"), None),
            P(("dp", "expert"), None),
            P(("dp", "expert"), None),
            P(("dp", "expert")),
            P(("dp", "expert"), None),
            P(("dp", "expert"), None, None, None),
            P(("dp", "expert"), None, None, None),
            P(("dp", "expert"), None, None),
            P(("dp", "expert"), None, None),
            P(("dp", "expert"), None, None),
        ),
        out_specs=(
            P(("dp", "expert"), None),
            P(("dp", "expert"), None),
            P(("dp", "expert"), None),
            P(("dp", "expert"), None),
        ),
        check_vma=False,
    )
```

profile of v0, /device:TPU:0, one launch (start us, length us, event | category | flops | bytes accessed | tf_op | source)
XLA Modules:
  0.0 815.8 jit_solution(17227868202378087919)
XLA Ops:
  10.8 0.7 multiply_reduce_fusion.2
  11.8 0.8 copy.131
  12.7 7.6 scatter_custom_fusion
  20.3 0.8 copy.132
  21.0 11.4 %all-to-all-start = ((bf16[128,1,8]{2,1,0:T(2,128)(2,1)}), bf16[128,1,8]{2,1,0:T(2,128)(2,1)S(1)}, u32[]{:S(2)}, u32[]{:S(2)}) async-start(bf16[128,1,8]{2,1,0:T(2,128)(2,1)} %copy.132), calls=%async_computation | async-start | bytes 131072 | tf_op jit(solution)/shard_map/all_to_all | solution.py:69
  32.7 15.9 %scatter_custom_fusion.1 = bf16[1024,4096]{1,0:T(8,128)(2,1)} fusion(s32[1024]{0:T(1024)S(1)} %reshape.140, bf16[]{:T(256)} %constant.6.clone.1, bf16[128,4096]{1,0:T(8,128)(2,1)S(1)} %copy-done), kind=kCustom, calls=%fused_computation.11 | custom fusion | bytes 9437186
  48.6 10.4 %all-to-all-start.1 = ((bf16[128,8,4096]{2,1,0:T(8,128)(2,1)}), bf16[128,8,4096]{2,1,0:T(8,128)(2,1)}, u32[]{:S(2)}, u32[]{:S(2)}) async-start(bf16[128,8,4096]{2,1,0:T(8,128)(2,1)} %bitcast.69), calls=%async_computation.1 | async-start | bytes 16777216 | tf_op jit(solution)/shard_map/all_to_all | solution.py:68
  59.7 4.5 fusion.29
  64.2 1.4 copy-done.3
  65.6 2.0 bitcast_convert_fusion.2
  67.5 3.6 copy.135
  71.2 2.0 bitcast_convert_fusion.1
  73.2 3.7 copy.134
  77.1 91.2 %all-to-all-done.1 = bf16[128,8,4096]{2,1,0:T(8,128)(2,1)} async-done(((bf16[128,8,4096]{2,1,0:T(8,128)(2,1)}), bf16[128,8,4096]{2,1,0:T(8,128)(2,1)}, u32[]{:S(2)}, u32[]{:S(2)}) %all-to-all-start.1) | async-done | bytes 8388640 | tf_op jit(solution)/shard_map/all_to_all | solution.py:68
  168.3 14.1 %multiply_reduce_fusion = (bf16[1024]{0:T(1024)(128)(2,1)S(1)}, f32[1024,768]{0,1:T(8,128)}) fusion(f32[1024,768]{0,1:T(8,128)} %copy.134, f32[1024,768]{0,1:T(8,128)} %copy.135, bf16[1,768,4096]{2,1,0:T(8,128)(2,1)} %param.25, bf16[128,8,4096]{2,1,0:T(8,128)(2,1)} %all-to-all-done.1), kind=kOutput, calls=%fused_computation.20 | convolution fusion | flops 6447954944 | bytes 24119296 | tf_op jit(solution)/shard_map/erd,efd->erf/dot_general | solution.py:8
  182.4 0.8 convert_element_type.79
  183.2 10.9 %all-to-all-start.3 = ((bf16[1,128,8]{2,0,1:T(2,128)(2,1)}), bf16[1,128,8]{2,0,1:T(2,128)(2,1)S(1)}, u32[]{:S(2)}, u32[]{:S(2)}) async-start(bf16[1,128,8]{2,0,1:T(2,128)(2,1)} %convert_element_type.79), calls=%async_computation.3 | async-start | bytes 131072 | tf_op jit(solution)/shard_map/all_to_all | solution.py:78
  194.0 16.7 %fusion.8 = f32[1024,4096]{1,0:T(8,128)} fusion(bf16[1,4096,768]{2,1,0:T(8,128)(2,1)} %param.23, f32[1024,768]{0,1:T(8,128)} %copy.135, f32[1024,768]{0,1:T(8,128)} %copy.134, f32[1024,768]{0,1:T(8,128)} %get-tuple-element.33, f32[1024]{0:T(1024)S(1)} %reshape.119), kind=kOutput, calls=%fused_computation.14 | convolution fusion | flops 6451101696 | bytes 32509952 | tf_op jit(solution)/shard_map/erf,edf->erd/dot_general | solution.py:21
  210.7 15.3 %fusion = bf16[1,1024,4096]{2,1,0:T(8,128)(2,1)} fusion(f32[1024,4096]{1,0:T(8,128)} %fusion.8, bf16[1,4096,768]{2,1,0:T(8,128)(2,1)} %param.24, f32[1024,768]{0,1:T(8,128)} %get-tuple-element.33, f32[1024]{0:T(1024)S(1)} %reshape.119, f32[1024,768]{0,1:T(8,128)} %copy.135), kind=kOutput, calls=%fused_computation.5 | convolution fusion | flops 6456344576 | bytes 37752832 | tf_op jit(solution)/shard_map/erf,edf->erd/dot_general | solution.py:24
  226.1 20.1 %copy.152 = bf16[1,1024,4096]{2,0,1:T(2,128)(2,1)} copy(bf16[1,1024,4096]{2,1,0:T(8,128)(2,1)} %fusion) | data formatting | bytes 16777216 | tf_op jit(solution)/shard_map/convert_element_type | solution.py:27
  246.7 52.5 %reduce.13 = bf16[1024,4096]{1,0:T(8,128)(2,1)} reduce(bf16[1024,1,4096]{2,1,0:T(2,128)(2,1)} %bitcast.68, bf16[]{:T(256)} %broadcast.108), dimensions={1}, to_apply=%bitcast.63.reduce_sub_computation | reduce | bytes 16777218
  299.1 15.9 %reshape.164 = bf16[128,2,16384]{2,1,0:T(2,128)(2,1)} reshape(bf16[1024,4096]{1,0:T(8,128)(2,1)} %reduce.13) | data formatting | bytes 16777216
  315.0 10.5 %all-to-all-start.2 = ((bf16[128,2,16384]{2,1,0:T(2,128)(2,1)}), bf16[128,2,16384]{2,1,0:T(2,128)(2,1)}, u32[]{:S(2)}, u32[]{:S(2)}) async-start(bf16[128,2,16384]{2,1,0:T(2,128)(2,1)} %reshape.164), calls=%async_computation.2 | async-start | bytes 16777216 | tf_op jit(solution)/shard_map/all_to_all | solution.py:77
  325.8 4.6 convolution_convert_fusion
  330.5 8.2 %gather_fusion.1 = bf16[1024]{0:T(1024)(128)(2,1)S(1)} fusion(bf16[128,8]{0,1:T(8,128)(2,1)S(1)} %bitcast.65, s32[1024]{0:T(1024)S(1)} %reshape.122), kind=kCustom, calls=%fused_computation.1 | custom fusion | bytes 12288 | tf_op jit(solution)/shard_map/gather | solution.py:86
  339.5 97.7 %all-to-all-done.2 = bf16[128,2,16384]{2,1,0:T(2,128)(2,1)} async-done(((bf16[128,2,16384]{2,1,0:T(2,128)(2,1)}), bf16[128,2,16384]{2,1,0:T(2,128)(2,1)}, u32[]{:S(2)}, u32[]{:S(2)}) %all-to-all-start.2) | async-done | bytes 8388640 | tf_op jit(solution)/shard_map/all_to_all | solution.py:77
  437.2 38.4 %reshape.165 = bf16[1024,1,4096]{2,1,0:T(2,128)(2,1)} reshape(bf16[128,2,16384]{2,1,0:T(2,128)(2,1)} %all-to-all-done.2) | data formatting | bytes 16777216
  475.6 16.8 %copy.150 = bf16[1,1024,4096]{2,1,0:T(8,128)(2,1)} copy(bf16[1,1024,4096]{2,0,1:T(2,128)(2,1)} %bitcast.67) | data formatting | bytes 16777216
  492.5 42.7 %gather_fusion = bf16[1024,4096]{1,0:T(8,128)(2,1)} fusion(bf16[128,8,4096]{2,1,0:T(8,128)(2,1)} %bitcast.66, s32[1024]{0:T(1024)S(1)} %reshape.122), kind=kCustom, calls=%fused_computation | custom fusion | bytes 16785408 | tf_op jit(solution)/shard_map/gather | solution.py:81
  535.2 5.9 fusion.1
  541.1 2.1 copy.151
  543.2 264.9 %reduce-scatter.2.cloned.1.call-done = f32[32,512]{1,0:T(8,128)} async-done(((f32[4096,512]{1,0:T(8,128)}), f32[32,512]{1,0:T(8,128)}) %reduce-scatter.2.cloned.1.call-update) | async-done | bytes 65552 | tf_op jit(solution)/shard_map/reduce_scatter | solution.py:94
  (41 shorter events, 5.1 us)
Async XLA Ops:
  8.0 24.7 %copy-start = (bf16[128,4096]{1,0:T(8,128)(2,1)S(1)}, bf16[128,4096]{1,0:T(8,128)(2,1)}, u32[]{:S(2)}) copy-start(bf16[128,4096]{1,0:T(8,128)(2,1)} %param.16) | copy-start | bytes 3145732
  8.0 317.7 %all-gather.2.cloned.1.call-start = ((), (), s32[]{:S(2)}) async-start(), calls=%async_computation.5 | async-start | bytes 4456448 | tf_op jit(solution)/shard_map/all_gather | solution.py:91
  21.0 27.6 %all-to-all-start = ((bf16[128,1,8]{2,1,0:T(2,128)(2,1)}), bf16[128,1,8]{2,1,0:T(2,128)(2,1)S(1)}, u32[]{:S(2)}, u32[]{:S(2)}) async-start(bf16[128,1,8]{2,1,0:T(2,128)(2,1)} %copy.132), calls=%async_computation | async-start | bytes 131072 | tf_op jit(solution)/shard_map/all_to_all | solution.py:69
  48.6 11.0 %copy-start.2 = (bf16[128,4096]{1,0:T(8,128)(2,1)S(1)}, bf16[128,4096]{1,0:T(8,128)(2,1)}, u32[]{:S(2)}) copy-start(bf16[128,4096]{1,0:T(8,128)(2,1)} %param.13) | copy-start | bytes 3145732
  48.6 11.0 %copy-start.5 = (bf16[128,512]{1,0:T(8,128)(2,1)S(1)}, bf16[128,512]{1,0:T(8,128)(2,1)}, u32[]{:S(2)}) copy-start(bf16[128,512]{1,0:T(8,128)(2,1)} %param.14) | copy-start | bytes 393220
  48.6 119.7 %all-to-all-start.1 = ((bf16[128,8,4096]{2,1,0:T(8,128)(2,1)}), bf16[128,8,4096]{2,1,0:T(8,128)(2,1)}, u32[]{:S(2)}, u32[]{:S(2)}) async-start(bf16[128,8,4096]{2,1,0:T(8,128)(2,1)} %bitcast.69), calls=%async_computation.1 | async-start | bytes 16777216 | tf_op jit(solution)/shard_map/all_to_all | solution.py:68
  59.1 749.0 %reduce-scatter.2.cloned.1.call-start = ((), (), s32[]{:S(2)}) async-start(), calls=%async_computation.6 | async-start | bytes 8454144 | tf_op jit(solution)/shard_map/reduce_scatter | solution.py:94
  64.1 1.4 copy-start.3
  67.5 3.6 copy-start.4
  183.2 131.9 %all-to-all-start.3 = ((bf16[1,128,8]{2,0,1:T(2,128)(2,1)}), bf16[1,128,8]{2,0,1:T(2,128)(2,1)S(1)}, u32[]{:S(2)}, u32[]{:S(2)}) async-start(bf16[1,128,8]{2,0,1:T(2,128)(2,1)} %convert_element_type.79), calls=%async_computation.3 | async-start | bytes 131072 | tf_op jit(solution)/shard_map/all_to_all | solution.py:78
  315.0 10.5 %copy-start.6 = (s32[128,8]{0,1:T(8,128)S(1)}, s32[128,8]{0,1:T(8,128)}, u32[]{:S(2)}) copy-start(s32[128,8]{0,1:T(8,128)} %param.17) | copy-start | bytes 12292
  315.0 10.5 %copy-start.7 = (s32[128,8]{0,1:T(8,128)S(1)}, s32[128,8]{0,1:T(8,128)}, u32[]{:S(2)}) copy-start(s32[128,8]{0,1:T(8,128)} %param.18) | copy-start | bytes 12292
  315.0 122.2 %all-to-all-start.2 = ((bf16[128,2,16384]{2,1,0:T(2,128)(2,1)}), bf16[128,2,16384]{2,1,0:T(2,128)(2,1)}, u32[]{:S(2)}, u32[]{:S(2)}) async-start(bf16[128,2,16384]{2,1,0:T(2,128)(2,1)} %reshape.164), calls=%async_computation.2 | async-start | bytes 16777216 | tf_op jit(solution)/shard_map/all_to_all | solution.py:77
  535.2 272.9 %copy-start.1 = (bf16[128,4096]{1,0:T(8,128)(2,1)S(1)}, bf16[128,4096]{1,0:T(8,128)(2,1)}, u32[]{:S(2)}) copy-start(bf16[128,4096]{1,0:T(8,128)(2,1)} %param.16) | copy-start | bytes 3145732
Sparse Core Ops, SparseCore 0:
  10.6 40.3 all-gather.1
Sparse Core Ops, SparseCore 1:
  64.3 743.8 reduce-scatter.1
where the time goes:
time: 823 us; the launch traced here: 816 us
  waiting for transfers between devices  455 us (55%)
  local copies, waits for them, and re-layouts  180 us (22%)
  matrix products  61.2 us (7%)
  other arithmetic  59.4 us (7%)
  starting transfers between devices  43.8 us (5%)
  between operations  16.5 us (2%)
    reduce_scatter x1, waiting for transfers between devices, body(): lax.psum_scatter(jnp.einsum('tr,tk->rk', value_input, value_grad, preferr...  265 us
    unnamed x28, local copies, waits for them, and re-layouts  97.9 us
    all_to_all x1, waiting for transfers between devices, body(): lax.all_to_all(input_grads, ('dp', 'expert'), split_axis=1, concat_axis=0...  97.7 us
    all_to_all x1, waiting for transfers between devices, body(): lax.all_to_all(send_rows, ('dp', 'expert'), split_axis=0, concat_axis=1,...  91.2 us
    unnamed x4, other arithmetic  53.9 us
    gather x1, local copies, waits for them, and re-layouts, body(): picked = slot_inputs[safe_ids, route_slots]  42.7 us
    convert_element_type x1, local copies, waits for them, and re-layouts, expert_grads(): return (input_grads.astype(jnp.bfloat16), weight_grads)  20.1 us
    dot_general x1, matrix products, expert_grads(): jnp.einsum('erf,edf->erd', gate_grad, gate_proj, preferred_element_type=j...  16.7 us
  transfers between devices with their start and end apart: 6, of which 3 were waited for; matrix products, arithmetic and copies ran while one was open for 37% of the time, Pallas kernels for 0%

commit v1 on v0

v1 whole, which is shorter than its diff:
```python
import functools

import jax
import jax.numpy as jnp
from jax import lax
from jax.experimental import pallas as pl
from jax.experimental.pallas import tpu as pltpu
from jax.sharding import PartitionSpec as P

AXES = ("dp", "expert")
MIB = 1024 * 1024
NT = (((1,), (1,)), ((), ()))


def dot_nt(left, right):
    return lax.dot_general(left, right, NT, preferred_element_type=jnp.float32)


def exchange(array, axes):
    return lax.all_to_all(array, axes, split_axis=0, concat_axis=0, tiled=True)


def rows_kernel(slot_ref, grad_ref, out_ref):
    rows, width = out_ref.shape
    tokens = grad_ref.shape[0]
    slot = lax.broadcasted_iota(jnp.int32, (rows, tokens), 0) + pl.program_id(0) * rows
    hit = slot_ref[0:1, :] == slot
    for k in range(1, slot_ref.shape[0]):
        hit = hit | (slot_ref[k : k + 1, :] == slot)
    pick = jnp.where(hit, 1.0, 0.0).astype(jnp.bfloat16)
    step = min(width, 1024)
    for c in range(0, width, step):
        out_ref[:, c : c + step] = jnp.dot(
            pick, grad_ref[:, c : c + step], preferred_element_type=jnp.float32
        ).astype(jnp.bfloat16)


def build_rows(slot_t, out_grad, start, width, slots):
    tokens = out_grad.shape[0]
    rows = 256
    return pl.pallas_call(
        rows_kernel,
        grid=(slots // rows,),
        in_specs=[
            pl.BlockSpec(slot_t.shape, lambda i: (0, 0)),
            pl.BlockSpec((tokens, width), lambda i: (0, start // width)),
        ],
        out_specs=pl.BlockSpec((rows, width), lambda i: (i, 0)),
        out_shape=jax.ShapeDtypeStruct((slots, width), jnp.bfloat16),
        compiler_params=pltpu.CompilerParams(vmem_limit_bytes=32 * MIB),
        cost_estimate=pl.CostEstimate(
            flops=2 * slots * tokens * width, bytes_accessed=2 * (slots + tokens) * width, transcendentals=0
        ),
        name="build_rows",
    )(slot_t, out_grad)


def hidden_kernel(x_ref, down_ref, gate_ref, up_ref, hidden_ref, score_ref, acc_ref):
    k = pl.program_id(0)
    rows, ffw = acc_ref.shape
    part = 256

    @pl.when(k == 0)
    def _():
        acc_ref[...] = jnp.zeros_like(acc_ref)

    for r in range(0, rows, part):
        acc_ref[r : r + part, :] += dot_nt(x_ref[r : r + part, :], down_ref[...])

    @pl.when(k == pl.num_programs(0) - 1)
    def _():
        for r in range(0, rows, part):
            here = slice(r, r + part)
            back = acc_ref[here, :]
            gate = gate_ref[here, :].astype(jnp.float32)
            up = up_ref[here, :].astype(jnp.float32)
            sig = 1.0 / (1.0 + jnp.exp(-gate))
            silu = gate * sig
            up_grad = back * silu
            hidden_ref[here, ffw:] = up_grad.astype(jnp.bfloat16)
            hidden_ref[here, :ffw] = (back * up * sig * (1.0 + gate * (1.0 - sig))).astype(jnp.bfloat16)
            term = up_grad * up
            lanes = term[:, 0:128]
            for c in range(128, ffw, 128):
                lanes = lanes + term[:, c : c + 128]
            score_ref[:, here] = jnp.sum(lanes.T, axis=0, keepdims=True)


def hidden_grads(rows_in, down, gate, up):
    slots, width = rows_in.shape
    ffw = down.shape[0]
    block = 512
    return pl.pallas_call(
        hidden_kernel,
        grid=(width // block,),
        in_specs=[
            pl.BlockSpec((slots, block), lambda k: (0, k)),
            pl.BlockSpec((ffw, block), lambda k: (0, k)),
            pl.BlockSpec((slots, ffw), lambda k: (0, 0)),
            pl.BlockSpec((slots, ffw), lambda k: (0, 0)),
        ],
        out_specs=[
            pl.BlockSpec((slots, 2 * ffw), lambda k: (0, 0)),
            pl.BlockSpec((1, slots), lambda k: (0, 0)),
        ],
        out_shape=[
            jax.ShapeDtypeStruct((slots, 2 * ffw), jnp.bfloat16),
            jax.ShapeDtypeStruct((1, slots), jnp.float32),
        ],
        scratch_shapes=[pltpu.VMEM((slots, ffw), jnp.float32)],
        compiler_params=pltpu.CompilerParams(vmem_limit_bytes=48 * MIB),
        cost_estimate=pl.CostEstimate(
            flops=2 * slots * width * ffw,
            bytes_accessed=2 * (slots * width + ffw * width + 4 * slots * ffw),
            transcendentals=slots * ffw,
        ),
        name="hidden_grads",
    )(rows_in, down, gate, up)


def slot_kernel(hidden_ref, gate_w_ref, up_w_ref, out_ref):
    ffw = gate_w_ref.shape[1]
    rows = out_ref.shape[0]
    part = 256
    for r in range(0, rows, part):
        here = slice(r, r + part)
        out_ref[here, :] = (
            dot_nt(hidden_ref[here, :ffw], gate_w_ref[...]) + dot_nt(hidden_ref[here, ffw:], up_w_ref[...])
        ).astype(jnp.bfloat16)


def slot_grads(hidden, gate_w, up_w, start, width):
    slots = hidden.shape[0]
    ffw = gate_w.shape[1]
    block = 512
    first = start // block
    return pl.pallas_call(
        slot_kernel,
        grid=(width // block,),
        in_specs=[
            pl.BlockSpec((slots, 2 * ffw), lambda j: (0, 0)),
            pl.BlockSpec((block, ffw), lambda j: (first + j, 0)),
            pl.BlockSpec((block, ffw), lambda j: (first + j, 0)),
        ],
        out_specs=pl.BlockSpec((slots, block), lambda j: (0, j)),
        out_shape=jax.ShapeDtypeStruct((slots, width), jnp.bfloat16),
        compiler_params=pltpu.CompilerParams(vmem_limit_bytes=48 * MIB),
        cost_estimate=pl.CostEstimate(
            flops=4 * slots * width * ffw,
            bytes_accessed=2 * (slots * width + 2 * ffw * width + 2 * slots * ffw),
            transcendentals=0,
        ),
        name="slot_grads",
    )(hidden, gate_w, up_w)


def combine_kernel(slot_ref, weight_ref, rows_ref, out_ref, mix_ref):
    @pl.when(pl.program_id(0) == 0)
    def _():
        slot = lax.broadcasted_iota(jnp.int32, mix_ref.shape, 1)
        mix = jnp.zeros(mix_ref.shape, jnp.float32)
        for k in range(slot_ref.shape[1]):
            mix = mix + jnp.where(slot_ref[:, k : k + 1] == slot, weight_ref[:, k : k + 1], 0.0)
        mix_ref[...] = mix.astype(jnp.bfloat16)

    out_ref[...] = jnp.dot(mix_ref[...], rows_ref[...], preferred_element_type=jnp.float32).astype(jnp.bfloat16)


def combine(slot, weight, returned):
    slots, width = returned.shape
    tokens = slot.shape[0]
    block = 512
    return pl.pallas_call(
        combine_kernel,
        grid=(width // block,),
        in_specs=[
            pl.BlockSpec(slot.shape, lambda j: (0, 0)),
            pl.BlockSpec(weight.shape, lambda j: (0, 0)),
            pl.BlockSpec((slots, block), lambda j: (0, j)),
        ],
        out_specs=pl.BlockSpec((tokens, block), lambda j: (0, j)),
        out_shape=jax.ShapeDtypeStruct((tokens, width), jnp.bfloat16),
        scratch_shapes=[pltpu.VMEM((tokens, slots), jnp.bfloat16)],
        compiler_params=pltpu.CompilerParams(vmem_limit_bytes=32 * MIB),
        cost_estimate=pl.CostEstimate(
            flops=2 * slots * tokens * width, bytes_accessed=2 * (slots + tokens) * width, transcendentals=0
        ),
        name="combine",
    )(slot, weight, returned)


def body(
    value_input,
    value_grad,
    value_weight,
    out_grad,
    route_ids,
    route_slots,
    seq_lengths,
    route_weights,
    gate_act,
    up_act,
    w_gate,
    w_up,
    w_down,
):
    tokens, width = out_grad.shape
    dp = lax.axis_size("dp")
    experts = lax.axis_size("expert")
    devices = dp * experts
    capacity = gate_act.shape[2]
    ffw = gate_act.shape[3]
    slots = devices * capacity

    live = jnp.arange(tokens, dtype=jnp.int32) < seq_lengths[0]
    slot = jnp.where(live[:, None], route_ids * capacity + route_slots, -1)

    with jax.named_scope("dispatch"):
        send = build_rows(slot.T, out_grad, 0, width, slots)
        routed = exchange(send.reshape(devices, capacity, width), AXES).reshape(slots, width)

    with jax.named_scope("value"):
        cols = width // dp
        grad_all = lax.all_gather(value_grad, "dp", axis=0, tiled=True)
        input_cols = value_input.reshape(tokens, dp, cols).transpose(1, 0, 2)
        input_all = exchange(input_cols, "dp").reshape(dp * tokens, cols)
        value_cols = jnp.einsum("tk,rk->tr", grad_all, value_weight, preferred_element_type=jnp.float32)
        value_cols = exchange(value_cols.astype(jnp.bfloat16).reshape(dp, tokens, cols), "dp")
        value_input_grad = value_cols.transpose(1, 0, 2).reshape(tokens, width)
        term = jnp.einsum("tr,tk->rk", input_all, grad_all, preferred_element_type=jnp.float32)
        terms = exchange(term.reshape(experts, cols // experts, term.shape[1]), "expert")
        value_weight_grad = jnp.sum(terms, axis=0)

    with jax.named_scope("experts"):
        hidden, score = hidden_grads(
            routed, w_down[0], gate_act.reshape(slots, ffw), up_act.reshape(slots, ffw)
        )
        slot_input = slot_grads(hidden, w_gate[0], w_up[0], 0, width)

    with jax.named_scope("return"):
        returned = exchange(slot_input.reshape(devices, capacity, width), AXES).reshape(slots, width)
        scores = exchange(score.astype(jnp.bfloat16).reshape(devices, 1, capacity), AXES).reshape(slots)
        moe_input_grad = combine(slot, route_weights.astype(jnp.float32), returned)
        weight_grad = jnp.sum(
            jnp.where(
                slot[:, :, None] == jnp.arange(slots, dtype=jnp.int32),
                scores.astype(jnp.float32),
                0.0,
            ),
            axis=2,
        ).astype(jnp.bfloat16)
    return (moe_input_grad, weight_grad, value_input_grad, value_weight_grad)


def solution(mesh):
    split = P(AXES, None)
    return jax.shard_map(
        body,
        mesh=mesh,
        in_specs=(
            split,
            split,
            P("dp", None),
            split,
            split,
            split,
            P(AXES),
            split,
            P(AXES, None, None, None),
            P(AXES, None, None, None),
            P(AXES, None, None),
            P(AXES, None, None),
            P(AXES, None, None),
        ),
        out_specs=(split, split, split, split),
        check_vma=False,
    )
```

time: 823 us -> 372 us (0.45)
  waiting for transfers between devices: 455 us -> 227 us
  local copies, waits for them, and re-layouts: 180 us -> 12.9 us
  other arithmetic: 59.4 us -> 1.64 us
  matrix products: 61.2 us -> 6.55 us
  Pallas kernels: 0 us -> 44.7 us
  blocking collectives: 0 us -> 26.1 us
    reduce_scatter x1 -> x0, waiting for transfers between devices: 265 us -> none  [body(): lax.psum_scatter(jnp.einsum('tr,tk->rk', value_input, value_grad, preferr...]
    unnamed x28 -> x27, local copies, waits for them, and re-layouts: 97.9 us -> 8.34 us
    dot_general x6 -> x2, matrix products: 61.2 us -> 6.55 us  [the longest x1 3.46 us: body(): jnp.einsum('tk,rk->tr', grad_all, value_weight, preferred_element_type=jn...]
    unnamed x4 -> x0, other arithmetic: 53.9 us -> none
    gather x4 -> x0, local copies, waits for them, and re-layouts: 51.1 us -> none  [the longest x1 42.7 us: body(): picked = slot_inputs[safe_ids, route_slots]]
    pallas_call x0 -> x4, Pallas kernels: none -> 44.7 us  [the longest x1 17.1 us: slot_grads(): pl.pallas_call(slot_kernel, grid=(width // block,), in_specs=[pl.BlockSpe...]
    convert_element_type x5 -> x2, local copies, waits for them, and re-layouts: 28.2 us -> 0.2 us  [the longest x1 0.11 us: body(): moe_input_grad = combine(slot, route_weights.astype(jnp.float32), returned)]
    all_to_all x0 -> x1, blocking collectives: none -> 26.1 us  [exchange(): return lax.all_to_all(array, axes, split_axis=0, concat_axis=0, tiled=True)]
  transfers between devices with their start and end apart: 6 -> 6, of which waited for: 3 -> 4; matrix products, arithmetic and copies ran while one was open for 37% -> 3% of each run, Pallas kernels for 0% -> 10%
where the time goes in v1:
time: 372 us; the launch traced here: 371 us
  waiting for transfers between devices  227 us (61%)
  Pallas kernels  44.7 us (12%)
  starting transfers between devices  37.1 us (10%)
  blocking collectives  26.1 us (7%)
  between operations  14.9 us (4%)
  local copies, waits for them, and re-layouts  12.9 us (3%)
  matrix products  6.55 us (2%)
    all_to_all x5, waiting for transfers between devices, exchange(): return lax.all_to_all(array, axes, split_axis=0, concat_axis=0, tiled=True)  212 us
    all_to_all x5, starting transfers between devices, exchange(): return lax.all_to_all(array, axes, split_axis=0, concat_axis=0, tiled=True)  37.1 us
    all_to_all x1, blocking collectives, exchange(): return lax.all_to_all(array, axes, split_axis=0, concat_axis=0, tiled=True)  26.1 us
    pallas_call x1, Pallas kernels, slot_grads(): pl.pallas_call(slot_kernel, grid=(width // block,), in_specs=[pl.BlockSpe...  17.1 us
    pallas_call x1, Pallas kernels, hidden_grads(): pl.pallas_call(hidden_kernel, grid=(width // block,), in_specs=[pl.BlockS...  15.9 us
    all_gather x1, waiting for transfers between devices, body(): grad_all = lax.all_gather(value_grad, 'dp', axis=0, tiled=True)  14.7 us
    pallas_call x1, Pallas kernels, combine(): pl.pallas_call(combine_kernel, grid=(width // block,), in_specs=[pl.Block...  8.7 us
    unnamed x27, local copies, waits for them, and re-layouts  8.34 us
  transfers between devices with their start and end apart: 6, of which 4 were waited for; matrix products, arithmetic and copies ran while one was open for 3% of the time, Pallas kernels for 10%

profile of v1, /device:TPU:0, one launch (start us, length us, event | category | flops | bytes accessed | tf_op | source)
XLA Modules:
  0.0 370.7 jit_solution(17946319946498645518)
XLA Ops:
  7.2 0.7 all-gather.2.cloned.1.call-update
  7.9 1.6 copy.66
  9.5 0.5 copy.67
  10.1 26.1 %all_to_all.30 = bf16[16,128,256]{2,1,0:T(8,128)(2,1)S(1)} all-to-all(bf16[16,128,256]{2,1,0:T(8,128)(2,1)S(1)} %copy.67), channel_id=1, replica_groups=mesh['dp'=16,'expert'=8] {'dp'}, dimensions={0} | all-to-all | bytes 2097152 | tf_op jit(solution)/shard_map/value/all_to_all | solution.py:20
  36.1 0.6 copy.68
  36.8 14.7 %all-gather.2.cloned.1.call-done = bf16[2048,512]{1,0:T(8,128)(2,1)} async-done(((bf16[128,512]{1,0:T(8,128)(2,1)}), bf16[2048,512]{1,0:T(8,128)(2,1)}) %all-gather.2.cloned.1.call-update) | async-done | bytes 2097168 | tf_op jit(solution)/shard_map/value/all_gather | solution.py:224
  51.5 3.1 fusion
  54.6 6.4 %all-to-all-start.5 = ((f32[8,32,512]{2,1,0:T(8,128)}), f32[8,32,512]{2,1,0:T(8,128)S(1)}, u32[]{:S(2)}, u32[]{:S(2)}) async-start(f32[8,32,512]{2,1,0:T(8,128)} %fusion), calls=%async_computation.5 | async-start | bytes 1048576 | tf_op jit(solution)/shard_map/value/all_to_all | solution.py:20
  61.0 0.1 copy.60
  61.1 0.1 copy.61
  62.0 3.0 build_rows.1
  65.0 3.2 copy-done.2
  68.3 4.0 %all-to-all-done.5 = f32[8,32,512]{2,1,0:T(8,128)S(1)} async-done(((f32[8,32,512]{2,1,0:T(8,128)}), f32[8,32,512]{2,1,0:T(8,128)S(1)}, u32[]{:S(2)}, u32[]{:S(2)}) %all-to-all-start.5) | async-done | bytes 524320 | tf_op jit(solution)/shard_map/value/all_to_all | solution.py:20
  72.3 0.8 copy-done.7
  73.1 6.3 %all-to-all-start = ((bf16[128,8,4096]{2,1,0:T(8,128)(2,1)}), bf16[128,8,4096]{2,1,0:T(8,128)(2,1)}, u32[]{:S(2)}, u32[]{:S(2)}) async-start(bf16[128,8,4096]{2,1,0:T(8,128)(2,1)} %bitcast.29), calls=%async_computation | async-start | bytes 16777216 | tf_op jit(solution)/shard_map/dispatch/all_to_all | solution.py:20
  79.5 3.5 convolution_convert_fusion
  82.9 104.4 %all-to-all-done = bf16[128,8,4096]{2,1,0:T(8,128)(2,1)} async-done(((bf16[128,8,4096]{2,1,0:T(8,128)(2,1)}), bf16[128,8,4096]{2,1,0:T(8,128)(2,1)}, u32[]{:S(2)}, u32[]{:S(2)}) %all-to-all-start) | async-done | bytes 8388640 | tf_op jit(solution)/shard_map/dispatch/all_to_all | solution.py:20
  187.3 4.4 %all-to-all-start.3 = ((bf16[16,128,256]{2,1,0:T(8,128)(2,1)}), bf16[16,128,256]{2,1,0:T(8,128)(2,1)}, u32[]{:S(2)}, u32[]{:S(2)}) async-start(bf16[16,128,256]{2,1,0:T(8,128)(2,1)} %bitcast.34), calls=%async_computation.3 | async-start | bytes 2097152 | tf_op jit(solution)/shard_map/value/all_to_all | solution.py:20
  191.8 15.9 %hidden_grads.1 = (bf16[1024,1536]{1,0:T(8,128)(2,1)}, f32[1,1024]{1,0:T(1,128)S(1)}) custom-call(bf16[1024,4096]{1,0:T(8,128)(2,1)} %bitcast.3.x_ref, bf16[768,4096]{1,0:T(8,128)(2,1)} %bitcast.39, bf16[1024,768]{1,0:T(8,128)(2,1)S(1)} %bitcast.31, bf16[1024,768]{1,0:T(8,128)(2,1)S(1)} %bitcast.32), custom_call_target="tpu_custom_call" | custom-call | flops 6442450944 | bytes 20971520 | tf_op jit(solution)/shard_map/experts/hidden_grads/pallas_call | solution.py:93
  207.7 0.8 reshape.64
  208.4 9.6 %all-to-all-start.2 = ((bf16[128,1,8]{2,1,0:T(2,128)(2,1)}), bf16[128,1,8]{2,1,0:T(2,128)(2,1)S(1)}, u32[]{:S(2)}, u32[]{:S(2)}) async-start(bf16[128,1,8]{2,1,0:T(2,128)(2,1)} %reshape.64), calls=%async_computation.2 | async-start | bytes 131072 | tf_op jit(solution)/shard_map/return/all_to_all | solution.py:20
  218.0 1.9 copy-done.6
  219.9 17.1 %slot_grads.1 = bf16[1024,4096]{1,0:T(8,128)(2,1)} custom-call(bf16[1024,1536]{1,0:T(8,128)(2,1)S(1)} %copy-done.6, bf16[4096,768]{1,0:T(8,128)(2,1)} %bitcast.40, bf16[4096,768]{1,0:T(8,128)(2,1)} %bitcast.41), custom_call_target="tpu_custom_call" | custom-call | flops 12884901888 | bytes 24117248 | tf_op jit(solution)/shard_map/experts/slot_grads/pallas_call | solution.py:137
  237.0 10.3 %all-to-all-start.1 = ((bf16[128,8,4096]{2,1,0:T(8,128)(2,1)}), bf16[128,8,4096]{2,1,0:T(8,128)(2,1)}, u32[]{:S(2)}, u32[]{:S(2)}) async-start(bf16[128,8,4096]{2,1,0:T(8,128)(2,1)} %bitcast.33), calls=%async_computation.1 | async-start | bytes 16777216 | tf_op jit(solution)/shard_map/return/all_to_all | solution.py:20
  247.3 0.1 copy.63.weight_ref
  247.4 0.7 reduce_sum.19
  248.1 2.3 copy.70
  250.4 0.2 convert_reduce_fusion
  250.7 0.7 select_reduce_fusion
  251.4 0.7 copy.69
  252.0 103.2 %all-to-all-done.1 = bf16[128,8,4096]{2,1,0:T(8,128)(2,1)} async-done(((bf16[128,8,4096]{2,1,0:T(8,128)(2,1)}), bf16[128,8,4096]{2,1,0:T(8,128)(2,1)}, u32[]{:S(2)}, u32[]{:S(2)}) %all-to-all-start.1) | async-done | bytes 8388640 | tf_op jit(solution)/shard_map/return/all_to_all | solution.py:20
  355.2 8.7 %combine.1 = bf16[128,4096]{1,0:T(8,128)(2,1)} custom-call(s32[128,8]{1,0:T(8,128)S(1)} %add_select_fusion.slot_ref, f32[128,8]{1,0:T(8,128)S(1)} %copy.63.weight_ref, bf16[1024,4096]{1,0:T(8,128)(2,1)} %bitcast.10.rows_ref), custom_call_target="tpu_custom_call" | custom-call | flops 1073741824 | bytes 9437184 | tf_op jit(solution)/shard_map/return/combine/pallas_call | solution.py:173
  (30 shorter events, 0.4 us)
Async XLA Ops:
  7.2 72.3 %copy-start = (bf16[256,512]{1,0:T(8,128)(2,1)S(1)}, bf16[256,512]{1,0:T(8,128)(2,1)}, u32[]{:S(2)}) copy-start(bf16[256,512]{1,0:T(8,128)(2,1)} %param.15) | copy-start | bytes 786436
  7.2 44.3 %all-gather.2.cloned.1.call-start = ((), (), s32[]{:S(2)}) async-start(), calls=%async_computation.6 | async-start | bytes 2228224 | tf_op jit(solution)/shard_map/value/all_gather | solution.py:224
  36.8 24.2 %copy-start.10 = (s32[128,8]{0,1:T(8,128)S(1)}, s32[128,8]{0,1:T(8,128)}, u32[]{:S(2)}) copy-start(s32[128,8]{0,1:T(8,128)} %param.17) | copy-start | bytes 12292
  36.8 24.3 %copy-start.9 = (s32[128,8]{0,1:T(8,128)S(1)}, s32[128,8]{0,1:T(8,128)}, u32[]{:S(2)}) copy-start(s32[128,8]{0,1:T(8,128)} %param.18) | copy-start | bytes 12292
  36.8 25.2 %copy-start.3 = (bf16[128,4096]{1,0:T(8,128)(2,1)S(1)}, bf16[128,4096]{1,0:T(8,128)(2,1)}, u32[]{:S(2)}) copy-start(bf16[128,4096]{1,0:T(8,128)(2,1)} %grad_ref.1) | copy-start | bytes 3145732
  54.6 17.7 %all-to-all-start.5 = ((f32[8,32,512]{2,1,0:T(8,128)}), f32[8,32,512]{2,1,0:T(8,128)S(1)}, u32[]{:S(2)}, u32[]{:S(2)}) async-start(f32[8,32,512]{2,1,0:T(8,128)} %fusion), calls=%async_computation.5 | async-start | bytes 1048576 | tf_op jit(solution)/shard_map/value/all_to_all | solution.py:20
  65.0 3.2 copy-start.2
  72.3 0.8 copy-start.7
  73.1 114.2 %all-to-all-start = ((bf16[128,8,4096]{2,1,0:T(8,128)(2,1)}), bf16[128,8,4096]{2,1,0:T(8,128)(2,1)}, u32[]{:S(2)}, u32[]{:S(2)}) async-start(bf16[128,8,4096]{2,1,0:T(8,128)(2,1)} %bitcast.29), calls=%async_computation | async-start | bytes 16777216 | tf_op jit(solution)/shard_map/dispatch/all_to_all | solution.py:20
  79.4 112.3 %copy-start.4 = (bf16[1,128,8,768]{3,2,1,0:T(8,128)(2,1)S(1)}, bf16[1,128,8,768]{3,2,1,0:T(8,128)(2,1)}, u32[]{:S(2)}) copy-start(bf16[1,128,8,768]{3,2,1,0:T(8,128)(2,1)} %param.21) | copy-start | bytes 4718596
  79.5 112.3 %copy-start.5 = (bf16[1,128,8,768]{3,2,1,0:T(8,128)(2,1)S(1)}, bf16[1,128,8,768]{3,2,1,0:T(8,128)(2,1)}, u32[]{:S(2)}) copy-start(bf16[1,128,8,768]{3,2,1,0:T(8,128)(2,1)} %param.22) | copy-start | bytes 4718596
  187.3 21.1 %all-to-all-start.3 = ((bf16[16,128,256]{2,1,0:T(8,128)(2,1)}), bf16[16,128,256]{2,1,0:T(8,128)(2,1)}, u32[]{:S(2)}, u32[]{:S(2)}) async-start(bf16[16,128,256]{2,1,0:T(8,128)(2,1)} %bitcast.34), calls=%async_computation.3 | async-start | bytes 2097152 | tf_op jit(solution)/shard_map/value/all_to_all | solution.py:20
  208.4 28.6 %all-to-all-start.2 = ((bf16[128,1,8]{2,1,0:T(2,128)(2,1)}), bf16[128,1,8]{2,1,0:T(2,128)(2,1)S(1)}, u32[]{:S(2)}, u32[]{:S(2)}) async-start(bf16[128,1,8]{2,1,0:T(2,128)(2,1)} %reshape.64), calls=%async_computation.2 | async-start | bytes 131072 | tf_op jit(solution)/shard_map/return/all_to_all | solution.py:20
  218.0 1.9 copy-start.6
  237.0 10.3 %copy-start.11 = (bf16[128,8]{0,1:T(8,128)(2,1)S(1)}, bf16[128,8]{0,1:T(8,128)(2,1)}, u32[]{:S(2)}) copy-start(bf16[128,8]{0,1:T(8,128)(2,1)} %param.20) | copy-start | bytes 6148
  237.0 10.4 %copy-start.8 = (f32[8,32,512]{2,1,0:T(8,128)S(1)}, f32[8,32,512]{2,1,0:T(8,128)}, u32[]{:S(2)}) copy-start(f32[8,32,512]{2,1,0:T(8,128)} %copy-done.7) | copy-start | bytes 1572868
  237.0 118.2 %all-to-all-start.1 = ((bf16[128,8,4096]{2,1,0:T(8,128)(2,1)}), bf16[128,8,4096]{2,1,0:T(8,128)(2,1)}, u32[]{:S(2)}, u32[]{:S(2)}) async-start(bf16[128,8,4096]{2,1,0:T(8,128)(2,1)} %bitcast.33), calls=%async_computation.1 | async-start | bytes 16777216 | tf_op jit(solution)/shard_map/return/all_to_all | solution.py:20
  355.2 8.7 %copy-start.1 = (bf16[256,512]{1,0:T(8,128)(2,1)S(1)}, bf16[256,512]{1,0:T(8,128)(2,1)}, u32[]{:S(2)}) copy-start(bf16[256,512]{1,0:T(8,128)(2,1)} %param.15) | copy-start | bytes 786436
Sparse Core Ops, SparseCore 0:
  9.7 41.7 all-gather.1

commit v2 on v1

v2 whole, which is shorter than its diff:
```python
import functools

import jax
import jax.numpy as jnp
from jax import lax
from jax.experimental import pallas as pl
from jax.experimental.pallas import tpu as pltpu
from jax.sharding import PartitionSpec as P

AXES = ("dp", "expert")
MIB = 1024 * 1024
LANES = 128
CAPACITY = 8
NT = (((1,), (1,)), ((), ()))


def dot_nt(left, right):
    return lax.dot_general(left, right, NT, preferred_element_type=jnp.float32)


def exchange(array, axes):
    return lax.all_to_all(array, axes, split_axis=0, concat_axis=0, tiled=True)


def rows_kernel(length_ref, ids_ref, slots_ref, grad_ref, out_ref):
    rows, width = out_ref.shape
    top, tokens = ids_ref.shape
    live = lax.broadcasted_iota(jnp.int32, (1, tokens), 1) < length_ref[0]
    slot = lax.broadcasted_iota(jnp.int32, (rows, tokens), 0) + pl.program_id(0) * rows
    hit = None
    for k in range(top):
        name = jnp.where(live, ids_ref[k : k + 1, :] * CAPACITY + slots_ref[k : k + 1, :], -1)
        hit = name == slot if hit is None else hit | (name == slot)
    pick = jnp.where(hit, 1.0, 0.0).astype(jnp.bfloat16)
    step = 1024
    for c in range(0, width, step):
        out_ref[:, c : c + step] = jnp.dot(
            pick, grad_ref[:, c : c + step], preferred_element_type=jnp.float32
        ).astype(jnp.bfloat16)


def build_rows(seq_lengths, ids_t, slots_t, out_grad, slots):
    tokens, width = out_grad.shape
    rows = 256
    return pl.pallas_call(
        rows_kernel,
        grid=(slots // rows,),
        in_specs=[
            pl.BlockSpec(memory_space=pltpu.SMEM),
            pl.BlockSpec(ids_t.shape, lambda i: (0, 0)),
            pl.BlockSpec(slots_t.shape, lambda i: (0, 0)),
            pl.BlockSpec((tokens, width), lambda i: (0, 0)),
        ],
        out_specs=pl.BlockSpec((rows, width), lambda i: (i, 0)),
        out_shape=pltpu.HBM((slots, width), jnp.bfloat16),
        compiler_params=pltpu.CompilerParams(vmem_limit_bytes=32 * MIB),
        cost_estimate=pl.CostEstimate(
            flops=2 * slots * tokens * width, bytes_accessed=2 * (slots + tokens) * width, transcendentals=0
        ),
        name="build_rows",
    )(seq_lengths, *[pltpu.with_memory_space_constraint(a, pltpu.HBM) for a in (ids_t, slots_t, out_grad)])


def hidden_kernel(x_ref, down_ref, gate_ref, up_ref, hidden_ref, score_ref):
    rows = x_ref.shape[0]
    ffw = down_ref.shape[0]
    part = 256
    score = jnp.zeros((rows, LANES), jnp.float32)
    for c in range(0, ffw, part):
        cols = slice(c, c + part)
        back = dot_nt(x_ref[...], down_ref[cols, :])
        gate = gate_ref[:, cols].astype(jnp.float32)
        up = up_ref[:, cols].astype(jnp.float32)
        sig = 1.0 / (1.0 + jnp.exp(-gate))
        up_grad = back * (gate * sig)
        hidden_ref[:, ffw + c : ffw + c + part] = up_grad.astype(jnp.bfloat16)
        hidden_ref[:, cols] = (back * up * sig * (1.0 + gate * (1.0 - sig))).astype(jnp.bfloat16)
        term = up_grad * up
        for lane in range(0, part, LANES):
            score = score + term[:, lane : lane + LANES]
    score = jnp.sum(score, axis=1, keepdims=True)
    score_ref[...] = jnp.broadcast_to(score, score_ref.shape).astype(jnp.bfloat16)


def hidden_grads(rows_in, down, gate, up, score_at):
    slots, width = rows_in.shape
    ffw = down.shape[0]
    rows = 256
    return pl.pallas_call(
        hidden_kernel,
        grid=(slots // rows,),
        in_specs=[
            pl.BlockSpec((rows, width), lambda i: (i, 0)),
            pl.BlockSpec(memory_space=pltpu.VMEM),
            pl.BlockSpec((rows, ffw), lambda i: (i, 0)),
            pl.BlockSpec((rows, ffw), lambda i: (i, 0)),
        ],
        out_specs=[
            pl.BlockSpec((rows, 2 * ffw), lambda i: (i, 0)),
            pl.BlockSpec((rows, LANES), lambda i: (i, score_at // LANES)),
        ],
        out_shape=[
            jax.ShapeDtypeStruct((slots, 2 * ffw), jnp.bfloat16),
            pltpu.HBM((slots, score_at + LANES), jnp.bfloat16),
        ],
        compiler_params=pltpu.CompilerParams(vmem_limit_bytes=32 * MIB),
        cost_estimate=pl.CostEstimate(flops=1, bytes_accessed=1, transcendentals=0),
        name="hidden_grads",
    )(
        rows_in,
        pltpu.with_memory_space_constraint(down, pltpu.VMEM),
        pltpu.with_memory_space_constraint(gate, pltpu.HBM),
        pltpu.with_memory_space_constraint(up, pltpu.HBM),
    )


def slot_kernel(hidden_ref, gate_w_ref, up_w_ref, *refs):
    out_ref = refs[-1]
    ffw = gate_w_ref.shape[1]
    part = 256
    for r in range(0, out_ref.shape[0], part):
        here = slice(r, r + part)
        out_ref[here, :] = (
            dot_nt(hidden_ref[here, :ffw], gate_w_ref[...]) + dot_nt(hidden_ref[here, ffw:], up_w_ref[...])
        ).astype(jnp.bfloat16)


def slot_grads(hidden, gate_w, up_w, start, width, into=None):
    slots = hidden.shape[0]
    ffw = gate_w.shape[1]
    block = 512
    first = start // block
    before = () if into is None else (into,)
    cost = pl.CostEstimate(flops=1, bytes_accessed=1, transcendentals=0)
    if into is None:
        cost = pl.CostEstimate(
            flops=4 * slots * width * ffw,
            bytes_accessed=2 * (slots * width + 2 * ffw * width + 2 * slots * ffw),
            transcendentals=0,
        )
    return pl.pallas_call(
        slot_kernel,
        grid=(width // block,),
        in_specs=[
            pl.BlockSpec((slots, 2 * ffw), lambda j: (0, 0)),
            pl.BlockSpec((block, ffw), lambda j: (first + j, 0)),
            pl.BlockSpec((block, ffw), lambda j: (first + j, 0)),
        ]
        + [pl.BlockSpec(memory_space=pl.ANY)] * len(before),
        out_specs=pl.BlockSpec((slots, block), lambda j: (0, j)),
        out_shape=pltpu.HBM((slots, width if into is None else into.shape[1]), jnp.bfloat16),
        input_output_aliases={3: 0} if before else {},
        compiler_params=pltpu.CompilerParams(vmem_limit_bytes=32 * MIB),
        cost_estimate=cost,
        name="slot_grads",
    )(
        hidden,
        pltpu.with_memory_space_constraint(gate_w, pltpu.HBM),
        pltpu.with_memory_space_constraint(up_w, pltpu.HBM),
        *before,
    )


def mix_kernel(slot_ref, weight_ref, mix_ref):
    slot = lax.broadcasted_iota(jnp.int32, mix_ref.shape, 1)
    mix = jnp.zeros(mix_ref.shape, jnp.float32)
    for k in range(slot_ref.shape[1]):
        mix = mix + jnp.where(slot_ref[:, k : k + 1] == slot, weight_ref[:, k : k + 1], 0.0)
    mix_ref[...] = mix.astype(jnp.bfloat16)


def mix_weights(slot, weight, slots):
    return pl.pallas_call(
        mix_kernel,
        out_shape=jax.ShapeDtypeStruct((slot.shape[0], slots), jnp.bfloat16),
        name="mix_weights",
    )(slot, weight)


def combine_kernel(mix_ref, rows_ref, *refs):
    refs[-1][...] = jnp.dot(mix_ref[...], rows_ref[...], preferred_element_type=jnp.float32).astype(jnp.bfloat16)


def combine(mix, returned, start, cols, width, earlier=None):
    slots = returned.shape[0]
    tokens = mix.shape[0]
    block = 1024
    first = start // block
    before = () if earlier is None else (earlier,)
    return pl.pallas_call(
        combine_kernel,
        grid=(cols // block,),
        in_specs=[
            pl.BlockSpec(mix.shape, lambda j: (0, 0)),
            pl.BlockSpec((slots, block), lambda j: (0, j)),
        ]
        + [pl.BlockSpec(memory_space=pl.ANY)] * len(before),
        out_specs=pl.BlockSpec((tokens, block), lambda j: (0, first + j)),
        out_shape=jax.ShapeDtypeStruct((tokens, width), jnp.bfloat16),
        input_output_aliases={2: 0} if before else {},
        compiler_params=pltpu.CompilerParams(vmem_limit_bytes=32 * MIB),
        cost_estimate=pl.CostEstimate(
            flops=2 * slots * tokens * cols, bytes_accessed=2 * (slots + tokens) * cols, transcendentals=0
        ),
        name="combine",
    )(mix, returned, *before)


def place(index):
    dp, expert = index // 8, index % 8
    return [dp // 8, dp // 2 % 4, dp % 2, expert // 4, expert % 4]


def shift(array, axis, step):
    sizes = (2, 4, 2, 2, 4)
    pairs = []
    for source in range(128):
        at = place(source)
        for a, s in zip(axis, step):
            at[a] = (at[a] + s) % sizes[a]
        pairs.append((source, (((at[0] * 4 + at[1]) * 2 + at[2]) * 2 + at[3]) * 4 + at[4]))
    return lax.ppermute(array, AXES, pairs)


def value_weight_terms(value_input, value_grad):
    tokens, width = value_input.shape
    feats = value_grad.shape[1]
    dp, expert = lax.axis_index("dp"), lax.axis_index("expert")
    x_lo, z, core, x_hi, y = dp // 8, dp // 2 % 4, dp % 2, expert // 4, expert % 4
    parts = value_input.reshape(tokens, 2, 4, 2, 2, width // 32).transpose(3, 0, 1, 4, 2, 5)
    parts = parts.reshape(2, tokens, width // 2)
    own = jnp.where(core == 0, parts[0], parts[1])
    other = shift(jnp.where(core == 0, parts[1], parts[0]), (2,), (1,))
    other_grad = shift(value_grad, (2,), (1,))
    term = jnp.einsum("tr,tk->rk", own, value_grad, preferred_element_type=jnp.float32)
    term = term + jnp.einsum("tr,tk->rk", other, other_grad, preferred_element_type=jnp.float32)
    term = term.reshape(4, width // 8, feats)

    def pick(array, at, dim):
        return lax.dynamic_index_in_dim(array, at, dim, keepdims=False)

    total = pick(term, x_lo * 2 + x_hi, 0)
    for a, b in ((1, 0), (1, 1), (0, 1)):
        piece = pick(term, (x_lo + a) % 2 * 2 + (x_hi + b) % 2, 0).astype(jnp.bfloat16)
        total = total + shift(piece, (0, 3), (a, b)).astype(jnp.float32)
    for axis, here, lead in ((4, y, (4, 4)), (1, z, (4,))):
        term = total.reshape(*lead, -1, feats)
        dim = len(lead) - 1
        total = pick(term, here, dim)
        for k in (1, 3, 2):
            total = total + shift(pick(term, (here + k) % 4, dim), (axis,), (k,))
    return total.reshape(-1, feats)


def place(index):
    dp, expert = index // 8, index % 8
    return [dp // 8, dp // 2 % 4, dp % 2, expert // 4, expert % 4]


def shift(array, axis, step):
    sizes = (2, 4, 2, 2, 4)
    pairs = []
    for source in range(128):
        at = place(source)
        for a, s in zip(axis, step):
            at[a] = (at[a] + s) % sizes[a]
        pairs.append((source, (((at[0] * 4 + at[1]) * 2 + at[2]) * 2 + at[3]) * 4 + at[4]))
    return lax.ppermute(array, AXES, pairs)


def pick(array, at, dim):
    return lax.dynamic_index_in_dim(array, at, dim, keepdims=False)


def by_core(core, first, second):
    return jnp.where(core == 0, first, second), jnp.where(core == 0, second, first)


def body(
    value_input,
    value_grad,
    value_weight,
    out_grad,
    route_ids,
    route_slots,
    seq_lengths,
    route_weights,
    gate_act,
    up_act,
    w_gate,
    w_up,
    w_down,
):
    tokens, width = out_grad.shape
    dp = lax.axis_size("dp")
    experts = lax.axis_size("expert")
    devices = dp * experts
    capacity = gate_act.shape[2]
    ffw = gate_act.shape[3]
    slots = devices * capacity

    live = jnp.arange(tokens, dtype=jnp.int32) < seq_lengths[0]
    slot = jnp.where(live[:, None], route_ids * capacity + route_slots, -1)

    in_parts = ((0, 1024), (1024, 3072))
    dp, expert = lax.axis_index("dp"), lax.axis_index("expert")
    x_lo, z, core, x_hi, y = dp // 8, dp // 2 % 4, dp % 2, expert // 4, expert % 4
    feats = value_grad.shape[1]
    half, cols = width // 2, width // 16

    with jax.named_scope("value_first"):
        beside = shift(value_weight, (0,), (1,))

    with jax.named_scope("dispatch"):
        send = build_rows(seq_lengths, route_ids.T, route_slots.T, out_grad, slots)
        send, beside, value_in = lax.optimization_barrier((send, beside, value_input))
        routed = exchange(send.reshape(devices, capacity, width), AXES).reshape(slots, width)

    with jax.named_scope("value_second"):
        pair = jnp.stack(by_core(x_lo, value_weight, beside))
        halves = value_in.reshape(tokens, 8, 2, cols)
        own, other = by_core(core, halves[:, :, 0], halves[:, :, 1])
        other = jnp.concatenate([other.reshape(tokens, half), value_grad], axis=1)
        other = shift(other, (2,), (1,))
        inputs = jnp.concatenate([own.reshape(tokens, half), other[:, :half]])
        inputs = inputs.reshape(2 * tokens, 2, 4, 2, cols // 2)
        grads = jnp.concatenate([value_grad, other[:, half:]])

        def along_x(a, b):
            at = (0, (x_lo + a) % 2, 0, (x_hi + b) % 2, 0)
            part = lax.dynamic_slice(inputs, at, (2 * tokens, 1, 4, 1, cols // 2))
            return jnp.concatenate([part.reshape(2 * tokens, 2 * cols), grads], axis=1)

        steps = ((0, 1), (1, 0), (1, 1))
        kept = along_x(0, 0)
        packs = [along_x(*step) for step in steps]
        mix = mix_weights(slot, route_weights.astype(jnp.float32), slots)
        routed, mix, pair, kept, *packs = lax.optimization_barrier((routed, mix, pair, kept, *packs))
        below, above = shift(pair, (1,), (1,)), shift(pair, (1,), (3,))
        arrived = [shift(pack, (0, 3), step) for pack, step in zip(packs, steps)]

    with jax.named_scope("experts"):
        hidden, score = hidden_grads(
            routed, w_down[0], gate_act.reshape(slots, ffw), up_act.reshape(slots, ffw), in_parts[0][1]
        )
        slot_first = slot_grads(hidden, w_gate[0], w_up[0], *in_parts[0], score)
        slot_second = slot_grads(hidden, w_gate[0], w_up[0], *in_parts[1])

    with jax.named_scope("value_third"):
        held = lax.optimization_barrier((slot_first, below, above, *arrived))
        slot_first, below, above = held[:3]
        halfway = [shift(below[0], (1,), (1,)), shift(above[1], (1,), (3,))]
        packs = jnp.concatenate([kept, *held[3:]])
        term = jnp.einsum(
            "tr,tk->rk", packs[:, : 2 * cols], packs[:, 2 * cols :], preferred_element_type=jnp.float32
        )
        term = term.reshape(4, 4, cols // 8, feats)
        total = pick(term, y, 1)
        sent = [pick(term, (y + k) % 4, 1).astype(jnp.bfloat16) for k in (1, 2, 3)]
        terms = [shift(t, (4,), (k,)) for t, k in zip(sent, (1, 2, 3))]

    with jax.named_scope("return"):
        first = exchange(slot_first.reshape(devices, capacity, -1), AXES).reshape(slots, -1)
        held = lax.optimization_barrier((slot_second, *halfway, *terms))
        slot_second, halfway, terms = held[0], held[1:3], held[3:]
        second = exchange(slot_second.reshape(devices, capacity, -1), AXES).reshape(slots, -1)
        moe_input_grad = combine(mix, first, *in_parts[0], width)
        scores = first[:, in_parts[0][1]].astype(jnp.float32)
        weight_grad = jnp.sum(
            jnp.where(slot[:, :, None] == jnp.arange(slots, dtype=jnp.int32), scores, 0.0), axis=2
        ).astype(jnp.bfloat16)
        moe_input_grad = combine(mix, second, *in_parts[1], width, moe_input_grad)

    with jax.named_scope("value_last"):
        for part in terms:
            total = total + part.astype(jnp.float32)
        last = [shift(pick(total, (z + k) % 4, 0), (1,), (k,)) for k in (1, 2, 3)]

        ring = jnp.stack([pair, above, jnp.stack(halfway), below])
        across = shift(ring, (2,), (1,))

        def products(weight):
            out = jnp.einsum("tk,ixrk->ixtr", value_grad, weight, preferred_element_type=jnp.float32)
            out = out.astype(jnp.bfloat16)
            return lax.dynamic_slice_in_dim(jnp.concatenate([out, out]), (4 - z) % 4, 4, axis=0)

        both = jnp.stack(by_core(core, products(ring), products(across)))
        value_input_grad = both.transpose(3, 2, 1, 0, 4).reshape(tokens, width)

    with jax.named_scope("finish"):
        moe_input_grad, *last = lax.optimization_barrier((moe_input_grad, *last))
        value_weight_grad = pick(total, z, 0) + last[0] + last[1] + last[2]
    return (moe_input_grad, weight_grad, value_input_grad, value_weight_grad)


def solution(mesh):
    split = P(AXES, None)
    return jax.shard_map(
        body,
        mesh=mesh,
        in_specs=(
            split,
            split,
            P("dp", None),
            split,
            split,
            split,
            P(AXES),
            split,
            P(AXES, None, None, None),
            P(AXES, None, None, None),
            P(AXES, None, None),
            P(AXES, None, None),
            P(AXES, None, None),
        ),
        out_specs=(split, split, split, split),
        check_vma=False,
    )
```

time: 372 us -> 300 us (0.81); the launches traced: 371 us -> 295 us
  waiting for transfers between devices: 227 us -> 163 us
  blocking collectives: 26.1 us -> 0 us
  between operations: 14.9 us -> 1.83 us
  starting transfers between devices: 37.1 us -> 50.1 us
  other arithmetic: 1.64 us -> 11.3 us
  local copies, waits for them, and re-layouts: 12.9 us -> 16.7 us
    all_to_all x5 -> x3, waiting for transfers between devices: 212 us -> 155 us  [exchange(): return lax.all_to_all(array, axes, split_axis=0, concat_axis=0, tiled=True)]
    all_to_all x1 -> x0, blocking collectives: 26.1 us -> none  [exchange(): return lax.all_to_all(array, axes, split_axis=0, concat_axis=0, tiled=True)]
    ppermute x0 -> x16, starting transfers between devices: none -> 20.3 us  [shift(): return lax.ppermute(array, AXES, pairs)]
    all_gather x1 -> x0, waiting for transfers between devices: 14.7 us -> none  [body(): grad_all = lax.all_gather(value_grad, 'dp', axis=0, tiled=True)]
    ppermute x0 -> x16, waiting for transfers between devices: none -> 7.85 us  [shift(): return lax.ppermute(array, AXES, pairs)]
    all_to_all x5 -> x3, starting transfers between devices: 37.1 us -> 29.8 us  [exchange(): return lax.all_to_all(array, axes, split_axis=0, concat_axis=0, tiled=True)]
    pallas_call x2 -> x4, Pallas kernels: 24.6 us -> 19.7 us  [the longest x1 11.1 us: hidden_grads(): pl.pallas_call(hidden_kernel, grid=(slots // rows,), in_specs=[pl.BlockSp...]
    another operation x0 -> x5, other arithmetic: none -> 4.21 us  [the longest x2 3.7 us: body(): ring = jnp.stack([pair, above, jnp.stack(halfway), below])]
  transfers between devices with their start and end apart: 6 -> 19, of which waited for: 4 -> 5; matrix products, arithmetic and copies ran while one was open for 3% -> 8% of each run, Pallas kernels for 10% -> 16%
where the time goes in v2:
time: 300 us; the launch traced here: 295 us
  waiting for transfers between devices  163 us (54%)
  starting transfers between devices  50.1 us (17%)
  Pallas kernels  46.6 us (16%)
  local copies, waits for them, and re-layouts  16.7 us (6%)
  other arithmetic  11.3 us (4%)
  matrix products  5.32 us (2%)
    all_to_all x3, waiting for transfers between devices, exchange(): return lax.all_to_all(array, axes, split_axis=0, concat_axis=0, tiled=True)  155 us
    all_to_all x3, starting transfers between devices, exchange(): return lax.all_to_all(array, axes, split_axis=0, concat_axis=0, tiled=True)  29.8 us
    pallas_call x2, Pallas kernels, slot_grads(): pl.pallas_call(slot_kernel, grid=(width // block,), in_specs=[pl.BlockSpe...  20.7 us
    ppermute x16, starting transfers between devices, shift(): return lax.ppermute(array, AXES, pairs)  20.3 us
    unnamed x59, local copies, waits for them, and re-layouts  11.1 us
    pallas_call x1, Pallas kernels, hidden_grads(): pl.pallas_call(hidden_kernel, grid=(slots // rows,), in_specs=[pl.BlockSp...  11.1 us
    ppermute x16, waiting for transfers between devices, shift(): return lax.ppermute(array, AXES, pairs)  7.85 us
    pallas_call x1, Pallas kernels, build_rows(): pl.pallas_call(rows_kernel, grid=(slots // rows,), in_specs=[pl.BlockSpec...  6.22 us
  transfers between devices with their start and end apart: 19, of which 5 were waited for; matrix products, arithmetic and copies ran while one was open for 8% of the time, Pallas kernels for 16%

profile of v2, /device:TPU:0, one launch (start us, length us, event | category | flops | bytes accessed | tf_op | source)
XLA Modules:
  0.0 294.7 jit_solution(6021238654463615822)
XLA Ops:
  0.6 1.7 collective-permute-start
  2.9 6.2 %build_rows.1 = bf16[1024,4096]{1,0:T(8,128)(2,1)} custom-call(s32[1]{0:T(128)} %copy.80.length_ref, s32[8,128]{1,0:T(8,128)} %bitcast.119, s32[8,128]{1,0:T(8,128)} %bitcast.118, bf16[128,4096]{1,0:T(8,128)(2,1)} %grad_ref.1), custom_call_target="tpu_custom_call" | custom-call | flops 1073741824 | bytes 9437184 | tf_op jit(solution)/shard_map/dispatch/build_rows/pallas_call | solution.py:45
  9.2 11.5 %all-to-all-start = ((bf16[128,8,4096]{2,1,0:T(8,128)(2,1)}), bf16[128,8,4096]{2,1,0:T(8,128)(2,1)}, u32[]{:S(2)}, u32[]{:S(2)}) async-start(bf16[128,8,4096]{2,1,0:T(8,128)(2,1)} %bitcast.94), calls=%async_computation | async-start | bytes 16777216 | tf_op jit(solution)/shard_map/dispatch/all_to_all | solution.py:22
  24.2 2.4 mix_weights.1.mix_ref
  27.5 1.1 slice.38
  29.8 98.7 %all-to-all-done = bf16[128,8,4096]{2,1,0:T(8,128)(2,1)} async-done(((bf16[128,8,4096]{2,1,0:T(8,128)(2,1)}), bf16[128,8,4096]{2,1,0:T(8,128)(2,1)}, u32[]{:S(2)}, u32[]{:S(2)}) %all-to-all-start) | async-done | bytes 8388640 | tf_op jit(solution)/shard_map/dispatch/all_to_all | solution.py:22
  129.4 3.2 %collective-permute-start.6 = (bf16[256,1024]{0,1:T(8,128)(2,1)S(1)}, bf16[256,1024]{0,1:T(8,128)(2,1)S(1)}, u32[]{:S(2)}, u32[]{:S(2)}) collective-permute-start(bf16[256,1024]{0,1:T(8,128)(2,1)S(1)} %get-tuple-element.42), channel_id=1, source_target_pairs={{0,68},{1,69},{2,70},{3,71},{4,64},{5,65},{6,66},{7,67},{8,76},{9,... | collective-permute-start | bytes 1572872 | tf_op jit(solution)/shard_map/value_second/ppermute | solution.py:268
  132.6 2.0 collective-permute-start.2
  134.6 2.8 copy-done
  137.4 11.1 %hidden_grads.1 = (bf16[1024,1536]{1,0:T(8,128)(2,1)S(1)}, bf16[1024,1152]{1,0:T(8,128)(2,1)}) custom-call(bf16[1024,4096]{1,0:T(8,128)(2,1)} %bitcast.3.x_ref, bf16[768,4096]{1,0:T(8,128)(2,1)S(1)} %bitcast.93, bf16[1024,768]{1,0:T(8,128)(2,1)} %bitcast.107, bf16[1024,768]{1,0:T(8,128)(2,1)} %bitcast.108), custom_call_target="tpu_custom_call" | custom-call | flops 1 | bytes 1 | tf_op jit(solution)/shard_map/experts/hidden_grads/pallas_call | solution.py:89
  148.5 7.2 %slot_grads.3 = bf16[1024,1152]{1,0:T(8,128)(2,1)} custom-call(bf16[1024,1536]{1,0:T(8,128)(2,1)S(1)} %get-tuple-element.37.hidden_ref, bf16[4096,768]{1,0:T(8,128)(2,1)} %bitcast.97, bf16[4096,768]{1,0:T(8,128)(2,1)} %bitcast.99, bf16[1024,1152]{1,0:T(8,128)(2,1)} %get-tuple-element.38.refs_0_), custom_call_target="tpu_custom_call", output_to_operand_aliasing={{}: (3, {})} | custom-call | flops 1 | bytes 1 | tf_op jit(solution)/shard_map/experts/slot_grads/pallas_call | solution.py:141
  157.8 8.9 %all-to-all-start.2 = ((bf16[128,8,1152]{2,1,0:T(8,128)(2,1)}), bf16[128,8,1152]{2,1,0:T(8,128)(2,1)S(1)}, u32[]{:S(2)}, u32[]{:S(2)}) async-start(bf16[128,8,1152]{2,1,0:T(8,128)(2,1)} %bitcast.95), calls=%async_computation.2 | async-start | bytes 4718592 | tf_op jit(solution)/shard_map/return/all_to_all | solution.py:22
  168.0 2.9 collective-permute-start.8
  174.0 2.9 collective-permute-start.11
  176.9 2.3 collective-permute-start.10
  179.2 13.5 %slot_grads.2 = bf16[1024,3072]{1,0:T(8,128)(2,1)} custom-call(bf16[1024,1536]{1,0:T(8,128)(2,1)S(1)} %copy-done.2, bf16[4096,768]{1,0:T(8,128)(2,1)} %bitcast.98, bf16[4096,768]{1,0:T(8,128)(2,1)} %bitcast.100), custom_call_target="tpu_custom_call" | custom-call | flops 9663676416 | bytes 18874368 | tf_op jit(solution)/shard_map/experts/slot_grads/pallas_call | solution.py:141
  192.7 4.0 %collective-permute-done.11 = bf16[4,32,512]{2,1,0:T(8,128)(2,1)S(1)} collective-permute-done((bf16[4,32,512]{2,1,0:T(8,128)(2,1)S(1)}, bf16[4,32,512]{2,1,0:T(8,128)(2,1)S(1)}, u32[]{:S(2)}, u32[]{:S(2)}) %collective-permute-start.11) | collective-permute-done | bytes 131104 | tf_op jit(solution)/shard_map/value_third/ppermute | solution.py:268
  197.7 2.8 collective-permute-done.10
  201.8 9.4 %all-to-all-start.1 = ((bf16[128,8,3072]{2,1,0:T(8,128)(2,1)}), bf16[128,8,3072]{2,1,0:T(8,128)(2,1)}, u32[]{:S(2)}, u32[]{:S(2)}) async-start(bf16[128,8,3072]{2,1,0:T(8,128)(2,1)} %bitcast.96), calls=%async_computation.1 | async-start | bytes 12582912 | tf_op jit(solution)/shard_map/return/all_to_all | solution.py:22
  212.3 2.6 pad_maximum_fusion
  214.9 1.2 fusion.12
  216.8 2.9 collective-permute-start.14
  220.1 1.1 collective-permute-start.12
  221.2 2.3 fusion
  223.7 1.3 select_reduce_fusion
  225.0 1.4 copy.70
  226.4 1.2 combine.2.refs_0_
  227.5 2.3 fusion.1
  230.5 1.3 copy.71
  231.8 56.3 %all-to-all-done.1 = bf16[128,8,3072]{2,1,0:T(8,128)(2,1)} async-done(((bf16[128,8,3072]{2,1,0:T(8,128)(2,1)}), bf16[128,8,3072]{2,1,0:T(8,128)(2,1)}, u32[]{:S(2)}, u32[]{:S(2)}) %all-to-all-start.1) | async-done | bytes 6291488 | tf_op jit(solution)/shard_map/return/all_to_all | solution.py:22
  288.1 5.0 %combine.3 = bf16[128,4096]{1,0:T(8,128)(2,1)} custom-call(bf16[128,1024]{1,0:T(8,128)(2,1)S(1)} %copy-done.3, bf16[1024,3072]{1,0:T(8,128)(2,1)} %bitcast.27.rows_ref, bf16[128,4096]{1,0:T(8,128)(2,1)} %combine.2.refs_0_), custom_call_target="tpu_custom_call", output_to_operand_aliasing={{}: (2, {})} | custom-call | flops 805306368 | bytes 7077888 | tf_op jit(solution)/shard_map/return/combine/pallas_call | solution.py:190
  293.1 1.6 fusion.19
  (104 shorter events, 17.8 us)
Async XLA Ops:
  0.6 8.5 %collective-permute-start = (bf16[256,512]{1,0:T(8,128)(2,1)}, bf16[256,512]{1,0:T(8,128)(2,1)S(1)}, u32[]{:S(2)}, u32[]{:S(2)}) collective-permute-start(bf16[256,512]{1,0:T(8,128)(2,1)} %param.15), channel_id=1, source_target_pairs={{0,64},{1,65},{2,66},{3,67},{4,68},{5,69},{6,70},{7,71},{8,72},{9,... | collective-permute-start | bytes 786440 | tf_op jit(solution)/shard_map/value_first/ppermute | solution.py:268
  9.2 11.5 %copy-start.4 = (bf16[128,512]{1,0:T(8,128)(2,1)S(1)}, bf16[128,512]{1,0:T(8,128)(2,1)}, u32[]{:S(2)}) copy-start(bf16[128,512]{1,0:T(8,128)(2,1)} %param.14) | copy-start | bytes 393220
  9.2 11.6 %copy-start.24 = (s32[128,8]{0,1:T(8,128)S(1)}, s32[128,8]{0,1:T(8,128)}, u32[]{:S(2)}) copy-start(s32[128,8]{0,1:T(8,128)} %param.17) | copy-start | bytes 12292
  9.2 11.7 %copy-start.8 = (bf16[128,4096]{1,0:T(8,128)(2,1)S(1)}, bf16[128,4096]{1,0:T(8,128)(2,1)}, u32[]{:S(2)}) copy-start(bf16[128,4096]{1,0:T(8,128)(2,1)} %param.13) | copy-start | bytes 3145732
  9.2 119.3 %all-to-all-start = ((bf16[128,8,4096]{2,1,0:T(8,128)(2,1)}), bf16[128,8,4096]{2,1,0:T(8,128)(2,1)}, u32[]{:S(2)}, u32[]{:S(2)}) async-start(bf16[128,8,4096]{2,1,0:T(8,128)(2,1)} %bitcast.94), calls=%async_computation | async-start | bytes 16777216 | tf_op jit(solution)/shard_map/dispatch/all_to_all | solution.py:22
  21.5 5.1 %copy-start.18 = (bf16[256,512]{1,0:T(8,128)(2,1)S(1)}, bf16[256,512]{1,0:T(8,128)(2,1)}, u32[]{:S(2)}) copy-start(bf16[256,512]{1,0:T(8,128)(2,1)} %param.15) | copy-start | bytes 786436
  22.5 4.2 %collective-permute-start.1 = (bf16[128,2560]{0,1:T(8,128)(2,1)}, bf16[128,2560]{0,1:T(8,128)(2,1)S(1)}, u32[]{:S(2)}, u32[]{:S(2)}) collective-permute-start(bf16[128,2560]{0,1:T(8,128)(2,1)} %pad_maximum_fusion.1), channel_id=1, source_target_pairs={{0,8},{1,9},{2,10},{3,11},{4,12},{5,13},{6,14},{7,15},{8,0},{9,1},... | collective-permute-start | bytes 1966088 | tf_op jit(solution)/shard_map/value_second/ppermute | solution.py:268
  128.5 27.2 %collective-permute-start.4 = (bf16[256,1024]{0,1:T(8,128)(2,1)}, bf16[256,1024]{0,1:T(8,128)(2,1)S(1)}, u32[]{:S(2)}, u32[]{:S(2)}) collective-permute-start(bf16[256,1024]{0,1:T(8,128)(2,1)} %get-tuple-element.40), channel_id=1, source_target_pairs={{0,4},{1,5},{2,6},{3,7},{4,0},{5,1},{6,2},{7,3},{8,12},{9,13},{10,... | collective-permute-start | bytes 1572872 | tf_op jit(solution)/shard_map/value_second/ppermute | solution.py:268
  128.8 26.9 %collective-permute-start.5 = (bf16[256,1024]{0,1:T(8,128)(2,1)S(1)}, bf16[256,1024]{0,1:T(8,128)(2,1)S(1)}, u32[]{:S(2)}, u32[]{:S(2)}) collective-permute-start(bf16[256,1024]{0,1:T(8,128)(2,1)S(1)} %get-tuple-element.41), channel_id=1, source_target_pairs={{0,64},{1,65},{2,66},{3,67},{4,68},{5,69},{6,70},{7,71},{8,72},{9,... | collective-permute-start | bytes 1572872 | tf_op jit(solution)/shard_map/value_second/ppermute | solution.py:268
  129.4 26.3 %collective-permute-start.6 = (bf16[256,1024]{0,1:T(8,128)(2,1)S(1)}, bf16[256,1024]{0,1:T(8,128)(2,1)S(1)}, u32[]{:S(2)}, u32[]{:S(2)}) collective-permute-start(bf16[256,1024]{0,1:T(8,128)(2,1)S(1)} %get-tuple-element.42), channel_id=1, source_target_pairs={{0,68},{1,69},{2,70},{3,71},{4,64},{5,65},{6,66},{7,67},{8,76},{9,... | collective-permute-start | bytes 1572872 | tf_op jit(solution)/shard_map/value_second/ppermute | solution.py:268
  132.6 23.2 %collective-permute-start.3 = (bf16[2,256,512]{2,1,0:T(8,128)(2,1)S(1)}, bf16[2,256,512]{2,1,0:T(8,128)(2,1)S(1)}, u32[]{:S(2)}, u32[]{:S(2)}) collective-permute-start(bf16[2,256,512]{2,1,0:T(8,128)(2,1)S(1)} %pad_maximum_fusion.2), channel_id=1, source_target_pairs={{0,48},{1,49},{2,50},{3,51},{4,52},{5,53},{6,54},{7,55},{8,56},{9,... | collective-permute-start | bytes 1572872 | tf_op jit(solution)/shard_map/value_second/ppermute | solution.py:268
  132.6 23.2 %collective-permute-start.2 = (bf16[2,256,512]{2,1,0:T(8,128)(2,1)S(1)}, bf16[2,256,512]{2,1,0:T(8,128)(2,1)S(1)}, u32[]{:S(2)}, u32[]{:S(2)}) collective-permute-start(bf16[2,256,512]{2,1,0:T(8,128)(2,1)S(1)} %pad_maximum_fusion.2), channel_id=1, source_target_pairs={{0,16},{1,17},{2,18},{3,19},{4,20},{5,21},{6,22},{7,23},{8,24},{9,... | collective-permute-start | bytes 1572872 | tf_op jit(solution)/shard_map/value_second/ppermute | solution.py:268
  148.5 7.2 %copy-start.1 = (bf16[1024,1536]{1,0:T(8,128)(2,1)}, bf16[1024,1536]{1,0:T(8,128)(2,1)S(1)}, u32[]{:S(2)}) copy-start(bf16[1024,1536]{1,0:T(8,128)(2,1)S(1)} %get-tuple-element.37.hidden_ref) | copy-start | bytes 9437188
  157.8 44.0 %all-to-all-start.2 = ((bf16[128,8,1152]{2,1,0:T(8,128)(2,1)}), bf16[128,8,1152]{2,1,0:T(8,128)(2,1)S(1)}, u32[]{:S(2)}, u32[]{:S(2)}) async-start(bf16[128,8,1152]{2,1,0:T(8,128)(2,1)} %bitcast.95), calls=%async_computation.2 | async-start | bytes 4718592 | tf_op jit(solution)/shard_map/return/all_to_all | solution.py:22
  166.9 5.1 %copy-start.12 = (bf16[256,1024]{0,1:T(8,128)(2,1)S(1)}, bf16[256,1024]{0,1:T(8,128)(2,1)}, u32[]{:S(2)}) copy-start(bf16[256,1024]{0,1:T(8,128)(2,1)} %copy-done.11) | copy-start | bytes 1572868
  166.9 5.2 %copy-start.14 = (bf16[256,1024]{0,1:T(8,128)(2,1)S(1)}, bf16[256,1024]{0,1:T(8,128)(2,1)}, u32[]{:S(2)}) copy-start(bf16[256,1024]{0,1:T(8,128)(2,1)} %copy-done.13) | copy-start | bytes 1572868
  166.9 5.3 %copy-start.16 = (bf16[256,1024]{0,1:T(8,128)(2,1)S(1)}, bf16[256,1024]{0,1:T(8,128)(2,1)}, u32[]{:S(2)}) copy-start(bf16[256,1024]{0,1:T(8,128)(2,1)} %copy-done.15) | copy-start | bytes 1572868
  168.0 32.5 %collective-permute-start.8 = (bf16[256,512]{1,0:T(8,128)(2,1)S(1)}, bf16[256,512]{1,0:T(8,128)(2,1)S(1)}, u32[]{:S(2)}, u32[]{:S(2)}) collective-permute-start(bf16[256,512]{1,0:T(8,128)(2,1)S(1)} %slice_bitcast_fusion), channel_id=1, source_target_pairs={{0,48},{1,49},{2,50},{3,51},{4,52},{5,53},{6,54},{7,55},{8,56},{9,... | collective-permute-start | bytes 786440 | tf_op jit(solution)/shard_map/value_third/ppermute | solution.py:268
  171.9 29.9 %collective-permute-start.7 = (bf16[256,512]{1,0:T(8,128)(2,1)S(1)}, bf16[256,512]{1,0:T(8,128)(2,1)}, u32[]{:S(2)}, u32[]{:S(2)}) collective-permute-start(bf16[256,512]{1,0:T(8,128)(2,1)S(1)} %slice_bitcast_fusion.1), channel_id=1, source_target_pairs={{0,16},{1,17},{2,18},{3,19},{4,20},{5,21},{6,22},{7,23},{8,24},{9,... | collective-permute-start | bytes 786440 | tf_op jit(solution)/shard_map/value_third/ppermute | solution.py:268
  172.2 7.0 %copy-start.2 = (bf16[1024,1536]{1,0:T(8,128)(2,1)S(1)}, bf16[1024,1536]{1,0:T(8,128)(2,1)}, u32[]{:S(2)}) copy-start(bf16[1024,1536]{1,0:T(8,128)(2,1)} %copy-done.1) | copy-start | bytes 9437188
  174.0 22.6 %collective-permute-start.11 = (bf16[4,32,512]{2,1,0:T(8,128)(2,1)S(1)}, bf16[4,32,512]{2,1,0:T(8,128)(2,1)S(1)}, u32[]{:S(2)}, u32[]{:S(2)}) collective-permute-start(bf16[4,32,512]{2,1,0:T(8,128)(2,1)S(1)} %get-tuple-element.78), channel_id=1, source_target_pairs={{0,3},{1,0},{2,1},{3,2},{4,7},{5,4},{6,5},{7,6},{8,11},{9,8},{10,9... | collective-permute-start | bytes 393224 | tf_op jit(solution)/shard_map/value_third/ppermute | solution.py:268
  176.9 20.7 %collective-permute-start.9 = (bf16[4,32,512]{2,1,0:T(8,128)(2,1)S(1)}, bf16[4,32,512]{2,1,0:T(8,128)(2,1)S(1)}, u32[]{:S(2)}, u32[]{:S(2)}) collective-permute-start(bf16[4,32,512]{2,1,0:T(8,128)(2,1)S(1)} %get-tuple-element.79), channel_id=1, source_target_pairs={{0,1},{1,2},{2,3},{3,0},{4,5},{5,6},{6,7},{7,4},{8,9},{9,10},{10,1... | collective-permute-start | bytes 393224 | tf_op jit(solution)/shard_map/value_third/ppermute | solution.py:268
  176.9 23.5 %collective-permute-start.10 = (bf16[4,32,512]{2,1,0:T(8,128)(2,1)S(1)}, bf16[4,32,512]{2,1,0:T(8,128)(2,1)S(1)}, u32[]{:S(2)}, u32[]{:S(2)}) collective-permute-start(bf16[4,32,512]{2,1,0:T(8,128)(2,1)S(1)} %get-tuple-element.80), channel_id=1, source_target_pairs={{0,2},{1,3},{2,0},{3,1},{4,6},{5,7},{6,4},{7,5},{8,10},{9,11},{10,... | collective-permute-start | bytes 393224 | tf_op jit(solution)/shard_map/value_third/ppermute | solution.py:268
  196.6 3.9 %copy-start.20 = (bf16[4,32,512]{2,1,0:T(8,128)(2,1)}, bf16[4,32,512]{2,1,0:T(8,128)(2,1)S(1)}, u32[]{:S(2)}) copy-start(bf16[4,32,512]{2,1,0:T(8,128)(2,1)S(1)} %collective-permute-done.11) | copy-start | bytes 393220
  201.8 10.5 %copy-start.6 = (bf16[2,256,512]{2,1,0:T(8,128)(2,1)S(1)}, bf16[2,256,512]{2,1,0:T(8,128)(2,1)}, u32[]{:S(2)}) copy-start(bf16[2,256,512]{2,1,0:T(8,128)(2,1)} %copy-done.5) | copy-start | bytes 1572868
  201.8 86.2 %all-to-all-start.1 = ((bf16[128,8,3072]{2,1,0:T(8,128)(2,1)}), bf16[128,8,3072]{2,1,0:T(8,128)(2,1)}, u32[]{:S(2)}, u32[]{:S(2)}) async-start(bf16[128,8,3072]{2,1,0:T(8,128)(2,1)} %bitcast.96), calls=%async_computation.1 | async-start | bytes 12582912 | tf_op jit(solution)/shard_map/return/all_to_all | solution.py:22
  214.9 12.6 %collective-permute-start.15 = (bf16[4,2,256,512]{3,2,1,0:T(8,128)(2,1)}, bf16[4,2,256,512]{3,2,1,0:T(8,128)(2,1)}, u32[]{:S(2)}, u32[]{:S(2)}) collective-permute-start(bf16[4,2,256,512]{3,2,1,0:T(8,128)(2,1)} %pad_maximum_fusion), channel_id=1, source_target_pairs={{0,8},{1,9},{2,10},{3,11},{4,12},{5,13},{6,14},{7,15},{8,0},{9,1},... | collective-permute-start | bytes 6291464 | tf_op jit(solution)/shard_map/value_last/ppermute | solution.py:268
  216.8 76.3 %collective-permute-start.14 = (f32[32,512]{1,0:T(8,128)}, f32[32,512]{1,0:T(8,128)}, u32[]{:S(2)}, u32[]{:S(2)}) collective-permute-start(f32[32,512]{1,0:T(8,128)} %get-tuple-element.89), channel_id=1, source_target_pairs={{0,48},{1,49},{2,50},{3,51},{4,52},{5,53},{6,54},{7,55},{8,56},{9,... | collective-permute-start | bytes 196616 | tf_op jit(solution)/shard_map/value_last/ppermute | solution.py:268
  219.8 73.3 %collective-permute-start.13 = (f32[32,512]{1,0:T(8,128)}, f32[32,512]{1,0:T(8,128)}, u32[]{:S(2)}, u32[]{:S(2)}) collective-permute-start(f32[32,512]{1,0:T(8,128)} %get-tuple-element.90), channel_id=1, source_target_pairs={{0,32},{1,33},{2,34},{3,35},{4,36},{5,37},{6,38},{7,39},{8,40},{9,... | collective-permute-start | bytes 196616 | tf_op jit(solution)/shard_map/value_last/ppermute | solution.py:268
  220.1 3.6 %copy-start.10 = (s32[128,8]{1,0:T(8,128)S(1)}, s32[128,8]{1,0:T(8,128)}, u32[]{:S(2)}) copy-start(s32[128,8]{1,0:T(8,128)} %add_select_fusion.slot_ref) | copy-start | bytes 12292
  220.1 6.3 %copy-start.3 = (bf16[128,1024]{1,0:T(8,128)(2,1)S(1)}, bf16[128,1024]{1,0:T(8,128)(2,1)}, u32[]{:S(2)}) copy-start(bf16[128,1024]{1,0:T(8,128)(2,1)} %mix_weights.1.mix_ref) | copy-start | bytes 786436
  220.1 73.0 %collective-permute-start.12 = (f32[32,512]{1,0:T(8,128)}, f32[32,512]{1,0:T(8,128)}, u32[]{:S(2)}, u32[]{:S(2)}) collective-permute-start(f32[32,512]{1,0:T(8,128)} %get-tuple-element.91), channel_id=1, source_target_pairs={{0,16},{1,17},{2,18},{3,19},{4,20},{5,21},{6,22},{7,23},{8,24},{9,... | collective-permute-start | bytes 196616 | tf_op jit(solution)/shard_map/value_last/ppermute | solution.py:268
  (14 other events, 17.2 us)

commit v3 on v2

--- a/solution.py
+++ b/solution.py
@@ -1,13 +1,15 @@
-import functools
+import math
 
 import jax
 import jax.numpy as jnp
 from jax import lax
 from jax.experimental import pallas as pl
 from jax.experimental.pallas import tpu as pltpu
-from jax.sharding import PartitionSpec as P
-
-AXES = ("dp", "expert")
+from jax.sharding import Mesh, PartitionSpec as P
+
+PLACE = ("x_lo", "z", "core", "x_hi", "y")
+SIZES = (2, 4, 2, 2, 4)
+ORDER = ("z", "y", "x_hi", "x_lo", "core")
 MIB = 1024 * 1024
 LANES = 128
 CAPACITY = 8
@@ -16,6 +18,11 @@
 
 def dot_nt(left, right):
     return lax.dot_general(left, right, NT, preferred_element_type=jnp.float32)
+
+
+def in_order(device):
+    x_lo, z, core, x_hi, y = device // 64, device // 16 % 4, device // 8 % 2, device // 4 % 2, device % 4
+    return (((z * 4 + y) * 2 + x_hi) * 2 + x_lo) * 2 + core
 
 
 def exchange(array, axes):
@@ -29,7 +36,8 @@
     slot = lax.broadcasted_iota(jnp.int32, (rows, tokens), 0) + pl.program_id(0) * rows
     hit = None
     for k in range(top):
-        name = jnp.where(live, ids_ref[k : k + 1, :] * CAPACITY + slots_ref[k : k + 1, :], -1)
+        name = in_order(ids_ref[k : k + 1, :]) * CAPACITY + slots_ref[k : k + 1, :]
+        name = jnp.where(live, name, -1)
         hit = name == slot if hit is None else hit | (name == slot)
     pick = jnp.where(hit, 1.0, 0.0).astype(jnp.bfloat16)
     step = 1024
@@ -206,66 +214,49 @@
     )(mix, returned, *before)
 
 
-def place(index):
-    dp, expert = index // 8, index % 8
-    return [dp // 8, dp // 2 % 4, dp % 2, expert // 4, expert % 4]
-
-
-def shift(array, axis, step):
-    sizes = (2, 4, 2, 2, 4)
+def term_kernel(place_ref, *refs):
+    packs, (own_ref, *sent_refs), term_ref = refs[:4], refs[4:8], refs[8]
+    cols = packs[0].shape[1] // 2
+    term = None
+    for pack in packs:
+        one = lax.dot_general(
+            pack[:, :cols], pack[:, cols:], (((0,), (0,)), ((), ())), preferred_element_type=jnp.float32
+        )
+        term = one if term is None else term + one
+    term_ref[...] = term
+    rows = cols // 16
+    for k, out_ref in enumerate((own_ref, *sent_refs)):
+        at = lax.rem(place_ref[0] + k, 4)
+        for z in range(4):
+            start = pl.multiple_of(z * 4 * rows + at * rows, rows)
+            out_ref[z * rows : (z + 1) * rows, :] = term_ref[pl.ds(start, rows), :].astype(out_ref.dtype)
+
+
+def split_terms(place, packs):
+    cols = packs[0].shape[1] // 2
+    shape = (cols // 4, cols)
+    return pl.pallas_call(
+        term_kernel,
+        in_specs=[pl.BlockSpec(memory_space=pltpu.SMEM)] + [pl.BlockSpec(memory_space=pltpu.VMEM)] * 4,
+        out_specs=[pl.BlockSpec(memory_space=pltpu.VMEM)] * 4,
+        out_shape=[jax.ShapeDtypeStruct(shape, jnp.float32)] + [jax.ShapeDtypeStruct(shape, jnp.bfloat16)] * 3,
+        scratch_shapes=[pltpu.VMEM((cols, cols), jnp.float32)],
+        compiler_params=pltpu.CompilerParams(vmem_limit_bytes=16 * MIB),
+        cost_estimate=pl.CostEstimate(flops=1, bytes_accessed=1, transcendentals=0),
+        name="split_terms",
+    )(place, *packs)
+
+
+def shift(array, axes, steps):
+    sizes = [lax.axis_size(axis) for axis in axes]
     pairs = []
-    for source in range(128):
-        at = place(source)
-        for a, s in zip(axis, step):
-            at[a] = (at[a] + s) % sizes[a]
-        pairs.append((source, (((at[0] * 4 + at[1]) * 2 + at[2]) * 2 + at[3]) * 4 + at[4]))
-    return lax.ppermute(array, AXES, pairs)
-
-
-def value_weight_terms(value_input, value_grad):
-    tokens, width = value_input.shape
-    feats = value_grad.shape[1]
-    dp, expert = lax.axis_index("dp"), lax.axis_index("expert")
-    x_lo, z, core, x_hi, y = dp // 8, dp // 2 % 4, dp % 2, expert // 4, expert % 4
-    parts = value_input.reshape(tokens, 2, 4, 2, 2, width // 32).transpose(3, 0, 1, 4, 2, 5)
-    parts = parts.reshape(2, tokens, width // 2)
-    own = jnp.where(core == 0, parts[0], parts[1])
-    other = shift(jnp.where(core == 0, parts[1], parts[0]), (2,), (1,))
-    other_grad = shift(value_grad, (2,), (1,))
-    term = jnp.einsum("tr,tk->rk", own, value_grad, preferred_element_type=jnp.float32)
-    term = term + jnp.einsum("tr,tk->rk", other, other_grad, preferred_element_type=jnp.float32)
-    term = term.reshape(4, width // 8, feats)
-
-    def pick(array, at, dim):
-        return lax.dynamic_index_in_dim(array, at, dim, keepdims=False)
-
-    total = pick(term, x_lo * 2 + x_hi, 0)
-    for a, b in ((1, 0), (1, 1), (0, 1)):
-        piece = pick(term, (x_lo + a) % 2 * 2 + (x_hi + b) % 2, 0).astype(jnp.bfloat16)
-        total = total + shift(piece, (0, 3), (a, b)).astype(jnp.float32)
-    for axis, here, lead in ((4, y, (4, 4)), (1, z, (4,))):
-        term = total.reshape(*lead, -1, feats)
-        dim = len(lead) - 1
-        total = pick(term, here, dim)
-        for k in (1, 3, 2):
-            total = total + shift(pick(term, (here + k) % 4, dim), (axis,), (k,))
-    return total.reshape(-1, feats)
-
-
-def place(index):
-    dp, expert = index // 8, index % 8
-    return [dp // 8, dp // 2 % 4, dp % 2, expert // 4, expert % 4]
-
-
-def shift(array, axis, step):
-    sizes = (2, 4, 2, 2, 4)
-    pairs = []
-    for source in range(128):
-        at = place(source)
-        for a, s in zip(axis, step):
-            at[a] = (at[a] + s) % sizes[a]
-        pairs.append((source, (((at[0] * 4 + at[1]) * 2 + at[2]) * 2 + at[3]) * 4 + at[4]))
-    return lax.ppermute(array, AXES, pairs)
+    for source in range(math.prod(sizes)):
+        target, rest, scale = 0, source, 1
+        for size, step in zip(reversed(sizes), reversed(steps)):
+            target += (rest % size + step) % size * scale
+            rest, scale = rest // size, scale * size
+        pairs.append((source, target))
+    return lax.ppermute(array, axes, pairs)
 
 
 def pick(array, at, dim):
@@ -292,36 +283,32 @@
     w_down,
 ):
     tokens, width = out_grad.shape
-    dp = lax.axis_size("dp")
-    experts = lax.axis_size("expert")
-    devices = dp * experts
-    capacity = gate_act.shape[2]
-    ffw = gate_act.shape[3]
+    feats = value_grad.shape[1]
+    devices, capacity, ffw = gate_act.shape[1:]
     slots = devices * capacity
+    x_lo, z, core, x_hi, y = (lax.axis_index(axis) for axis in PLACE)
+    half, cols = width // 2, width // 16
+    in_parts = ((0, 1024), (1024, 3072))
 
     live = jnp.arange(tokens, dtype=jnp.int32) < seq_lengths[0]
-    slot = jnp.where(live[:, None], route_ids * capacity + route_slots, -1)
-
-    in_parts = ((0, 1024), (1024, 3072))
-    dp, expert = lax.axis_index("dp"), lax.axis_index("expert")
-    x_lo, z, core, x_hi, y = dp // 8, dp // 2 % 4, dp % 2, expert // 4, expert % 4
-    feats = value_grad.shape[1]
-    half, cols = width // 2, width // 16
+    slot = jnp.where(live[:, None], in_order(route_ids) * capacity + route_slots, -1)
 
     with jax.named_scope("value_first"):
-        beside = shift(value_weight, (0,), (1,))
+        beside = shift(value_weight, ("x_lo",), (1,))
 
     with jax.named_scope("dispatch"):
         send = build_rows(seq_lengths, route_ids.T, route_slots.T, out_grad, slots)
-        send, beside, value_in = lax.optimization_barrier((send, beside, value_input))
-        routed = exchange(send.reshape(devices, capacity, width), AXES).reshape(slots, width)
+        send, beside, value_in, gate_act, up_act = lax.optimization_barrier(
+            (send, beside, value_input, gate_act, up_act)
+        )
+        routed = exchange(send.reshape(devices, capacity, width), ORDER).reshape(slots, width)
 
     with jax.named_scope("value_second"):
         pair = jnp.stack(by_core(x_lo, value_weight, beside))
         halves = value_in.reshape(tokens, 8, 2, cols)
         own, other = by_core(core, halves[:, :, 0], halves[:, :, 1])
         other = jnp.concatenate([other.reshape(tokens, half), value_grad], axis=1)
-        other = shift(other, (2,), (1,))
+        other = shift(other, ("core",), (1,))
         inputs = jnp.concatenate([own.reshape(tokens, half), other[:, :half]])
         inputs = inputs.reshape(2 * tokens, 2, 4, 2, cols // 2)
         grads = jnp.concatenate([value_grad, other[:, half:]])
@@ -335,35 +322,33 @@
         kept = along_x(0, 0)
         packs = [along_x(*step) for step in steps]
         mix = mix_weights(slot, route_weights.astype(jnp.float32), slots)
-        routed, mix, pair, kept, *packs = lax.optimization_barrier((routed, mix, pair, kept, *packs))
-        below, above = shift(pair, (1,), (1,)), shift(pair, (1,), (3,))
-        arrived = [shift(pack, (0, 3), step) for pack, step in zip(packs, steps)]
+        gate_act, up_act = (
+            a.reshape(*SIZES, capacity, ffw).transpose(1, 4, 3, 0, 2, 5, 6).reshape(slots, ffw)
+            for a in (gate_act, up_act)
+        )
+        routed, mix, pair, kept, gate_act, up_act, *packs = lax.optimization_barrier(
+            (routed, mix, pair, kept, gate_act, up_act, *packs)
+        )
+        below, above = shift(pair, ("z",), (1,)), shift(pair, ("z",), (3,))
+        arrived = [shift(pack, ("x_lo", "x_hi"), step) for pack, step in zip(packs, steps)]
 
     with jax.named_scope("experts"):
-        hidden, score = hidden_grads(
-            routed, w_down[0], gate_act.reshape(slots, ffw), up_act.reshape(slots, ffw), in_parts[0][1]
-        )
+        hidden, score = hidden_grads(routed, w_down[0], gate_act, up_act, in_parts[0][1])
         slot_first = slot_grads(hidden, w_gate[0], w_up[0], *in_parts[0], score)
         slot_second = slot_grads(hidden, w_gate[0], w_up[0], *in_parts[1])
 
     with jax.named_scope("value_third"):
         held = lax.optimization_barrier((slot_first, below, above, *arrived))
         slot_first, below, above = held[:3]
-        halfway = [shift(below[0], (1,), (1,)), shift(above[1], (1,), (3,))]
-        packs = jnp.concatenate([kept, *held[3:]])
-        term = jnp.einsum(
-            "tr,tk->rk", packs[:, : 2 * cols], packs[:, 2 * cols :], preferred_element_type=jnp.float32
-        )
-        term = term.reshape(4, 4, cols // 8, feats)
-        total = pick(term, y, 1)
-        sent = [pick(term, (y + k) % 4, 1).astype(jnp.bfloat16) for k in (1, 2, 3)]
-        terms = [shift(t, (4,), (k,)) for t, k in zip(sent, (1, 2, 3))]
+        total, *sent = split_terms(y.reshape(1), (kept, *held[3:]))
+        terms = [shift(t, ("y",), (k,)) for t, k in zip(sent, (1, 2, 3))]
+        halfway = [shift(below[0], ("z",), (1,)), shift(above[1], ("z",), (3,))]
 
     with jax.named_scope("return"):
-        first = exchange(slot_first.reshape(devices, capacity, -1), AXES).reshape(slots, -1)
+        first = exchange(slot_first.reshape(devices, capacity, -1), ORDER).reshape(slots, -1)
         held = lax.optimization_barrier((slot_second, *halfway, *terms))
         slot_second, halfway, terms = held[0], held[1:3], held[3:]
-        second = exchange(slot_second.reshape(devices, capacity, -1), AXES).reshape(slots, -1)
+        second = exchange(slot_second.reshape(devices, capacity, -1), ORDER).reshape(slots, -1)
         moe_input_grad = combine(mix, first, *in_parts[0], width)
         scores = first[:, in_parts[0][1]].astype(jnp.float32)
         weight_grad = jnp.sum(
@@ -374,10 +359,12 @@
     with jax.named_scope("value_last"):
         for part in terms:
             total = total + part.astype(jnp.float32)
-        last = [shift(pick(total, (z + k) % 4, 0), (1,), (k,)) for k in (1, 2, 3)]
+        total = total.reshape(4, cols // 8, feats)
+        last = [shift(pick(total, (z + k) % 4, 0), ("z",), (k,)) for k in (1, 2, 3)]
+        total = pick(total, z, 0)
 
         ring = jnp.stack([pair, above, jnp.stack(halfway), below])
-        across = shift(ring, (2,), (1,))
+        across = shift(ring, ("core",), (1,))
 
         def products(weight):
             out = jnp.einsum("tk,ixrk->ixtr", value_grad, weight, preferred_element_type=jnp.float32)
@@ -389,29 +376,30 @@
 
     with jax.named_scope("finish"):
         moe_input_grad, *last = lax.optimization_barrier((moe_input_grad, *last))
-        value_weight_grad = pick(total, z, 0) + last[0] + last[1] + last[2]
+        value_weight_grad = total + last[0] + last[1] + last[2]
     return (moe_input_grad, weight_grad, value_input_grad, value_weight_grad)
 
 
 def solution(mesh):
-    split = P(AXES, None)
+    places = Mesh(mesh.devices.reshape(SIZES), PLACE)
+    split = P(PLACE, None)
     return jax.shard_map(
         body,
-        mesh=mesh,
+        mesh=places,
         in_specs=(
             split,
             split,
-            P("dp", None),
-            split,
-            split,
-            split,
-            P(AXES),
-            split,
-            P(AXES, None, None, None),
-            P(AXES, None, None, None),
-            P(AXES, None, None),
-            P(AXES, None, None),
-            P(AXES, None, None),
+            P(PLACE[:3], None),
+            split,
+            split,
+            split,
+            P(PLACE),
+            split,
+            P(PLACE, None, None, None),
+            P(PLACE, None, None, None),
+            P(PLACE, None, None),
+            P(PLACE, None, None),
+            P(PLACE, None, None),
         ),
         out_specs=(split, split, split, split),
         check_vma=False,

time: 300 us -> 290 us (0.967); the launches traced: 295 us -> 288 us
  waiting for transfers between devices: 163 us -> 143 us
  starting transfers between devices: 50.1 us -> 56.7 us
  local copies, waits for them, and re-layouts: 16.7 us -> 22.9 us
    all_to_all x3, waiting for transfers between devices: 155 us -> 137 us  [exchange(): return lax.all_to_all(array, axes, split_axis=0, concat_axis=0, tiled=True)]
    ppermute x16, starting transfers between devices: 20.3 us -> 25.6 us  [shift(): return lax.ppermute(array, axes, pairs)]
    reshape x0 -> x6, local copies, waits for them, and re-layouts: none -> 3.28 us  [the longest x2 2.72 us: body(): a.reshape(*SIZES, capacity, ffw).transpose(1, 4, 3, 0, 2, 5, 6)]
  transfers between devices with their start and end apart: 19 -> 19, of which waited for: 5 -> 5; matrix products, arithmetic and copies ran while one was open for 8% -> 10% of each run, Pallas kernels for 16% -> 17%
where the time goes in v3:
time: 290 us; the launch traced here: 288 us
  waiting for transfers between devices  143 us (49%)
  starting transfers between devices  56.7 us (20%)
  Pallas kernels  47.7 us (16%)
  local copies, waits for them, and re-layouts  22.9 us (8%)
  other arithmetic  11.9 us (4%)
  matrix products  4.58 us (2%)
    all_to_all x3, waiting for transfers between devices, exchange(): return lax.all_to_all(array, axes, split_axis=0, concat_axis=0, tiled=True)  137 us
    all_to_all x3, starting transfers between devices, exchange(): return lax.all_to_all(array, axes, split_axis=0, concat_axis=0, tiled=True)  31.1 us
    ppermute x16, starting transfers between devices, shift(): return lax.ppermute(array, axes, pairs)  25.6 us
    pallas_call x2, Pallas kernels, slot_grads(): pl.pallas_call(slot_kernel, grid=(width // block,), in_specs=[pl.BlockSpe...  20.7 us
    unnamed x59, local copies, waits for them, and re-layouts  12.5 us
    pallas_call x1, Pallas kernels, hidden_grads(): pl.pallas_call(hidden_kernel, grid=(slots // rows,), in_specs=[pl.BlockSp...  11.1 us
    pallas_call x1, Pallas kernels, build_rows(): pl.pallas_call(rows_kernel, grid=(slots // rows,), in_specs=[pl.BlockSpec...  6.56 us
    pallas_call x2, Pallas kernels, combine(): pl.pallas_call(combine_kernel, grid=(cols // block,), in_specs=[pl.BlockS...  6.18 us
  transfers between devices with their start and end apart: 19, of which 5 were waited for; matrix products, arithmetic and copies ran while one was open for 10% of the time, Pallas kernels for 17%

profile of v3, /device:TPU:0, one launch (start us, length us, event | category | flops | bytes accessed | tf_op | source)
XLA Modules:
  0.0 288.3 jit_solution(15580281955603196620)
XLA Ops:
  0.6 1.7 collective-permute-start
  2.9 6.6 %build_rows.1 = bf16[1024,4096]{1,0:T(8,128)(2,1)} custom-call(s32[1]{0:T(128)} %copy.122.length_ref, s32[8,128]{1,0:T(8,128)} %bitcast.107, s32[8,128]{1,0:T(8,128)} %bitcast.108, bf16[128,4096]{1,0:T(8,128)(2,1)} %grad_ref.1), custom_call_target="tpu_custom_call" | custom-call | flops 1073741824 | bytes 9437184 | tf_op jit(solution)/shard_map/dispatch/build_rows/pallas_call | solution.py:53
  9.5 11.3 %all-to-all-start = ((bf16[128,8,4096]{2,1,0:T(8,128)(2,1)}), bf16[128,8,4096]{2,1,0:T(8,128)(2,1)}, u32[]{:S(2)}, u32[]{:S(2)}) async-start(bf16[128,8,4096]{2,1,0:T(8,128)(2,1)} %bitcast.81), calls=%async_computation | async-start | bytes 16777216 | tf_op jit(solution)/shard_map/dispatch/all_to_all | solution.py:29
  25.3 2.4 mix_weights.1.mix_ref
  27.8 1.4 copy.105
  29.7 1.3 copy.106
  34.4 1.3 pad_maximum_fusion.7
  35.7 83.5 %all-to-all-done = bf16[128,8,4096]{2,1,0:T(8,128)(2,1)} async-done(((bf16[128,8,4096]{2,1,0:T(8,128)(2,1)}), bf16[128,8,4096]{2,1,0:T(8,128)(2,1)}, u32[]{:S(2)}, u32[]{:S(2)}) %all-to-all-start) | async-done | bytes 8388640 | tf_op jit(solution)/shard_map/dispatch/all_to_all | solution.py:29
  119.2 3.2 %collective-permute-start.3 = (bf16[2,256,512]{2,1,0:T(8,128)(2,1)S(1)}, bf16[2,256,512]{2,1,0:T(8,128)(2,1)S(1)}, u32[]{:S(2)}, u32[]{:S(2)}) collective-permute-start(bf16[2,256,512]{2,1,0:T(8,128)(2,1)S(1)} %pad_maximum_fusion.2), channel_id=1, source_target_pairs={{0,48},{16,0},{32,16},{48,32},{1,49},{17,1},{33,17},{49,33},{2,50}... | collective-permute-start | bytes 1572872 | tf_op jit(solution)/shard_map/value_second/ppermute | solution.py:259
  122.5 2.1 collective-permute-start.4
  124.6 1.4 collective-permute-start.5
  126.0 2.7 collective-permute-start.6
  128.7 2.8 copy-done
  131.5 11.1 %hidden_grads.1 = (bf16[1024,1536]{1,0:T(8,128)(2,1)S(1)}, bf16[1024,1152]{1,0:T(8,128)(2,1)}) custom-call(bf16[1024,4096]{1,0:T(8,128)(2,1)} %bitcast.3.x_ref, bf16[768,4096]{1,0:T(8,128)(2,1)S(1)} %bitcast.80, bf16[1024,768]{1,0:T(8,128)(2,1)} %bitcast.84, bf16[1024,768]{1,0:T(8,128)(2,1)} %bitcast.85), custom_call_target="tpu_custom_call" | custom-call | flops 1 | bytes 1 | tf_op jit(solution)/shard_map/experts/hidden_grads/pallas_call | solution.py:97
  142.6 7.2 %slot_grads.3 = bf16[1024,1152]{1,0:T(8,128)(2,1)} custom-call(bf16[1024,1536]{1,0:T(8,128)(2,1)S(1)} %get-tuple-element.49.hidden_ref, bf16[4096,768]{1,0:T(8,128)(2,1)} %bitcast.86, bf16[4096,768]{1,0:T(8,128)(2,1)} %bitcast.88, bf16[1024,1152]{1,0:T(8,128)(2,1)} %get-tuple-element.50.refs_0_), custom_call_target="tpu_custom_call", output_to_operand_aliasing={{}: (3, {})} | custom-call | flops 1 | bytes 1 | tf_op jit(solution)/shard_map/experts/slot_grads/pallas_call | solution.py:149
  151.7 11.0 %all-to-all-start.2 = ((bf16[128,8,1152]{2,1,0:T(8,128)(2,1)}), bf16[128,8,1152]{2,1,0:T(8,128)(2,1)S(1)}, u32[]{:S(2)}, u32[]{:S(2)}) async-start(bf16[128,8,1152]{2,1,0:T(8,128)(2,1)} %bitcast.82), calls=%async_computation.2 | async-start | bytes 4718592 | tf_op jit(solution)/shard_map/return/all_to_all | solution.py:29
  165.9 2.4 collective-permute-start.8
  173.1 2.8 collective-permute-start.10
  175.9 1.4 collective-permute-start.11
  177.3 13.5 %slot_grads.2 = bf16[1024,3072]{1,0:T(8,128)(2,1)} custom-call(bf16[1024,1536]{1,0:T(8,128)(2,1)S(1)} %copy-done.2, bf16[4096,768]{1,0:T(8,128)(2,1)} %bitcast.87, bf16[4096,768]{1,0:T(8,128)(2,1)} %bitcast.89), custom_call_target="tpu_custom_call" | custom-call | flops 9663676416 | bytes 18874368 | tf_op jit(solution)/shard_map/experts/slot_grads/pallas_call | solution.py:149
  190.8 2.8 collective-permute-done.9
  193.5 2.9 %collective-permute-done.10 = bf16[128,512]{1,0:T(8,128)(2,1)S(1)} collective-permute-done((bf16[128,512]{1,0:T(8,128)(2,1)S(1)}, bf16[128,512]{1,0:T(8,128)(2,1)S(1)}, u32[]{:S(2)}, u32[]{:S(2)}) %collective-permute-start.10) | collective-permute-done | bytes 131104 | tf_op jit(solution)/shard_map/value_third/ppermute | solution.py:259
  197.9 8.8 %all-to-all-start.1 = ((bf16[128,8,3072]{2,1,0:T(8,128)(2,1)}), bf16[128,8,3072]{2,1,0:T(8,128)(2,1)}, u32[]{:S(2)}, u32[]{:S(2)}) async-start(bf16[128,8,3072]{2,1,0:T(8,128)(2,1)} %bitcast.83), calls=%async_computation.1 | async-start | bytes 12582912 | tf_op jit(solution)/shard_map/return/all_to_all | solution.py:29
  207.8 2.8 pad_maximum_fusion
  213.6 3.2 %collective-permute-start.13 = (f32[32,512]{1,0:T(8,128)}, f32[32,512]{1,0:T(8,128)}, u32[]{:S(2)}, u32[]{:S(2)}) collective-permute-start(f32[32,512]{1,0:T(8,128)} %get-tuple-element.103), channel_id=1, source_target_pairs={{0,32},{16,48},{32,0},{48,16},{1,33},{17,49},{33,1},{49,17},{2,34}... | collective-permute-start | bytes 196616 | tf_op jit(solution)/shard_map/value_last/ppermute | solution.py:259
  218.0 2.3 fusion
  221.7 1.4 copy.111
  224.3 2.3 fusion.1
  227.2 1.3 copy.112
  228.5 53.2 %all-to-all-done.1 = bf16[128,8,3072]{2,1,0:T(8,128)(2,1)} async-done(((bf16[128,8,3072]{2,1,0:T(8,128)(2,1)}), bf16[128,8,3072]{2,1,0:T(8,128)(2,1)}, u32[]{:S(2)}, u32[]{:S(2)}) %all-to-all-start.1) | async-done | bytes 6291488 | tf_op jit(solution)/shard_map/return/all_to_all | solution.py:29
  281.7 5.0 %combine.3 = bf16[128,4096]{1,0:T(8,128)(2,1)} custom-call(bf16[128,1024]{1,0:T(8,128)(2,1)S(1)} %copy-done.3, bf16[1024,3072]{1,0:T(8,128)(2,1)} %bitcast.28.rows_ref, bf16[128,4096]{1,0:T(8,128)(2,1)} %combine.2.refs_0_), custom_call_target="tpu_custom_call", output_to_operand_aliasing={{}: (2, {})} | custom-call | flops 805306368 | bytes 7077888 | tf_op jit(solution)/shard_map/return/combine/pallas_call | solution.py:198
  286.8 1.6 fusion.24
  (112 shorter events, 28.0 us)
Async XLA Ops:
  0.6 8.9 %collective-permute-start = (bf16[256,512]{1,0:T(8,128)(2,1)}, bf16[256,512]{1,0:T(8,128)(2,1)S(1)}, u32[]{:S(2)}, u32[]{:S(2)}) collective-permute-start(bf16[256,512]{1,0:T(8,128)(2,1)} %param.15), channel_id=1, source_target_pairs={{0,64},{64,0},{1,65},{65,1},{2,66},{66,2},{3,67},{67,3},{4,68},{68... | collective-permute-start | bytes 786440 | tf_op jit(solution)/shard_map/value_first/ppermute | solution.py:259
  9.5 11.3 %copy-start.25 = (s32[128,8]{0,1:T(8,128)S(1)}, s32[128,8]{0,1:T(8,128)}, u32[]{:S(2)}) copy-start(s32[128,8]{0,1:T(8,128)} %param.17) | copy-start | bytes 12292
  9.5 11.8 %copy-start.26 = (s32[128,8]{0,1:T(8,128)S(1)}, s32[128,8]{0,1:T(8,128)}, u32[]{:S(2)}) copy-start(s32[128,8]{0,1:T(8,128)} %param.18) | copy-start | bytes 12292
  9.5 11.8 %copy-start.17 = (bf16[128,4096]{1,0:T(8,128)(2,1)S(1)}, bf16[128,4096]{1,0:T(8,128)(2,1)}, u32[]{:S(2)}) copy-start(bf16[128,4096]{1,0:T(8,128)(2,1)} %param.13) | copy-start | bytes 3145732
  9.5 109.7 %all-to-all-start = ((bf16[128,8,4096]{2,1,0:T(8,128)(2,1)}), bf16[128,8,4096]{2,1,0:T(8,128)(2,1)}, u32[]{:S(2)}, u32[]{:S(2)}) async-start(bf16[128,8,4096]{2,1,0:T(8,128)(2,1)} %bitcast.81), calls=%async_computation | async-start | bytes 16777216 | tf_op jit(solution)/shard_map/dispatch/all_to_all | solution.py:29
  22.1 5.7 %copy-start.13 = (bf16[1,128,8,768]{3,2,1,0:T(8,128)(2,1)S(1)}, bf16[1,128,8,768]{3,2,1,0:T(8,128)(2,1)}, u32[]{:S(2)}) copy-start(bf16[1,128,8,768]{3,2,1,0:T(8,128)(2,1)} %param.21) | copy-start | bytes 4718596
  23.8 7.4 %collective-permute-start.1 = (bf16[128,2560]{1,0:T(8,128)(2,1)}, bf16[128,2560]{1,0:T(8,128)(2,1)}, u32[]{:S(2)}, u32[]{:S(2)}) collective-permute-start(bf16[128,2560]{1,0:T(8,128)(2,1)} %pad_maximum_fusion.1), channel_id=1, source_target_pairs={{0,8},{8,0},{1,9},{9,1},{2,10},{10,2},{3,11},{11,3},{4,12},{12,4},... | collective-permute-start | bytes 1966088 | tf_op jit(solution)/shard_map/value_second/ppermute | solution.py:259
  31.2 88.0 %copy-start.11 = (bf16[2,256,512]{2,1,0:T(8,128)(2,1)}, bf16[2,256,512]{2,1,0:T(8,128)(2,1)S(1)}, u32[]{:S(2)}) copy-start(bf16[2,256,512]{2,1,0:T(8,128)(2,1)S(1)} %pad_maximum_fusion.2) | copy-start | bytes 1572868
  119.2 30.5 %collective-permute-start.2 = (bf16[2,256,512]{2,1,0:T(8,128)(2,1)S(1)}, bf16[2,256,512]{2,1,0:T(8,128)(2,1)S(1)}, u32[]{:S(2)}, u32[]{:S(2)}) collective-permute-start(bf16[2,256,512]{2,1,0:T(8,128)(2,1)S(1)} %pad_maximum_fusion.2), channel_id=1, source_target_pairs={{0,16},{16,32},{32,48},{48,0},{1,17},{17,33},{33,49},{49,1},{2,18}... | collective-permute-start | bytes 1572872 | tf_op jit(solution)/shard_map/value_second/ppermute | solution.py:259
  119.2 30.5 %collective-permute-start.3 = (bf16[2,256,512]{2,1,0:T(8,128)(2,1)S(1)}, bf16[2,256,512]{2,1,0:T(8,128)(2,1)S(1)}, u32[]{:S(2)}, u32[]{:S(2)}) collective-permute-start(bf16[2,256,512]{2,1,0:T(8,128)(2,1)S(1)} %pad_maximum_fusion.2), channel_id=1, source_target_pairs={{0,48},{16,0},{32,16},{48,32},{1,49},{17,1},{33,17},{49,33},{2,50}... | collective-permute-start | bytes 1572872 | tf_op jit(solution)/shard_map/value_second/ppermute | solution.py:259
  122.5 27.3 %collective-permute-start.4 = (bf16[256,1024]{1,0:T(8,128)(2,1)}, bf16[256,1024]{1,0:T(8,128)(2,1)S(1)}, u32[]{:S(2)}, u32[]{:S(2)}) collective-permute-start(bf16[256,1024]{1,0:T(8,128)(2,1)} %get-tuple-element.52), channel_id=1, source_target_pairs={{0,4},{4,0},{64,68},{68,64},{1,5},{5,1},{65,69},{69,65},{2,6},{6,2... | collective-permute-start | bytes 1572872 | tf_op jit(solution)/shard_map/value_second/ppermute | solution.py:259
  124.6 25.2 %collective-permute-start.5 = (bf16[256,1024]{1,0:T(8,128)(2,1)}, bf16[256,1024]{1,0:T(8,128)(2,1)S(1)}, u32[]{:S(2)}, u32[]{:S(2)}) collective-permute-start(bf16[256,1024]{1,0:T(8,128)(2,1)} %get-tuple-element.53), channel_id=1, source_target_pairs={{0,64},{4,68},{64,0},{68,4},{1,65},{5,69},{65,1},{69,5},{2,66},{6,... | collective-permute-start | bytes 1572872 | tf_op jit(solution)/shard_map/value_second/ppermute | solution.py:259
  126.0 24.6 %collective-permute-start.6 = (bf16[256,1024]{1,0:T(8,128)(2,1)}, bf16[256,1024]{1,0:T(8,128)(2,1)S(1)}, u32[]{:S(2)}, u32[]{:S(2)}) collective-permute-start(bf16[256,1024]{1,0:T(8,128)(2,1)} %get-tuple-element.54), channel_id=1, source_target_pairs={{0,68},{4,64},{64,4},{68,0},{1,69},{5,65},{65,5},{69,1},{2,70},{6,... | collective-permute-start | bytes 1572872 | tf_op jit(solution)/shard_map/value_second/ppermute | solution.py:259
  142.6 7.2 %copy-start.1 = (bf16[1024,1536]{1,0:T(8,128)(2,1)}, bf16[1024,1536]{1,0:T(8,128)(2,1)S(1)}, u32[]{:S(2)}) copy-start(bf16[1024,1536]{1,0:T(8,128)(2,1)S(1)} %get-tuple-element.49.hidden_ref) | copy-start | bytes 9437188
  151.7 46.2 %all-to-all-start.2 = ((bf16[128,8,1152]{2,1,0:T(8,128)(2,1)}), bf16[128,8,1152]{2,1,0:T(8,128)(2,1)S(1)}, u32[]{:S(2)}, u32[]{:S(2)}) async-start(bf16[128,8,1152]{2,1,0:T(8,128)(2,1)} %bitcast.82), calls=%async_computation.2 | async-start | bytes 4718592 | tf_op jit(solution)/shard_map/return/all_to_all | solution.py:29
  162.7 14.6 %copy-start.2 = (bf16[1024,1536]{1,0:T(8,128)(2,1)S(1)}, bf16[1024,1536]{1,0:T(8,128)(2,1)}, u32[]{:S(2)}) copy-start(bf16[1024,1536]{1,0:T(8,128)(2,1)} %copy-done.1) | copy-start | bytes 9437188
  163.8 33.1 %collective-permute-start.7 = (bf16[256,512]{1,0:T(8,128)(2,1)S(1)}, bf16[256,512]{1,0:T(8,128)(2,1)S(1)}, u32[]{:S(2)}, u32[]{:S(2)}) collective-permute-start(bf16[256,512]{1,0:T(8,128)(2,1)S(1)} %slice_bitcast_fusion.1), channel_id=1, source_target_pairs={{0,16},{16,32},{32,48},{48,0},{1,17},{17,33},{33,49},{49,1},{2,18}... | collective-permute-start | bytes 786440 | tf_op jit(solution)/shard_map/value_third/ppermute | solution.py:259
  165.9 32.0 %collective-permute-start.8 = (bf16[256,512]{1,0:T(8,128)(2,1)S(1)}, bf16[256,512]{1,0:T(8,128)(2,1)}, u32[]{:S(2)}, u32[]{:S(2)}) collective-permute-start(bf16[256,512]{1,0:T(8,128)(2,1)S(1)} %slice_bitcast_fusion), channel_id=1, source_target_pairs={{0,48},{16,0},{32,16},{48,32},{1,49},{17,1},{33,17},{49,33},{2,50}... | collective-permute-start | bytes 786440 | tf_op jit(solution)/shard_map/value_third/ppermute | solution.py:259
  172.0 21.6 %collective-permute-start.9 = (bf16[128,512]{1,0:T(8,128)(2,1)S(1)}, bf16[128,512]{1,0:T(8,128)(2,1)S(1)}, u32[]{:S(2)}, u32[]{:S(2)}) collective-permute-start(bf16[128,512]{1,0:T(8,128)(2,1)S(1)} %get-tuple-element.61), channel_id=1, source_target_pairs={{0,1},{1,2},{2,3},{3,0},{4,5},{5,6},{6,7},{7,4},{8,9},{9,10},{10,1... | collective-permute-start | bytes 393224 | tf_op jit(solution)/shard_map/value_third/ppermute | solution.py:259
  173.1 23.4 %collective-permute-start.10 = (bf16[128,512]{1,0:T(8,128)(2,1)S(1)}, bf16[128,512]{1,0:T(8,128)(2,1)S(1)}, u32[]{:S(2)}, u32[]{:S(2)}) collective-permute-start(bf16[128,512]{1,0:T(8,128)(2,1)S(1)} %get-tuple-element.62), channel_id=1, source_target_pairs={{0,2},{1,3},{2,0},{3,1},{4,6},{5,7},{6,4},{7,5},{8,10},{9,11},{10,... | collective-permute-start | bytes 393224 | tf_op jit(solution)/shard_map/value_third/ppermute | solution.py:259
  175.9 20.6 %collective-permute-start.11 = (bf16[128,512]{1,0:T(8,128)(2,1)S(1)}, bf16[128,512]{1,0:T(8,128)(2,1)S(1)}, u32[]{:S(2)}, u32[]{:S(2)}) collective-permute-start(bf16[128,512]{1,0:T(8,128)(2,1)S(1)} %get-tuple-element.63), channel_id=1, source_target_pairs={{0,3},{1,0},{2,1},{3,2},{4,7},{5,4},{6,5},{7,6},{8,11},{9,8},{10,9... | collective-permute-start | bytes 393224 | tf_op jit(solution)/shard_map/value_third/ppermute | solution.py:259
  193.5 3.3 %copy-start.22 = (bf16[128,512]{1,0:T(8,128)(2,1)}, bf16[128,512]{1,0:T(8,128)(2,1)S(1)}, u32[]{:S(2)}) copy-start(bf16[128,512]{1,0:T(8,128)(2,1)S(1)} %collective-permute-done.9) | copy-start | bytes 393220
  197.9 8.9 %copy-start.21 = (bf16[256,512]{1,0:T(8,128)(2,1)S(1)}, bf16[256,512]{1,0:T(8,128)(2,1)}, u32[]{:S(2)}) copy-start(bf16[256,512]{1,0:T(8,128)(2,1)} %copy-done.20) | copy-start | bytes 786436
  197.9 9.9 %copy-start.12 = (bf16[2,256,512]{2,1,0:T(8,128)(2,1)S(1)}, bf16[2,256,512]{2,1,0:T(8,128)(2,1)}, u32[]{:S(2)}) copy-start(bf16[2,256,512]{2,1,0:T(8,128)(2,1)} %copy-done.11) | copy-start | bytes 1572868
  197.9 83.8 %all-to-all-start.1 = ((bf16[128,8,3072]{2,1,0:T(8,128)(2,1)}), bf16[128,8,3072]{2,1,0:T(8,128)(2,1)}, u32[]{:S(2)}, u32[]{:S(2)}) async-start(bf16[128,8,3072]{2,1,0:T(8,128)(2,1)} %bitcast.83), calls=%async_computation.1 | async-start | bytes 12582912 | tf_op jit(solution)/shard_map/return/all_to_all | solution.py:29
  207.8 2.8 copy-start.9
  210.6 13.7 %collective-permute-start.15 = (bf16[4,2,256,512]{3,2,1,0:T(8,128)(2,1)}, bf16[4,2,256,512]{3,2,1,0:T(8,128)(2,1)}, u32[]{:S(2)}, u32[]{:S(2)}) collective-permute-start(bf16[4,2,256,512]{3,2,1,0:T(8,128)(2,1)} %pad_maximum_fusion), channel_id=1, source_target_pairs={{0,8},{8,0},{1,9},{9,1},{2,10},{10,2},{3,11},{11,3},{4,12},{12,4},... | collective-permute-start | bytes 6291464 | tf_op jit(solution)/shard_map/value_last/ppermute | solution.py:259
  212.4 74.4 %collective-permute-start.12 = (f32[32,512]{1,0:T(8,128)}, f32[32,512]{1,0:T(8,128)}, u32[]{:S(2)}, u32[]{:S(2)}) collective-permute-start(f32[32,512]{1,0:T(8,128)} %get-tuple-element.104), channel_id=1, source_target_pairs={{0,16},{16,32},{32,48},{48,0},{1,17},{17,33},{33,49},{49,1},{2,18}... | collective-permute-start | bytes 196616 | tf_op jit(solution)/shard_map/value_last/ppermute | solution.py:259
  213.6 73.2 %collective-permute-start.13 = (f32[32,512]{1,0:T(8,128)}, f32[32,512]{1,0:T(8,128)}, u32[]{:S(2)}, u32[]{:S(2)}) collective-permute-start(f32[32,512]{1,0:T(8,128)} %get-tuple-element.103), channel_id=1, source_target_pairs={{0,32},{16,48},{32,0},{48,16},{1,33},{17,49},{33,1},{49,17},{2,34}... | collective-permute-start | bytes 196616 | tf_op jit(solution)/shard_map/value_last/ppermute | solution.py:259
  216.8 3.6 %copy-start.18 = (s32[128,8]{1,0:T(8,128)S(1)}, s32[128,8]{1,0:T(8,128)}, u32[]{:S(2)}) copy-start(s32[128,8]{1,0:T(8,128)} %broadcast_select_fusion.2.slot_ref) | copy-start | bytes 12292
  216.8 6.3 %copy-start.3 = (bf16[128,1024]{1,0:T(8,128)(2,1)S(1)}, bf16[128,1024]{1,0:T(8,128)(2,1)}, u32[]{:S(2)}) copy-start(bf16[128,1024]{1,0:T(8,128)(2,1)} %mix_weights.1.mix_ref) | copy-start | bytes 786436
  216.8 70.0 %collective-permute-start.14 = (f32[32,512]{1,0:T(8,128)}, f32[32,512]{1,0:T(8,128)}, u32[]{:S(2)}, u32[]{:S(2)}) collective-permute-start(f32[32,512]{1,0:T(8,128)} %get-tuple-element.102), channel_id=1, source_target_pairs={{0,48},{16,0},{32,16},{48,32},{1,49},{17,1},{33,17},{49,33},{2,50}... | collective-permute-start | bytes 196616 | tf_op jit(solution)/shard_map/value_last/ppermute | solution.py:259
  (15 other events, 18.1 us)

commit v4 on v3

--- a/solution.py
+++ b/solution.py
@@ -208,7 +208,9 @@
         input_output_aliases={2: 0} if before else {},
         compiler_params=pltpu.CompilerParams(vmem_limit_bytes=32 * MIB),
         cost_estimate=pl.CostEstimate(
-            flops=2 * slots * tokens * cols, bytes_accessed=2 * (slots + tokens) * cols, transcendentals=0
+            flops=10**12 if earlier is None else 2 * slots * tokens * cols,
+            bytes_accessed=2 * (slots + tokens) * cols,
+            transcendentals=0,
         ),
         name="combine",
     )(mix, returned, *before)
@@ -326,11 +328,11 @@
             a.reshape(*SIZES, capacity, ffw).transpose(1, 4, 3, 0, 2, 5, 6).reshape(slots, ffw)
             for a in (gate_act, up_act)
         )
-        routed, mix, pair, kept, gate_act, up_act, *packs = lax.optimization_barrier(
-            (routed, mix, pair, kept, gate_act, up_act, *packs)
-        )
         below, above = shift(pair, ("z",), (1,)), shift(pair, ("z",), (3,))
         arrived = [shift(pack, ("x_lo", "x_hi"), step) for pack, step in zip(packs, steps)]
+        routed, mix, kept, gate_act, up_act, *_ = lax.optimization_barrier(
+            (routed, mix, kept, gate_act, up_act, pair, *packs)
+        )
 
     with jax.named_scope("experts"):
         hidden, score = hidden_grads(routed, w_down[0], gate_act, up_act, in_parts[0][1])
@@ -346,10 +348,10 @@
 
     with jax.named_scope("return"):
         first = exchange(slot_first.reshape(devices, capacity, -1), ORDER).reshape(slots, -1)
-        held = lax.optimization_barrier((slot_second, *halfway, *terms))
-        slot_second, halfway, terms = held[0], held[1:3], held[3:]
         second = exchange(slot_second.reshape(devices, capacity, -1), ORDER).reshape(slots, -1)
         moe_input_grad = combine(mix, first, *in_parts[0], width)
+        moe_input_grad, *held = lax.optimization_barrier((moe_input_grad, *halfway, *terms))
+        halfway, terms = held[:2], held[2:]
         scores = first[:, in_parts[0][1]].astype(jnp.float32)
         weight_grad = jnp.sum(
             jnp.where(slot[:, :, None] == jnp.arange(slots, dtype=jnp.int32), scores, 0.0), axis=2
@@ -375,7 +377,7 @@
         value_input_grad = both.transpose(3, 2, 1, 0, 4).reshape(tokens, width)
 
     with jax.named_scope("finish"):
-        moe_input_grad, *last = lax.optimization_barrier((moe_input_grad, *last))
+        moe_input_grad, total, *last = lax.optimization_barrier((moe_input_grad, total, *last))
         value_weight_grad = total + last[0] + last[1] + last[2]
     return (moe_input_grad, weight_grad, value_input_grad, value_weight_grad)
 

time: 290 us -> 277 us (0.955)
  local copies, waits for them, and re-layouts: 22.9 us -> 15.4 us
  waiting for transfers between devices: 143 us -> 139 us
    ppermute x16, waiting for transfers between devices: 6.12 us -> 0.04 us  [shift(): return lax.ppermute(array, axes, pairs)]
    unnamed x59 -> x31, local copies, waits for them, and re-layouts: 12.5 us -> 6.51 us
    ppermute x16, starting transfers between devices: 25.6 us -> 21.6 us  [shift(): return lax.ppermute(array, axes, pairs)]
  transfers between devices with their start and end apart: 19 -> 19, of which waited for: 5 -> 3; matrix products, arithmetic and copies ran while one was open for 10% -> 9% of each run, Pallas kernels for 17% -> 18%
where the time goes in v4:
time: 277 us; the launch traced here: 276 us
  waiting for transfers between devices  139 us (50%)
  starting transfers between devices  55.4 us (20%)
  Pallas kernels  50.4 us (18%)
  local copies, waits for them, and re-layouts  15.4 us (6%)
  other arithmetic  11.3 us (4%)
  matrix products  3.01 us (1%)
    all_to_all x3, waiting for transfers between devices, exchange(): return lax.all_to_all(array, axes, split_axis=0, concat_axis=0, tiled=True)  139 us
    all_to_all x3, starting transfers between devices, exchange(): return lax.all_to_all(array, axes, split_axis=0, concat_axis=0, tiled=True)  33.7 us
    ppermute x16, starting transfers between devices, shift(): return lax.ppermute(array, axes, pairs)  21.6 us
    pallas_call x2, Pallas kernels, slot_grads(): pl.pallas_call(slot_kernel, grid=(width // block,), in_specs=[pl.BlockSpe...  19.5 us
    pallas_call x1, Pallas kernels, hidden_grads(): pl.pallas_call(hidden_kernel, grid=(slots // rows,), in_specs=[pl.BlockSp...  11.1 us
    pallas_call x2, Pallas kernels, combine(): pl.pallas_call(combine_kernel, grid=(cols // block,), in_specs=[pl.BlockS...  7.84 us
    pallas_call x1, Pallas kernels, build_rows(): pl.pallas_call(rows_kernel, grid=(slots // rows,), in_specs=[pl.BlockSpec...  6.53 us
    unnamed x31, local copies, waits for them, and re-layouts  6.51 us
  transfers between devices with their start and end apart: 19, of which 3 were waited for; matrix products, arithmetic and copies ran while one was open for 9% of the time, Pallas kernels for 18%

profile of v4, /device:TPU:0, one launch (start us, length us, event | category | flops | bytes accessed | tf_op | source)
XLA Modules:
  0.0 275.7 jit_solution(9570377736603530284)
XLA Ops:
  0.6 1.7 collective-permute-start
  2.9 6.5 %build_rows.1 = bf16[1024,4096]{1,0:T(8,128)(2,1)} custom-call(s32[1]{0:T(128)} %copy.122.length_ref, s32[8,128]{1,0:T(8,128)} %bitcast.97, s32[8,128]{1,0:T(8,128)} %bitcast.98, bf16[128,4096]{1,0:T(8,128)(2,1)} %grad_ref.1), custom_call_target="tpu_custom_call" | custom-call | flops 1073741824 | bytes 9437184 | tf_op jit(solution)/shard_map/dispatch/build_rows/pallas_call | solution.py:53
  9.5 11.3 %all-to-all-start = ((bf16[128,8,4096]{2,1,0:T(8,128)(2,1)}), bf16[128,8,4096]{2,1,0:T(8,128)(2,1)}, u32[]{:S(2)}, u32[]{:S(2)}) async-start(bf16[128,8,4096]{2,1,0:T(8,128)(2,1)} %bitcast.76), calls=%async_computation | async-start | bytes 16777216 | tf_op jit(solution)/shard_map/dispatch/all_to_all | solution.py:29
  25.5 2.9 %collective-permute-start.3 = (bf16[2,256,512]{2,1,0:T(8,128)(2,1)}, bf16[2,256,512]{2,1,0:T(8,128)(2,1)}, u32[]{:S(2)}, u32[]{:S(2)}) collective-permute-start(bf16[2,256,512]{2,1,0:T(8,128)(2,1)} %get-tuple-element.95), channel_id=1, source_target_pairs={{0,48},{16,0},{32,16},{48,32},{1,49},{17,1},{33,17},{49,33},{2,50}... | collective-permute-start | bytes 1572872 | tf_op jit(solution)/shard_map/value_second/ppermute | solution.py:261
  29.6 1.5 pad_maximum_fusion.7
  31.1 2.7 collective-permute-start.6
  36.0 2.4 mix_weights.1.mix_ref
  38.5 1.4 copy.105
  39.9 1.4 copy.106
  41.2 78.5 %all-to-all-done = bf16[128,8,4096]{2,1,0:T(8,128)(2,1)} async-done(((bf16[128,8,4096]{2,1,0:T(8,128)(2,1)}), bf16[128,8,4096]{2,1,0:T(8,128)(2,1)}, u32[]{:S(2)}, u32[]{:S(2)}) %all-to-all-start) | async-done | bytes 8388640 | tf_op jit(solution)/shard_map/dispatch/all_to_all | solution.py:29
  119.8 2.8 %copy-done = bf16[1,768,4096]{2,1,0:T(8,128)(2,1)S(1)} copy-done((bf16[1,768,4096]{2,1,0:T(8,128)(2,1)S(1)}, bf16[1,768,4096]{2,1,0:T(8,128)(2,1)}, u32[]{:S(2)}) %copy-start) | copy-done | bytes 6291480
  122.6 11.1 %hidden_grads.1 = (bf16[1024,1536]{1,0:T(8,128)(2,1)S(1)}, bf16[1024,1152]{1,0:T(8,128)(2,1)}) custom-call(bf16[1024,4096]{1,0:T(8,128)(2,1)} %bitcast.3.x_ref, bf16[768,4096]{1,0:T(8,128)(2,1)S(1)} %bitcast.75, bf16[1024,768]{1,0:T(8,128)(2,1)} %bitcast.79, bf16[1024,768]{1,0:T(8,128)(2,1)} %bitcast.80), custom_call_target="tpu_custom_call" | custom-call | flops 1 | bytes 1 | tf_op jit(solution)/shard_map/experts/hidden_grads/pallas_call | solution.py:97
  133.6 6.1 %slot_grads.3 = bf16[1024,1152]{1,0:T(8,128)(2,1)} custom-call(bf16[1024,1536]{1,0:T(8,128)(2,1)S(1)} %get-tuple-element.46.hidden_ref, bf16[4096,768]{1,0:T(8,128)(2,1)} %bitcast.81, bf16[4096,768]{1,0:T(8,128)(2,1)} %bitcast.83, bf16[1024,1152]{1,0:T(8,128)(2,1)} %get-tuple-element.47.refs_0_), custom_call_target="tpu_custom_call", output_to_operand_aliasing={{}: (3, {})} | custom-call | flops 1 | bytes 1 | tf_op jit(solution)/shard_map/experts/slot_grads/pallas_call | solution.py:149
  139.8 16.5 %all-to-all-start.2 = ((bf16[128,8,1152]{2,1,0:T(8,128)(2,1)}), bf16[128,8,1152]{2,1,0:T(8,128)(2,1)}, u32[]{:S(2)}, u32[]{:S(2)}) async-start(bf16[128,8,1152]{2,1,0:T(8,128)(2,1)} %bitcast.77), calls=%async_computation.2 | async-start | bytes 4718592 | tf_op jit(solution)/shard_map/return/all_to_all | solution.py:29
  157.3 2.9 %split_terms.1 = (f32[128,512]{1,0:T(8,128)S(1)}, bf16[128,512]{1,0:T(8,128)(2,1)}, bf16[128,512]{1,0:T(8,128)(2,1)}, bf16[128,512]{1,0:T(8,128)(2,1)}) custom-call(s32[1]{0:T(128)} %bitcast.30.place_ref, bf16[256,1024]{1,0:T(8,128)(2,1)S(1)} %copy-done.1, bf16[256,1024]{1,0:T(8,128)(2,1)} %collective-permute-done.4.refs_1_, ...), custom_call_target="tpu_custom_call" | custom-call | flops 1 | bytes 1 | tf_op jit(solution)/shard_map/value_third/split_terms/pallas_call | solution.py:240
  161.1 2.7 collective-permute-start.10
  163.9 1.4 collective-permute-start.11
  165.3 1.7 slice_bitcast_fusion
  166.9 3.5 %collective-permute-start.8 = (bf16[256,512]{1,0:T(8,128)(2,1)}, bf16[256,512]{1,0:T(8,128)(2,1)}, u32[]{:S(2)}, u32[]{:S(2)}) collective-permute-start(bf16[256,512]{1,0:T(8,128)(2,1)} %slice_bitcast_fusion), channel_id=1, source_target_pairs={{0,48},{16,0},{32,16},{48,32},{1,49},{17,1},{33,17},{49,33},{2,50}... | collective-permute-start | bytes 786440 | tf_op jit(solution)/shard_map/value_third/ppermute | solution.py:261
  170.4 1.7 slice_bitcast_fusion.1
  172.1 13.5 %slot_grads.2 = bf16[1024,3072]{1,0:T(8,128)(2,1)} custom-call(bf16[1024,1536]{1,0:T(8,128)(2,1)S(1)} %get-tuple-element.46.hidden_ref, bf16[4096,768]{1,0:T(8,128)(2,1)} %bitcast.82, bf16[4096,768]{1,0:T(8,128)(2,1)} %bitcast.84), custom_call_target="tpu_custom_call" | custom-call | flops 9663676416 | bytes 18874368 | tf_op jit(solution)/shard_map/experts/slot_grads/pallas_call | solution.py:149
  185.5 3.6 %all-to-all-done.2 = bf16[128,8,1152]{2,1,0:T(8,128)(2,1)} async-done(((bf16[128,8,1152]{2,1,0:T(8,128)(2,1)}), bf16[128,8,1152]{2,1,0:T(8,128)(2,1)}, u32[]{:S(2)}, u32[]{:S(2)}) %all-to-all-start.2) | async-done | bytes 2359328 | tf_op jit(solution)/shard_map/return/all_to_all | solution.py:29
  189.1 5.9 %all-to-all-start.1 = ((bf16[128,8,3072]{2,1,0:T(8,128)(2,1)}), bf16[128,8,3072]{2,1,0:T(8,128)(2,1)}, u32[]{:S(2)}, u32[]{:S(2)}) async-start(bf16[128,8,3072]{2,1,0:T(8,128)(2,1)} %bitcast.78), calls=%async_computation.1 | async-start | bytes 12582912 | tf_op jit(solution)/shard_map/return/all_to_all | solution.py:29
  195.1 2.8 %combine.2.refs_0_ = bf16[128,4096]{1,0:T(8,128)(2,1)} custom-call(bf16[128,1024]{1,0:T(8,128)(2,1)S(1)} %copy-done.2, bf16[1024,1152]{1,0:T(8,128)(2,1)} %bitcast.27.rows_ref), custom_call_target="tpu_custom_call" | custom-call | flops 999999995904 | bytes 2359296 | tf_op jit(solution)/shard_map/return/combine/pallas_call | solution.py:198
  199.0 1.5 pad_maximum_fusion
  200.7 1.1 convert_reduce_fusion
  204.3 2.9 %collective-permute-start.14 = (f32[32,512]{1,0:T(8,128)S(1)}, f32[32,512]{1,0:T(8,128)S(1)}, u32[]{:S(2)}, u32[]{:S(2)}) collective-permute-start(f32[32,512]{1,0:T(8,128)S(1)} %get-tuple-element.98), channel_id=1, source_target_pairs={{0,48},{16,0},{32,16},{48,32},{1,49},{17,1},{33,17},{49,33},{2,50}... | collective-permute-start | bytes 196616 | tf_op jit(solution)/shard_map/value_last/ppermute | solution.py:261
  207.5 1.1 collective-permute-start.12
  209.4 2.3 fusion.1
  212.3 1.3 copy.112
  213.6 56.4 %all-to-all-done.1 = bf16[128,8,3072]{2,1,0:T(8,128)(2,1)} async-done(((bf16[128,8,3072]{2,1,0:T(8,128)(2,1)}), bf16[128,8,3072]{2,1,0:T(8,128)(2,1)}, u32[]{:S(2)}, u32[]{:S(2)}) %all-to-all-start.1) | async-done | bytes 6291488 | tf_op jit(solution)/shard_map/return/all_to_all | solution.py:29
  270.0 5.0 %combine.3 = bf16[128,4096]{1,0:T(8,128)(2,1)} custom-call(bf16[128,1024]{1,0:T(8,128)(2,1)S(1)} %copy-done.2, bf16[1024,3072]{1,0:T(8,128)(2,1)} %bitcast.25.rows_ref, bf16[128,4096]{1,0:T(8,128)(2,1)} %combine.2.refs_0_), custom_call_target="tpu_custom_call", output_to_operand_aliasing={{}: (2, {})} | custom-call | flops 805306368 | bytes 7077888 | tf_op jit(solution)/shard_map/return/combine/pallas_call | solution.py:198
  (84 shorter events, 15.8 us)
Async XLA Ops:
  0.6 8.8 %collective-permute-start = (bf16[256,512]{1,0:T(8,128)(2,1)}, bf16[256,512]{1,0:T(8,128)(2,1)S(1)}, u32[]{:S(2)}, u32[]{:S(2)}) collective-permute-start(bf16[256,512]{1,0:T(8,128)(2,1)} %param.15), channel_id=1, source_target_pairs={{0,64},{64,0},{1,65},{65,1},{2,66},{66,2},{3,67},{67,3},{4,68},{68... | collective-permute-start | bytes 786440 | tf_op jit(solution)/shard_map/value_first/ppermute | solution.py:261
  9.5 11.3 %copy-start.8 = (bf16[128,4096]{1,0:T(8,128)(2,1)S(1)}, bf16[128,4096]{1,0:T(8,128)(2,1)}, u32[]{:S(2)}) copy-start(bf16[128,4096]{1,0:T(8,128)(2,1)} %param.13) | copy-start | bytes 3145732
  9.5 110.3 %all-to-all-start = ((bf16[128,8,4096]{2,1,0:T(8,128)(2,1)}), bf16[128,8,4096]{2,1,0:T(8,128)(2,1)}, u32[]{:S(2)}, u32[]{:S(2)}) async-start(bf16[128,8,4096]{2,1,0:T(8,128)(2,1)} %bitcast.76), calls=%async_computation | async-start | bytes 16777216 | tf_op jit(solution)/shard_map/dispatch/all_to_all | solution.py:29
  21.5 1.8 copy-start.11
  21.5 1.9 copy-start.13
  21.5 2.9 %copy-start.10 = (bf16[256,512]{1,0:T(8,128)(2,1)S(1)}, bf16[256,512]{1,0:T(8,128)(2,1)}, u32[]{:S(2)}) copy-start(bf16[256,512]{1,0:T(8,128)(2,1)} %param.15) | copy-start | bytes 786436
  23.3 5.2 %collective-permute-start.1 = (bf16[128,2560]{1,0:T(8,128)(2,1)}, bf16[128,2560]{1,0:T(8,128)(2,1)S(1)}, u32[]{:S(2)}, u32[]{:S(2)}) collective-permute-start(bf16[128,2560]{1,0:T(8,128)(2,1)} %pad_maximum_fusion.1), channel_id=1, source_target_pairs={{0,8},{8,0},{1,9},{9,1},{2,10},{10,2},{3,11},{11,3},{4,12},{12,4},... | collective-permute-start | bytes 1966088 | tf_op jit(solution)/shard_map/value_second/ppermute | solution.py:261
  25.5 114.2 %collective-permute-start.3 = (bf16[2,256,512]{2,1,0:T(8,128)(2,1)}, bf16[2,256,512]{2,1,0:T(8,128)(2,1)}, u32[]{:S(2)}, u32[]{:S(2)}) collective-permute-start(bf16[2,256,512]{2,1,0:T(8,128)(2,1)} %get-tuple-element.95), channel_id=1, source_target_pairs={{0,48},{16,0},{32,16},{48,32},{1,49},{17,1},{33,17},{49,33},{2,50}... | collective-permute-start | bytes 1572872 | tf_op jit(solution)/shard_map/value_second/ppermute | solution.py:261
  28.4 111.3 %collective-permute-start.2 = (bf16[2,256,512]{2,1,0:T(8,128)(2,1)}, bf16[2,256,512]{2,1,0:T(8,128)(2,1)}, u32[]{:S(2)}, u32[]{:S(2)}) collective-permute-start(bf16[2,256,512]{2,1,0:T(8,128)(2,1)} %get-tuple-element.95), channel_id=1, source_target_pairs={{0,16},{16,32},{32,48},{48,0},{1,17},{17,33},{33,49},{49,1},{2,18}... | collective-permute-start | bytes 1572872 | tf_op jit(solution)/shard_map/value_second/ppermute | solution.py:261
  29.4 5.8 %copy-start.12 = (s32[128,8]{0,1:T(8,128)S(1)}, s32[128,8]{0,1:T(8,128)}, u32[]{:S(2)}) copy-start(s32[128,8]{0,1:T(8,128)} %param.18) | copy-start | bytes 12292
  29.6 8.9 %copy-start.6 = (bf16[1,128,8,768]{3,2,1,0:T(8,128)(2,1)S(1)}, bf16[1,128,8,768]{3,2,1,0:T(8,128)(2,1)}, u32[]{:S(2)}) copy-start(bf16[1,128,8,768]{3,2,1,0:T(8,128)(2,1)} %param.21) | copy-start | bytes 4718596
  31.1 8.8 %copy-start.7 = (bf16[1,128,8,768]{3,2,1,0:T(8,128)(2,1)S(1)}, bf16[1,128,8,768]{3,2,1,0:T(8,128)(2,1)}, u32[]{:S(2)}) copy-start(bf16[1,128,8,768]{3,2,1,0:T(8,128)(2,1)} %param.22) | copy-start | bytes 4718596
  31.1 108.6 %collective-permute-start.6 = (bf16[256,1024]{1,0:T(8,128)(2,1)}, bf16[256,1024]{1,0:T(8,128)(2,1)}, u32[]{:S(2)}, u32[]{:S(2)}) collective-permute-start(bf16[256,1024]{1,0:T(8,128)(2,1)} %get-tuple-element.102), channel_id=1, source_target_pairs={{0,68},{4,64},{64,4},{68,0},{1,69},{5,65},{65,5},{69,1},{2,70},{6,... | collective-permute-start | bytes 1572872 | tf_op jit(solution)/shard_map/value_second/ppermute | solution.py:261
  33.8 105.9 %collective-permute-start.4 = (bf16[256,1024]{1,0:T(8,128)(2,1)}, bf16[256,1024]{1,0:T(8,128)(2,1)}, u32[]{:S(2)}, u32[]{:S(2)}) collective-permute-start(bf16[256,1024]{1,0:T(8,128)(2,1)} %get-tuple-element.103), channel_id=1, source_target_pairs={{0,4},{4,0},{64,68},{68,64},{1,5},{5,1},{65,69},{69,65},{2,6},{6,2... | collective-permute-start | bytes 1572872 | tf_op jit(solution)/shard_map/value_second/ppermute | solution.py:261
  34.6 105.1 %collective-permute-start.5 = (bf16[256,1024]{1,0:T(8,128)(2,1)}, bf16[256,1024]{1,0:T(8,128)(2,1)}, u32[]{:S(2)}, u32[]{:S(2)}) collective-permute-start(bf16[256,1024]{1,0:T(8,128)(2,1)} %get-tuple-element.104), channel_id=1, source_target_pairs={{0,64},{4,68},{64,0},{68,4},{1,65},{5,69},{65,1},{69,5},{2,66},{6,... | collective-permute-start | bytes 1572872 | tf_op jit(solution)/shard_map/value_second/ppermute | solution.py:261
  119.8 2.8 %copy-start = (bf16[1,768,4096]{2,1,0:T(8,128)(2,1)S(1)}, bf16[1,768,4096]{2,1,0:T(8,128)(2,1)}, u32[]{:S(2)}) copy-start(bf16[1,768,4096]{2,1,0:T(8,128)(2,1)} %param.25) | copy-start | bytes 18874372
  139.8 49.3 %all-to-all-start.2 = ((bf16[128,8,1152]{2,1,0:T(8,128)(2,1)}), bf16[128,8,1152]{2,1,0:T(8,128)(2,1)}, u32[]{:S(2)}, u32[]{:S(2)}) async-start(bf16[128,8,1152]{2,1,0:T(8,128)(2,1)} %bitcast.77), calls=%async_computation.2 | async-start | bytes 4718592 | tf_op jit(solution)/shard_map/return/all_to_all | solution.py:29
  156.2 1.0 copy-start.1
  160.2 37.7 %collective-permute-start.9 = (bf16[128,512]{1,0:T(8,128)(2,1)}, bf16[128,512]{1,0:T(8,128)(2,1)}, u32[]{:S(2)}, u32[]{:S(2)}) collective-permute-start(bf16[128,512]{1,0:T(8,128)(2,1)} %get-tuple-element.55), channel_id=1, source_target_pairs={{0,1},{1,2},{2,3},{3,0},{4,5},{5,6},{6,7},{7,4},{8,9},{9,10},{10,1... | collective-permute-start | bytes 393224 | tf_op jit(solution)/shard_map/value_third/ppermute | solution.py:261
  161.1 36.8 %collective-permute-start.10 = (bf16[128,512]{1,0:T(8,128)(2,1)}, bf16[128,512]{1,0:T(8,128)(2,1)}, u32[]{:S(2)}, u32[]{:S(2)}) collective-permute-start(bf16[128,512]{1,0:T(8,128)(2,1)} %get-tuple-element.56), channel_id=1, source_target_pairs={{0,2},{1,3},{2,0},{3,1},{4,6},{5,7},{6,4},{7,5},{8,10},{9,11},{10,... | collective-permute-start | bytes 393224 | tf_op jit(solution)/shard_map/value_third/ppermute | solution.py:261
  163.9 34.0 %collective-permute-start.11 = (bf16[128,512]{1,0:T(8,128)(2,1)}, bf16[128,512]{1,0:T(8,128)(2,1)}, u32[]{:S(2)}, u32[]{:S(2)}) collective-permute-start(bf16[128,512]{1,0:T(8,128)(2,1)} %get-tuple-element.57), channel_id=1, source_target_pairs={{0,3},{1,0},{2,1},{3,2},{4,7},{5,4},{6,5},{7,6},{8,11},{9,8},{10,9... | collective-permute-start | bytes 393224 | tf_op jit(solution)/shard_map/value_third/ppermute | solution.py:261
  166.9 31.0 %collective-permute-start.8 = (bf16[256,512]{1,0:T(8,128)(2,1)}, bf16[256,512]{1,0:T(8,128)(2,1)}, u32[]{:S(2)}, u32[]{:S(2)}) collective-permute-start(bf16[256,512]{1,0:T(8,128)(2,1)} %slice_bitcast_fusion), channel_id=1, source_target_pairs={{0,48},{16,0},{32,16},{48,32},{1,49},{17,1},{33,17},{49,33},{2,50}... | collective-permute-start | bytes 786440 | tf_op jit(solution)/shard_map/value_third/ppermute | solution.py:261
  172.1 25.8 %collective-permute-start.7 = (bf16[256,512]{1,0:T(8,128)(2,1)}, bf16[256,512]{1,0:T(8,128)(2,1)}, u32[]{:S(2)}, u32[]{:S(2)}) collective-permute-start(bf16[256,512]{1,0:T(8,128)(2,1)} %slice_bitcast_fusion.1), channel_id=1, source_target_pairs={{0,16},{16,32},{32,48},{48,0},{1,17},{17,33},{33,49},{49,1},{2,18}... | collective-permute-start | bytes 786440 | tf_op jit(solution)/shard_map/value_third/ppermute | solution.py:261
  189.1 6.0 %copy-start.2 = (bf16[128,1024]{1,0:T(8,128)(2,1)S(1)}, bf16[128,1024]{1,0:T(8,128)(2,1)}, u32[]{:S(2)}) copy-start(bf16[128,1024]{1,0:T(8,128)(2,1)} %mix_weights.1.mix_ref) | copy-start | bytes 786436
  189.1 80.9 %all-to-all-start.1 = ((bf16[128,8,3072]{2,1,0:T(8,128)(2,1)}), bf16[128,8,3072]{2,1,0:T(8,128)(2,1)}, u32[]{:S(2)}, u32[]{:S(2)}) async-start(bf16[128,8,3072]{2,1,0:T(8,128)(2,1)} %bitcast.78), calls=%async_computation.1 | async-start | bytes 12582912 | tf_op jit(solution)/shard_map/return/all_to_all | solution.py:29
  195.1 3.9 %copy-start.3 = (bf16[1,2,256,512]{3,2,1,0:T(8,128)(2,1)S(1)}, bf16[1,2,256,512]{3,2,1,0:T(8,128)(2,1)}, u32[]{:S(2)}) copy-start(bf16[1,2,256,512]{3,2,1,0:T(8,128)(2,1)} %get-tuple-element.94) | copy-start | bytes 1572868
  199.0 2.8 %copy-start.9 = (s32[128,8]{1,0:T(8,128)S(1)}, s32[128,8]{1,0:T(8,128)}, u32[]{:S(2)}) copy-start(s32[128,8]{1,0:T(8,128)} %broadcast_select_fusion.2.slot_ref) | copy-start | bytes 12292
  199.0 9.6 %copy-start.5 = (bf16[128,512]{1,0:T(8,128)(2,1)S(1)}, bf16[128,512]{1,0:T(8,128)(2,1)}, u32[]{:S(2)}) copy-start(bf16[128,512]{1,0:T(8,128)(2,1)} %param.14) | copy-start | bytes 393220
  200.5 8.8 %collective-permute-start.15 = (bf16[4,2,256,512]{3,2,1,0:T(8,128)(2,1)S(1)}, bf16[4,2,256,512]{3,2,1,0:T(8,128)(2,1)}, u32[]{:S(2)}, u32[]{:S(2)}) collective-permute-start(bf16[4,2,256,512]{3,2,1,0:T(8,128)(2,1)S(1)} %pad_maximum_fusion), channel_id=1, source_target_pairs={{0,8},{8,0},{1,9},{9,1},{2,10},{10,2},{3,11},{11,3},{4,12},{12,4},... | collective-permute-start | bytes 6291464 | tf_op jit(solution)/shard_map/value_last/ppermute | solution.py:261
  204.3 70.8 %collective-permute-start.14 = (f32[32,512]{1,0:T(8,128)S(1)}, f32[32,512]{1,0:T(8,128)S(1)}, u32[]{:S(2)}, u32[]{:S(2)}) collective-permute-start(f32[32,512]{1,0:T(8,128)S(1)} %get-tuple-element.98), channel_id=1, source_target_pairs={{0,48},{16,0},{32,16},{48,32},{1,49},{17,1},{33,17},{49,33},{2,50}... | collective-permute-start | bytes 196616 | tf_op jit(solution)/shard_map/value_last/ppermute | solution.py:261
  207.2 67.9 %collective-permute-start.13 = (f32[32,512]{1,0:T(8,128)S(1)}, f32[32,512]{1,0:T(8,128)S(1)}, u32[]{:S(2)}, u32[]{:S(2)}) collective-permute-start(f32[32,512]{1,0:T(8,128)S(1)} %get-tuple-element.99), channel_id=1, source_target_pairs={{0,32},{16,48},{32,0},{48,16},{1,33},{17,49},{33,1},{49,17},{2,34}... | collective-permute-start | bytes 196616 | tf_op jit(solution)/shard_map/value_last/ppermute | solution.py:261
  207.5 67.6 %collective-permute-start.12 = (f32[32,512]{1,0:T(8,128)S(1)}, f32[32,512]{1,0:T(8,128)S(1)}, u32[]{:S(2)}, u32[]{:S(2)}) collective-permute-start(f32[32,512]{1,0:T(8,128)S(1)} %get-tuple-element.100), channel_id=1, source_target_pairs={{0,16},{16,32},{32,48},{48,0},{1,17},{17,33},{33,49},{49,1},{2,18}... | collective-permute-start | bytes 196616 | tf_op jit(solution)/shard_map/value_last/ppermute | solution.py:261
  (1 other events, 0.9 us)

commit v5 on v4

--- a/solution.py
+++ b/solution.py
@@ -9,7 +9,7 @@
 
 PLACE = ("x_lo", "z", "core", "x_hi", "y")
 SIZES = (2, 4, 2, 2, 4)
-ORDER = ("z", "y", "x_hi", "x_lo", "core")
+ORDER = ("z", "y", "x_hi", "core", "x_lo")
 MIB = 1024 * 1024
 LANES = 128
 CAPACITY = 8
@@ -22,7 +22,7 @@
 
 def in_order(device):
     x_lo, z, core, x_hi, y = device // 64, device // 16 % 4, device // 8 % 2, device // 4 % 2, device % 4
-    return (((z * 4 + y) * 2 + x_hi) * 2 + x_lo) * 2 + core
+    return (((z * 4 + y) * 2 + x_hi) * 2 + core) * 2 + x_lo
 
 
 def exchange(array, axes):
@@ -69,57 +69,82 @@
     )(seq_lengths, *[pltpu.with_memory_space_constraint(a, pltpu.HBM) for a in (ids_t, slots_t, out_grad)])
 
 
-def hidden_kernel(x_ref, down_ref, gate_ref, up_ref, hidden_ref, score_ref):
-    rows = x_ref.shape[0]
-    ffw = down_ref.shape[0]
+def hidden_kernel(x_ref, down_ref, gate_hbm, up_hbm, hidden_ref, score_ref, back_ref, gate_ref, up_ref, sems):
+    k = pl.program_id(0)
+    last = pl.num_programs(0) - 1
+    rows, ffw = back_ref.shape
     part = 256
-    score = jnp.zeros((rows, LANES), jnp.float32)
-    for c in range(0, ffw, part):
-        cols = slice(c, c + part)
-        back = dot_nt(x_ref[...], down_ref[cols, :])
-        gate = gate_ref[:, cols].astype(jnp.float32)
-        up = up_ref[:, cols].astype(jnp.float32)
-        sig = 1.0 / (1.0 + jnp.exp(-gate))
-        up_grad = back * (gate * sig)
-        hidden_ref[:, ffw + c : ffw + c + part] = up_grad.astype(jnp.bfloat16)
-        hidden_ref[:, cols] = (back * up * sig * (1.0 + gate * (1.0 - sig))).astype(jnp.bfloat16)
-        term = up_grad * up
-        for lane in range(0, part, LANES):
-            score = score + term[:, lane : lane + LANES]
-    score = jnp.sum(score, axis=1, keepdims=True)
-    score_ref[...] = jnp.broadcast_to(score, score_ref.shape).astype(jnp.bfloat16)
+    copies = [
+        pltpu.make_async_copy(gate_hbm, gate_ref, sems.at[0]),
+        pltpu.make_async_copy(up_hbm, up_ref, sems.at[1]),
+    ]
+
+    @pl.when(k == 0)
+    def _():
+        for copy in copies:
+            copy.start()
+        for r in range(0, rows, part):
+            back_ref[r : r + part, :] = dot_nt(x_ref[r : r + part, :], down_ref[...])
+
+    @pl.when(jnp.logical_and(k > 0, k < last))
+    def _():
+        for r in range(0, rows, part):
+            back_ref[r : r + part, :] += dot_nt(x_ref[r : r + part, :], down_ref[...])
+
+    @pl.when(k == last)
+    def _():
+        for copy in copies:
+            copy.wait()
+        for r in range(0, rows, part):
+            here = slice(r, r + part)
+            score = jnp.zeros((part, LANES), jnp.float32)
+            for c in range(0, ffw, part):
+                cols = slice(c, c + part)
+                back = back_ref[here, cols] + dot_nt(x_ref[here, :], down_ref[cols, :])
+                gate = gate_ref[here, cols].astype(jnp.float32)
+                up = up_ref[here, cols].astype(jnp.float32)
+                sig = 1.0 / (1.0 + jnp.exp(-gate))
+                up_grad = back * (gate * sig)
+                hidden_ref[here, ffw + c : ffw + c + part] = up_grad.astype(jnp.bfloat16)
+                hidden_ref[here, cols] = (back * up * sig * (1.0 + gate * (1.0 - sig))).astype(jnp.bfloat16)
+                term = up_grad * up
+                for lane in range(0, part, LANES):
+                    score = score + term[:, lane : lane + LANES]
+            score = jnp.sum(score, axis=1, keepdims=True)
+            score_ref[here, :] = jnp.broadcast_to(score, (part, LANES)).astype(jnp.bfloat16)
 
 
 def hidden_grads(rows_in, down, gate, up, score_at):
     slots, width = rows_in.shape
     ffw = down.shape[0]
-    rows = 256
+    block = 1024
     return pl.pallas_call(
         hidden_kernel,
-        grid=(slots // rows,),
+        grid=(width // block,),
         in_specs=[
-            pl.BlockSpec((rows, width), lambda i: (i, 0)),
-            pl.BlockSpec(memory_space=pltpu.VMEM),
-            pl.BlockSpec((rows, ffw), lambda i: (i, 0)),
-            pl.BlockSpec((rows, ffw), lambda i: (i, 0)),
+            pl.BlockSpec((slots, block), lambda k: (0, k)),
+            pl.BlockSpec((ffw, block), lambda k: (0, k)),
+            pl.BlockSpec(memory_space=pl.ANY),
+            pl.BlockSpec(memory_space=pl.ANY),
         ],
         out_specs=[
-            pl.BlockSpec((rows, 2 * ffw), lambda i: (i, 0)),
-            pl.BlockSpec((rows, LANES), lambda i: (i, score_at // LANES)),
+            pl.BlockSpec((slots, 2 * ffw), lambda k: (0, 0)),
+            pl.BlockSpec((slots, LANES), lambda k: (0, score_at // LANES)),
         ],
         out_shape=[
             jax.ShapeDtypeStruct((slots, 2 * ffw), jnp.bfloat16),
             pltpu.HBM((slots, score_at + LANES), jnp.bfloat16),
         ],
-        compiler_params=pltpu.CompilerParams(vmem_limit_bytes=32 * MIB),
+        scratch_shapes=[
+            pltpu.VMEM((slots, ffw), jnp.float32),
+            pltpu.VMEM((slots, ffw), jnp.bfloat16),
+            pltpu.VMEM((slots, ffw), jnp.bfloat16),
+            pltpu.SemaphoreType.DMA((2,)),
+        ],
+        compiler_params=pltpu.CompilerParams(vmem_limit_bytes=44 * MIB),
         cost_estimate=pl.CostEstimate(flops=1, bytes_accessed=1, transcendentals=0),
         name="hidden_grads",
-    )(
-        rows_in,
-        pltpu.with_memory_space_constraint(down, pltpu.VMEM),
-        pltpu.with_memory_space_constraint(gate, pltpu.HBM),
-        pltpu.with_memory_space_constraint(up, pltpu.HBM),
-    )
+    )(rows_in, *[pltpu.with_memory_space_constraint(a, pltpu.HBM) for a in (down, gate, up)])
 
 
 def slot_kernel(hidden_ref, gate_w_ref, up_w_ref, *refs):
@@ -325,7 +350,7 @@
         packs = [along_x(*step) for step in steps]
         mix = mix_weights(slot, route_weights.astype(jnp.float32), slots)
         gate_act, up_act = (
-            a.reshape(*SIZES, capacity, ffw).transpose(1, 4, 3, 0, 2, 5, 6).reshape(slots, ffw)
+            a.reshape(*SIZES, capacity, ffw).transpose(1, 4, 3, 2, 0, 5, 6).reshape(slots, ffw)
             for a in (gate_act, up_act)
         )
         below, above = shift(pair, ("z",), (1,)), shift(pair, ("z",), (3,))

time: 277 us -> 275 us (level)
    unnamed x31 -> x29, local copies, waits for them, and re-layouts: 6.51 us -> 3.73 us
  transfers between devices with their start and end apart: 19 -> 19, of which waited for: 3 -> 3; matrix products, arithmetic and copies ran while one was open for 9% -> 9% of each run, Pallas kernels for 18% -> 19%
where the time goes in v5:
time: 275 us; the launch traced here: 274 us
  waiting for transfers between devices  141 us (51%)
  starting transfers between devices  52.7 us (19%)
  Pallas kernels  51.1 us (19%)
  local copies, waits for them, and re-layouts  12.7 us (5%)
  other arithmetic  11.2 us (4%)
  matrix products  2.99 us (1%)
    all_to_all x3, waiting for transfers between devices, exchange(): return lax.all_to_all(array, axes, split_axis=0, concat_axis=0, tiled=True)  141 us
    all_to_all x3, starting transfers between devices, exchange(): return lax.all_to_all(array, axes, split_axis=0, concat_axis=0, tiled=True)  31.1 us
    ppermute x16, starting transfers between devices, shift(): return lax.ppermute(array, axes, pairs)  21.6 us
    pallas_call x2, Pallas kernels, slot_grads(): pl.pallas_call(slot_kernel, grid=(width // block,), in_specs=[pl.BlockSpe...  19.5 us
    pallas_call x1, Pallas kernels, hidden_grads(): pl.pallas_call(hidden_kernel, grid=(width // block,), in_specs=[pl.BlockS...  11.9 us
    pallas_call x2, Pallas kernels, combine(): pl.pallas_call(combine_kernel, grid=(cols // block,), in_specs=[pl.BlockS...  7.84 us
    pallas_call x1, Pallas kernels, build_rows(): pl.pallas_call(rows_kernel, grid=(slots // rows,), in_specs=[pl.BlockSpec...  6.51 us
  transfers between devices with their start and end apart: 19, of which 3 were waited for; matrix products, arithmetic and copies ran while one was open for 9% of the time, Pallas kernels for 19%

profile of v5, /device:TPU:0, one launch (start us, length us, event | category | flops | bytes accessed | tf_op | source)
XLA Modules:
  0.0 273.8 jit_solution(8957910729135082470)
XLA Ops:
  0.6 1.7 collective-permute-start
  2.9 6.5 %build_rows.1 = bf16[1024,4096]{1,0:T(8,128)(2,1)} custom-call(s32[1]{0:T(128)} %copy.122.length_ref, s32[8,128]{1,0:T(8,128)} %bitcast.97, s32[8,128]{1,0:T(8,128)} %bitcast.98, bf16[128,4096]{1,0:T(8,128)(2,1)} %grad_ref.1), custom_call_target="tpu_custom_call" | custom-call | flops 1073741824 | bytes 9437184 | tf_op jit(solution)/shard_map/dispatch/build_rows/pallas_call | solution.py:53
  9.5 11.3 %all-to-all-start = ((bf16[128,8,4096]{2,1,0:T(8,128)(2,1)}), bf16[128,8,4096]{2,1,0:T(8,128)(2,1)}, u32[]{:S(2)}, u32[]{:S(2)}) async-start(bf16[128,8,4096]{2,1,0:T(8,128)(2,1)} %bitcast.75), calls=%async_computation | async-start | bytes 16777216 | tf_op jit(solution)/shard_map/dispatch/all_to_all | solution.py:29
  25.5 2.9 %collective-permute-start.3 = (bf16[2,256,512]{2,1,0:T(8,128)(2,1)}, bf16[2,256,512]{2,1,0:T(8,128)(2,1)}, u32[]{:S(2)}, u32[]{:S(2)}) collective-permute-start(bf16[2,256,512]{2,1,0:T(8,128)(2,1)} %get-tuple-element.95), channel_id=1, source_target_pairs={{0,48},{16,0},{32,16},{48,32},{1,49},{17,1},{33,17},{49,33},{2,50}... | collective-permute-start | bytes 1572872 | tf_op jit(solution)/shard_map/value_second/ppermute | solution.py:286
  29.6 1.5 pad_maximum_fusion.7
  31.0 2.7 collective-permute-start.6
  36.0 2.4 mix_weights.1.mix_ref
  38.4 1.4 copy.105
  39.8 1.4 copy.106
  41.2 80.2 %all-to-all-done = bf16[128,8,4096]{2,1,0:T(8,128)(2,1)} async-done(((bf16[128,8,4096]{2,1,0:T(8,128)(2,1)}), bf16[128,8,4096]{2,1,0:T(8,128)(2,1)}, u32[]{:S(2)}, u32[]{:S(2)}) %all-to-all-start) | async-done | bytes 8388640 | tf_op jit(solution)/shard_map/dispatch/all_to_all | solution.py:29
  121.4 11.9 %hidden_grads.1 = (bf16[1024,1536]{1,0:T(8,128)(2,1)S(1)}, bf16[1024,1152]{1,0:T(8,128)(2,1)}) custom-call(bf16[1024,4096]{1,0:T(8,128)(2,1)} %bitcast.3.x_ref, bf16[768,4096]{1,0:T(8,128)(2,1)} %bitcast.77, bf16[1024,768]{1,0:T(8,128)(2,1)} %bitcast.79, bf16[1024,768]{1,0:T(8,128)(2,1)} %bitcast.80), custom_call_target="tpu_custom_call" | custom-call | flops 1 | bytes 1 | tf_op jit(solution)/shard_map/experts/hidden_grads/pallas_call | solution.py:121
  133.3 6.1 %slot_grads.3 = bf16[1024,1152]{1,0:T(8,128)(2,1)} custom-call(bf16[1024,1536]{1,0:T(8,128)(2,1)S(1)} %get-tuple-element.46.hidden_ref, bf16[4096,768]{1,0:T(8,128)(2,1)} %bitcast.81, bf16[4096,768]{1,0:T(8,128)(2,1)} %bitcast.83, bf16[1024,1152]{1,0:T(8,128)(2,1)} %get-tuple-element.47.refs_0_), custom_call_target="tpu_custom_call", output_to_operand_aliasing={{}: (3, {})} | custom-call | flops 1 | bytes 1 | tf_op jit(solution)/shard_map/experts/slot_grads/pallas_call | solution.py:174
  139.4 13.9 %all-to-all-start.2 = ((bf16[128,8,1152]{2,1,0:T(8,128)(2,1)}), bf16[128,8,1152]{2,1,0:T(8,128)(2,1)}, u32[]{:S(2)}, u32[]{:S(2)}) async-start(bf16[128,8,1152]{2,1,0:T(8,128)(2,1)} %bitcast.76), calls=%async_computation.2 | async-start | bytes 4718592 | tf_op jit(solution)/shard_map/return/all_to_all | solution.py:29
  154.4 2.9 %split_terms.1 = (f32[128,512]{1,0:T(8,128)S(1)}, bf16[128,512]{1,0:T(8,128)(2,1)}, bf16[128,512]{1,0:T(8,128)(2,1)}, bf16[128,512]{1,0:T(8,128)(2,1)}) custom-call(s32[1]{0:T(128)} %bitcast.30.place_ref, bf16[256,1024]{1,0:T(8,128)(2,1)S(1)} %copy-done, bf16[256,1024]{1,0:T(8,128)(2,1)} %collective-permute-done.4.refs_1_, ...), custom_call_target="tpu_custom_call" | custom-call | flops 1 | bytes 1 | tf_op jit(solution)/shard_map/value_third/split_terms/pallas_call | solution.py:265
  158.2 2.7 collective-permute-start.10
  160.9 1.4 collective-permute-start.11
  162.4 1.7 slice_bitcast_fusion
  164.0 3.5 %collective-permute-start.8 = (bf16[256,512]{1,0:T(8,128)(2,1)}, bf16[256,512]{1,0:T(8,128)(2,1)}, u32[]{:S(2)}, u32[]{:S(2)}) collective-permute-start(bf16[256,512]{1,0:T(8,128)(2,1)} %slice_bitcast_fusion), channel_id=1, source_target_pairs={{0,48},{16,0},{32,16},{48,32},{1,49},{17,1},{33,17},{49,33},{2,50}... | collective-permute-start | bytes 786440 | tf_op jit(solution)/shard_map/value_third/ppermute | solution.py:286
  167.5 1.7 slice_bitcast_fusion.1
  169.1 13.4 %slot_grads.2 = bf16[1024,3072]{1,0:T(8,128)(2,1)} custom-call(bf16[1024,1536]{1,0:T(8,128)(2,1)S(1)} %get-tuple-element.46.hidden_ref, bf16[4096,768]{1,0:T(8,128)(2,1)} %bitcast.82, bf16[4096,768]{1,0:T(8,128)(2,1)} %bitcast.84), custom_call_target="tpu_custom_call" | custom-call | flops 9663676416 | bytes 18874368 | tf_op jit(solution)/shard_map/experts/slot_grads/pallas_call | solution.py:174
  182.6 3.6 %all-to-all-done.2 = bf16[128,8,1152]{2,1,0:T(8,128)(2,1)} async-done(((bf16[128,8,1152]{2,1,0:T(8,128)(2,1)}), bf16[128,8,1152]{2,1,0:T(8,128)(2,1)}, u32[]{:S(2)}, u32[]{:S(2)}) %all-to-all-start.2) | async-done | bytes 2359328 | tf_op jit(solution)/shard_map/return/all_to_all | solution.py:29
  186.2 5.9 %all-to-all-start.1 = ((bf16[128,8,3072]{2,1,0:T(8,128)(2,1)}), bf16[128,8,3072]{2,1,0:T(8,128)(2,1)}, u32[]{:S(2)}, u32[]{:S(2)}) async-start(bf16[128,8,3072]{2,1,0:T(8,128)(2,1)} %bitcast.78), calls=%async_computation.1 | async-start | bytes 12582912 | tf_op jit(solution)/shard_map/return/all_to_all | solution.py:29
  192.2 2.8 %combine.2.refs_0_ = bf16[128,4096]{1,0:T(8,128)(2,1)} custom-call(bf16[128,1024]{1,0:T(8,128)(2,1)S(1)} %copy-done.1, bf16[1024,1152]{1,0:T(8,128)(2,1)} %bitcast.27.rows_ref), custom_call_target="tpu_custom_call" | custom-call | flops 999999995904 | bytes 2359296 | tf_op jit(solution)/shard_map/return/combine/pallas_call | solution.py:223
  196.1 1.5 pad_maximum_fusion
  197.8 1.1 convert_reduce_fusion
  200.2 1.1 convert_add_fusion
  201.4 2.9 %collective-permute-start.14 = (f32[32,512]{1,0:T(8,128)S(1)}, f32[32,512]{1,0:T(8,128)S(1)}, u32[]{:S(2)}, u32[]{:S(2)}) collective-permute-start(f32[32,512]{1,0:T(8,128)S(1)} %get-tuple-element.98), channel_id=1, source_target_pairs={{0,48},{16,0},{32,16},{48,32},{1,49},{17,1},{33,17},{49,33},{2,50}... | collective-permute-start | bytes 196616 | tf_op jit(solution)/shard_map/value_last/ppermute | solution.py:286
  204.6 1.1 collective-permute-start.12
  206.4 2.3 fusion.1
  209.4 1.3 copy.112
  210.7 57.4 %all-to-all-done.1 = bf16[128,8,3072]{2,1,0:T(8,128)(2,1)} async-done(((bf16[128,8,3072]{2,1,0:T(8,128)(2,1)}), bf16[128,8,3072]{2,1,0:T(8,128)(2,1)}, u32[]{:S(2)}, u32[]{:S(2)}) %all-to-all-start.1) | async-done | bytes 6291488 | tf_op jit(solution)/shard_map/return/all_to_all | solution.py:29
  268.1 5.0 %combine.3 = bf16[128,4096]{1,0:T(8,128)(2,1)} custom-call(bf16[128,1024]{1,0:T(8,128)(2,1)S(1)} %copy-done.1, bf16[1024,3072]{1,0:T(8,128)(2,1)} %bitcast.25.rows_ref, bf16[128,4096]{1,0:T(8,128)(2,1)} %combine.2.refs_0_), custom_call_target="tpu_custom_call", output_to_operand_aliasing={{}: (2, {})} | custom-call | flops 805306368 | bytes 7077888 | tf_op jit(solution)/shard_map/return/combine/pallas_call | solution.py:223
  (82 shorter events, 14.7 us)
Async XLA Ops:
  0.6 8.8 %collective-permute-start = (bf16[256,512]{1,0:T(8,128)(2,1)}, bf16[256,512]{1,0:T(8,128)(2,1)S(1)}, u32[]{:S(2)}, u32[]{:S(2)}) collective-permute-start(bf16[256,512]{1,0:T(8,128)(2,1)} %param.15), channel_id=1, source_target_pairs={{0,64},{64,0},{1,65},{65,1},{2,66},{66,2},{3,67},{67,3},{4,68},{68... | collective-permute-start | bytes 786440 | tf_op jit(solution)/shard_map/value_first/ppermute | solution.py:286
  9.5 11.3 %copy-start.7 = (bf16[128,4096]{1,0:T(8,128)(2,1)S(1)}, bf16[128,4096]{1,0:T(8,128)(2,1)}, u32[]{:S(2)}) copy-start(bf16[128,4096]{1,0:T(8,128)(2,1)} %param.13) | copy-start | bytes 3145732
  9.5 112.0 %all-to-all-start = ((bf16[128,8,4096]{2,1,0:T(8,128)(2,1)}), bf16[128,8,4096]{2,1,0:T(8,128)(2,1)}, u32[]{:S(2)}, u32[]{:S(2)}) async-start(bf16[128,8,4096]{2,1,0:T(8,128)(2,1)} %bitcast.75), calls=%async_computation | async-start | bytes 16777216 | tf_op jit(solution)/shard_map/dispatch/all_to_all | solution.py:29
  21.4 0.9 copy-start.3
  21.5 1.8 copy-start.10
  21.5 1.9 copy-start.12
  21.5 2.9 %copy-start.9 = (bf16[256,512]{1,0:T(8,128)(2,1)S(1)}, bf16[256,512]{1,0:T(8,128)(2,1)}, u32[]{:S(2)}) copy-start(bf16[256,512]{1,0:T(8,128)(2,1)} %param.15) | copy-start | bytes 786436
  23.2 5.2 %collective-permute-start.1 = (bf16[128,2560]{1,0:T(8,128)(2,1)}, bf16[128,2560]{1,0:T(8,128)(2,1)S(1)}, u32[]{:S(2)}, u32[]{:S(2)}) collective-permute-start(bf16[128,2560]{1,0:T(8,128)(2,1)} %pad_maximum_fusion.1), channel_id=1, source_target_pairs={{0,8},{8,0},{1,9},{9,1},{2,10},{10,2},{3,11},{11,3},{4,12},{12,4},... | collective-permute-start | bytes 1966088 | tf_op jit(solution)/shard_map/value_second/ppermute | solution.py:286
  25.5 113.9 %collective-permute-start.3 = (bf16[2,256,512]{2,1,0:T(8,128)(2,1)}, bf16[2,256,512]{2,1,0:T(8,128)(2,1)}, u32[]{:S(2)}, u32[]{:S(2)}) collective-permute-start(bf16[2,256,512]{2,1,0:T(8,128)(2,1)} %get-tuple-element.95), channel_id=1, source_target_pairs={{0,48},{16,0},{32,16},{48,32},{1,49},{17,1},{33,17},{49,33},{2,50}... | collective-permute-start | bytes 1572872 | tf_op jit(solution)/shard_map/value_second/ppermute | solution.py:286
  28.4 111.0 %collective-permute-start.2 = (bf16[2,256,512]{2,1,0:T(8,128)(2,1)}, bf16[2,256,512]{2,1,0:T(8,128)(2,1)}, u32[]{:S(2)}, u32[]{:S(2)}) collective-permute-start(bf16[2,256,512]{2,1,0:T(8,128)(2,1)} %get-tuple-element.95), channel_id=1, source_target_pairs={{0,16},{16,32},{32,48},{48,0},{1,17},{17,33},{33,49},{49,1},{2,18}... | collective-permute-start | bytes 1572872 | tf_op jit(solution)/shard_map/value_second/ppermute | solution.py:286
  29.4 5.8 %copy-start.11 = (s32[128,8]{0,1:T(8,128)S(1)}, s32[128,8]{0,1:T(8,128)}, u32[]{:S(2)}) copy-start(s32[128,8]{0,1:T(8,128)} %param.18) | copy-start | bytes 12292
  29.5 8.9 %copy-start.5 = (bf16[1,128,8,768]{3,2,1,0:T(8,128)(2,1)S(1)}, bf16[1,128,8,768]{3,2,1,0:T(8,128)(2,1)}, u32[]{:S(2)}) copy-start(bf16[1,128,8,768]{3,2,1,0:T(8,128)(2,1)} %param.21) | copy-start | bytes 4718596
  31.0 8.8 %copy-start.6 = (bf16[1,128,8,768]{3,2,1,0:T(8,128)(2,1)S(1)}, bf16[1,128,8,768]{3,2,1,0:T(8,128)(2,1)}, u32[]{:S(2)}) copy-start(bf16[1,128,8,768]{3,2,1,0:T(8,128)(2,1)} %param.22) | copy-start | bytes 4718596
  31.0 108.4 %collective-permute-start.6 = (bf16[256,1024]{1,0:T(8,128)(2,1)}, bf16[256,1024]{1,0:T(8,128)(2,1)}, u32[]{:S(2)}, u32[]{:S(2)}) collective-permute-start(bf16[256,1024]{1,0:T(8,128)(2,1)} %get-tuple-element.102), channel_id=1, source_target_pairs={{0,68},{4,64},{64,4},{68,0},{1,69},{5,65},{65,5},{69,1},{2,70},{6,... | collective-permute-start | bytes 1572872 | tf_op jit(solution)/shard_map/value_second/ppermute | solution.py:286
  33.8 105.7 %collective-permute-start.4 = (bf16[256,1024]{1,0:T(8,128)(2,1)}, bf16[256,1024]{1,0:T(8,128)(2,1)}, u32[]{:S(2)}, u32[]{:S(2)}) collective-permute-start(bf16[256,1024]{1,0:T(8,128)(2,1)} %get-tuple-element.103), channel_id=1, source_target_pairs={{0,4},{4,0},{64,68},{68,64},{1,5},{5,1},{65,69},{69,65},{2,6},{6,2... | collective-permute-start | bytes 1572872 | tf_op jit(solution)/shard_map/value_second/ppermute | solution.py:286
  34.6 104.8 %collective-permute-start.5 = (bf16[256,1024]{1,0:T(8,128)(2,1)}, bf16[256,1024]{1,0:T(8,128)(2,1)}, u32[]{:S(2)}, u32[]{:S(2)}) collective-permute-start(bf16[256,1024]{1,0:T(8,128)(2,1)} %get-tuple-element.104), channel_id=1, source_target_pairs={{0,64},{4,68},{64,0},{68,4},{1,65},{5,69},{65,1},{69,5},{2,66},{6,... | collective-permute-start | bytes 1572872 | tf_op jit(solution)/shard_map/value_second/ppermute | solution.py:286
  139.4 46.7 %all-to-all-start.2 = ((bf16[128,8,1152]{2,1,0:T(8,128)(2,1)}), bf16[128,8,1152]{2,1,0:T(8,128)(2,1)}, u32[]{:S(2)}, u32[]{:S(2)}) async-start(bf16[128,8,1152]{2,1,0:T(8,128)(2,1)} %bitcast.76), calls=%async_computation.2 | async-start | bytes 4718592 | tf_op jit(solution)/shard_map/return/all_to_all | solution.py:29
  153.3 1.0 copy-start
  157.3 37.7 %collective-permute-start.9 = (bf16[128,512]{1,0:T(8,128)(2,1)}, bf16[128,512]{1,0:T(8,128)(2,1)}, u32[]{:S(2)}, u32[]{:S(2)}) collective-permute-start(bf16[128,512]{1,0:T(8,128)(2,1)} %get-tuple-element.55), channel_id=1, source_target_pairs={{0,1},{1,2},{2,3},{3,0},{4,5},{5,6},{6,7},{7,4},{8,9},{9,10},{10,1... | collective-permute-start | bytes 393224 | tf_op jit(solution)/shard_map/value_third/ppermute | solution.py:286
  158.2 36.8 %collective-permute-start.10 = (bf16[128,512]{1,0:T(8,128)(2,1)}, bf16[128,512]{1,0:T(8,128)(2,1)}, u32[]{:S(2)}, u32[]{:S(2)}) collective-permute-start(bf16[128,512]{1,0:T(8,128)(2,1)} %get-tuple-element.56), channel_id=1, source_target_pairs={{0,2},{1,3},{2,0},{3,1},{4,6},{5,7},{6,4},{7,5},{8,10},{9,11},{10,... | collective-permute-start | bytes 393224 | tf_op jit(solution)/shard_map/value_third/ppermute | solution.py:286
  160.9 34.0 %collective-permute-start.11 = (bf16[128,512]{1,0:T(8,128)(2,1)}, bf16[128,512]{1,0:T(8,128)(2,1)}, u32[]{:S(2)}, u32[]{:S(2)}) collective-permute-start(bf16[128,512]{1,0:T(8,128)(2,1)} %get-tuple-element.57), channel_id=1, source_target_pairs={{0,3},{1,0},{2,1},{3,2},{4,7},{5,4},{6,5},{7,6},{8,11},{9,8},{10,9... | collective-permute-start | bytes 393224 | tf_op jit(solution)/shard_map/value_third/ppermute | solution.py:286
  164.0 31.0 %collective-permute-start.8 = (bf16[256,512]{1,0:T(8,128)(2,1)}, bf16[256,512]{1,0:T(8,128)(2,1)}, u32[]{:S(2)}, u32[]{:S(2)}) collective-permute-start(bf16[256,512]{1,0:T(8,128)(2,1)} %slice_bitcast_fusion), channel_id=1, source_target_pairs={{0,48},{16,0},{32,16},{48,32},{1,49},{17,1},{33,17},{49,33},{2,50}... | collective-permute-start | bytes 786440 | tf_op jit(solution)/shard_map/value_third/ppermute | solution.py:286
  169.1 25.9 %collective-permute-start.7 = (bf16[256,512]{1,0:T(8,128)(2,1)}, bf16[256,512]{1,0:T(8,128)(2,1)}, u32[]{:S(2)}, u32[]{:S(2)}) collective-permute-start(bf16[256,512]{1,0:T(8,128)(2,1)} %slice_bitcast_fusion.1), channel_id=1, source_target_pairs={{0,16},{16,32},{32,48},{48,0},{1,17},{17,33},{33,49},{49,1},{2,18}... | collective-permute-start | bytes 786440 | tf_op jit(solution)/shard_map/value_third/ppermute | solution.py:286
  186.2 6.0 %copy-start.1 = (bf16[128,1024]{1,0:T(8,128)(2,1)S(1)}, bf16[128,1024]{1,0:T(8,128)(2,1)}, u32[]{:S(2)}) copy-start(bf16[128,1024]{1,0:T(8,128)(2,1)} %mix_weights.1.mix_ref) | copy-start | bytes 786436
  186.2 81.9 %all-to-all-start.1 = ((bf16[128,8,3072]{2,1,0:T(8,128)(2,1)}), bf16[128,8,3072]{2,1,0:T(8,128)(2,1)}, u32[]{:S(2)}, u32[]{:S(2)}) async-start(bf16[128,8,3072]{2,1,0:T(8,128)(2,1)} %bitcast.78), calls=%async_computation.1 | async-start | bytes 12582912 | tf_op jit(solution)/shard_map/return/all_to_all | solution.py:29
  192.2 3.9 %copy-start.2 = (bf16[1,2,256,512]{3,2,1,0:T(8,128)(2,1)S(1)}, bf16[1,2,256,512]{3,2,1,0:T(8,128)(2,1)}, u32[]{:S(2)}) copy-start(bf16[1,2,256,512]{3,2,1,0:T(8,128)(2,1)} %get-tuple-element.94) | copy-start | bytes 1572868
  196.1 2.8 %copy-start.8 = (s32[128,8]{1,0:T(8,128)S(1)}, s32[128,8]{1,0:T(8,128)}, u32[]{:S(2)}) copy-start(s32[128,8]{1,0:T(8,128)} %broadcast_select_fusion.2.slot_ref) | copy-start | bytes 12292
  196.1 9.6 %copy-start.4 = (bf16[128,512]{1,0:T(8,128)(2,1)S(1)}, bf16[128,512]{1,0:T(8,128)(2,1)}, u32[]{:S(2)}) copy-start(bf16[128,512]{1,0:T(8,128)(2,1)} %param.14) | copy-start | bytes 393220
  197.6 8.8 %collective-permute-start.15 = (bf16[4,2,256,512]{3,2,1,0:T(8,128)(2,1)S(1)}, bf16[4,2,256,512]{3,2,1,0:T(8,128)(2,1)}, u32[]{:S(2)}, u32[]{:S(2)}) collective-permute-start(bf16[4,2,256,512]{3,2,1,0:T(8,128)(2,1)S(1)} %pad_maximum_fusion), channel_id=1, source_target_pairs={{0,8},{8,0},{1,9},{9,1},{2,10},{10,2},{3,11},{11,3},{4,12},{12,4},... | collective-permute-start | bytes 6291464 | tf_op jit(solution)/shard_map/value_last/ppermute | solution.py:286
  201.4 71.8 %collective-permute-start.14 = (f32[32,512]{1,0:T(8,128)S(1)}, f32[32,512]{1,0:T(8,128)S(1)}, u32[]{:S(2)}, u32[]{:S(2)}) collective-permute-start(f32[32,512]{1,0:T(8,128)S(1)} %get-tuple-element.98), channel_id=1, source_target_pairs={{0,48},{16,0},{32,16},{48,32},{1,49},{17,1},{33,17},{49,33},{2,50}... | collective-permute-start | bytes 196616 | tf_op jit(solution)/shard_map/value_last/ppermute | solution.py:286
  204.3 68.8 %collective-permute-start.13 = (f32[32,512]{1,0:T(8,128)S(1)}, f32[32,512]{1,0:T(8,128)S(1)}, u32[]{:S(2)}, u32[]{:S(2)}) collective-permute-start(f32[32,512]{1,0:T(8,128)S(1)} %get-tuple-element.99), channel_id=1, source_target_pairs={{0,32},{16,48},{32,0},{48,16},{1,33},{17,49},{33,1},{49,17},{2,34}... | collective-permute-start | bytes 196616 | tf_op jit(solution)/shard_map/value_last/ppermute | solution.py:286
  204.6 68.5 %collective-permute-start.12 = (f32[32,512]{1,0:T(8,128)S(1)}, f32[32,512]{1,0:T(8,128)S(1)}, u32[]{:S(2)}, u32[]{:S(2)}) collective-permute-start(f32[32,512]{1,0:T(8,128)S(1)} %get-tuple-element.100), channel_id=1, source_target_pairs={{0,16},{16,32},{32,48},{48,0},{1,17},{17,33},{33,49},{49,1},{2,18}... | collective-permute-start | bytes 196616 | tf_op jit(solution)/shard_map/value_last/ppermute | solution.py:286

commit v6 on v5

--- a/solution.py
+++ b/solution.py
@@ -9,7 +9,7 @@
 
 PLACE = ("x_lo", "z", "core", "x_hi", "y")
 SIZES = (2, 4, 2, 2, 4)
-ORDER = ("z", "y", "x_hi", "core", "x_lo")
+ORDER = ("z", "y", "x_lo", "x_hi", "core")
 MIB = 1024 * 1024
 LANES = 128
 CAPACITY = 8
@@ -22,7 +22,7 @@
 
 def in_order(device):
     x_lo, z, core, x_hi, y = device // 64, device // 16 % 4, device // 8 % 2, device // 4 % 2, device % 4
-    return (((z * 4 + y) * 2 + x_hi) * 2 + core) * 2 + x_lo
+    return (((z * 4 + y) * 2 + x_lo) * 2 + x_hi) * 2 + core
 
 
 def exchange(array, axes):
@@ -350,7 +350,7 @@
         packs = [along_x(*step) for step in steps]
         mix = mix_weights(slot, route_weights.astype(jnp.float32), slots)
         gate_act, up_act = (
-            a.reshape(*SIZES, capacity, ffw).transpose(1, 4, 3, 2, 0, 5, 6).reshape(slots, ffw)
+            a.reshape(*SIZES, capacity, ffw).transpose(1, 4, 0, 3, 2, 5, 6).reshape(slots, ffw)
             for a in (gate_act, up_act)
         )
         below, above = shift(pair, ("z",), (1,)), shift(pair, ("z",), (3,))

time: 275 us -> 272 us (0.989)
  waiting for transfers between devices: 141 us -> 137 us
    all_to_all x3, waiting for transfers between devices: 141 us -> 137 us  [exchange(): return lax.all_to_all(array, axes, split_axis=0, concat_axis=0, tiled=True)]
where the time goes in v6:
time: 272 us; the launch traced here: 271 us
  waiting for transfers between devices  137 us (50%)
  starting transfers between devices  53.5 us (20%)
  Pallas kernels  51.1 us (19%)
  local copies, waits for them, and re-layouts  12.6 us (5%)
  other arithmetic  11.2 us (4%)
  matrix products  2.99 us (1%)
    all_to_all x3, waiting for transfers between devices, exchange(): return lax.all_to_all(array, axes, split_axis=0, concat_axis=0, tiled=True)  137 us
    all_to_all x3, starting transfers between devices, exchange(): return lax.all_to_all(array, axes, split_axis=0, concat_axis=0, tiled=True)  31.9 us
    ppermute x16, starting transfers between devices, shift(): return lax.ppermute(array, axes, pairs)  21.6 us
    pallas_call x2, Pallas kernels, slot_grads(): pl.pallas_call(slot_kernel, grid=(width // block,), in_specs=[pl.BlockSpe...  19.5 us
    pallas_call x1, Pallas kernels, hidden_grads(): pl.pallas_call(hidden_kernel, grid=(width // block,), in_specs=[pl.BlockS...  11.9 us
    pallas_call x2, Pallas kernels, combine(): pl.pallas_call(combine_kernel, grid=(cols // block,), in_specs=[pl.BlockS...  7.84 us
    pallas_call x1, Pallas kernels, build_rows(): pl.pallas_call(rows_kernel, grid=(slots // rows,), in_specs=[pl.BlockSpec...  6.51 us
  transfers between devices with their start and end apart: 19, of which 3 were waited for; matrix products, arithmetic and copies ran while one was open for 9% of the time, Pallas kernels for 19%

profile of v6, /device:TPU:0, one launch (start us, length us, event | category | flops | bytes accessed | tf_op | source)
XLA Modules:
  0.0 270.7 jit_solution(6115275920120994423)
XLA Ops:
  0.6 1.7 collective-permute-start
  2.9 6.5 %build_rows.1 = bf16[1024,4096]{1,0:T(8,128)(2,1)} custom-call(s32[1]{0:T(128)} %copy.122.length_ref, s32[8,128]{1,0:T(8,128)} %bitcast.97, s32[8,128]{1,0:T(8,128)} %bitcast.98, bf16[128,4096]{1,0:T(8,128)(2,1)} %grad_ref.1), custom_call_target="tpu_custom_call" | custom-call | flops 1073741824 | bytes 9437184 | tf_op jit(solution)/shard_map/dispatch/build_rows/pallas_call | solution.py:53
  9.5 11.3 %all-to-all-start = ((bf16[128,8,4096]{2,1,0:T(8,128)(2,1)}), bf16[128,8,4096]{2,1,0:T(8,128)(2,1)}, u32[]{:S(2)}, u32[]{:S(2)}) async-start(bf16[128,8,4096]{2,1,0:T(8,128)(2,1)} %bitcast.75), calls=%async_computation | async-start | bytes 16777216 | tf_op jit(solution)/shard_map/dispatch/all_to_all | solution.py:29
  25.5 2.9 %collective-permute-start.3 = (bf16[2,256,512]{2,1,0:T(8,128)(2,1)}, bf16[2,256,512]{2,1,0:T(8,128)(2,1)}, u32[]{:S(2)}, u32[]{:S(2)}) collective-permute-start(bf16[2,256,512]{2,1,0:T(8,128)(2,1)} %get-tuple-element.95), channel_id=1, source_target_pairs={{0,48},{16,0},{32,16},{48,32},{1,49},{17,1},{33,17},{49,33},{2,50}... | collective-permute-start | bytes 1572872 | tf_op jit(solution)/shard_map/value_second/ppermute | solution.py:286
  29.6 1.5 pad_maximum_fusion.7
  31.0 2.7 %collective-permute-start.6 = (bf16[256,1024]{1,0:T(8,128)(2,1)}, bf16[256,1024]{1,0:T(8,128)(2,1)}, u32[]{:S(2)}, u32[]{:S(2)}) collective-permute-start(bf16[256,1024]{1,0:T(8,128)(2,1)} %get-tuple-element.102), channel_id=1, source_target_pairs={{0,68},{4,64},{64,4},{68,0},{1,69},{5,65},{65,5},{69,1},{2,70},{6,... | collective-permute-start | bytes 1572872 | tf_op jit(solution)/shard_map/value_second/ppermute | solution.py:286
  36.0 2.4 mix_weights.1.mix_ref
  38.4 1.4 copy.105
  39.8 1.4 copy.106
  41.2 77.6 %all-to-all-done = bf16[128,8,4096]{2,1,0:T(8,128)(2,1)} async-done(((bf16[128,8,4096]{2,1,0:T(8,128)(2,1)}), bf16[128,8,4096]{2,1,0:T(8,128)(2,1)}, u32[]{:S(2)}, u32[]{:S(2)}) %all-to-all-start) | async-done | bytes 8388640 | tf_op jit(solution)/shard_map/dispatch/all_to_all | solution.py:29
  118.8 11.9 %hidden_grads.1 = (bf16[1024,1536]{1,0:T(8,128)(2,1)S(1)}, bf16[1024,1152]{1,0:T(8,128)(2,1)}) custom-call(bf16[1024,4096]{1,0:T(8,128)(2,1)} %bitcast.3.x_ref, bf16[768,4096]{1,0:T(8,128)(2,1)} %bitcast.77, bf16[1024,768]{1,0:T(8,128)(2,1)} %bitcast.79, bf16[1024,768]{1,0:T(8,128)(2,1)} %bitcast.80), custom_call_target="tpu_custom_call" | custom-call | flops 1 | bytes 1 | tf_op jit(solution)/shard_map/experts/hidden_grads/pallas_call | solution.py:121
  130.7 6.1 %slot_grads.3 = bf16[1024,1152]{1,0:T(8,128)(2,1)} custom-call(bf16[1024,1536]{1,0:T(8,128)(2,1)S(1)} %get-tuple-element.46.hidden_ref, bf16[4096,768]{1,0:T(8,128)(2,1)} %bitcast.81, bf16[4096,768]{1,0:T(8,128)(2,1)} %bitcast.83, bf16[1024,1152]{1,0:T(8,128)(2,1)} %get-tuple-element.47.refs_0_), custom_call_target="tpu_custom_call", output_to_operand_aliasing={{}: (3, {})} | custom-call | flops 1 | bytes 1 | tf_op jit(solution)/shard_map/experts/slot_grads/pallas_call | solution.py:174
  136.8 14.7 %all-to-all-start.2 = ((bf16[128,8,1152]{2,1,0:T(8,128)(2,1)}), bf16[128,8,1152]{2,1,0:T(8,128)(2,1)}, u32[]{:S(2)}, u32[]{:S(2)}) async-start(bf16[128,8,1152]{2,1,0:T(8,128)(2,1)} %bitcast.76), calls=%async_computation.2 | async-start | bytes 4718592 | tf_op jit(solution)/shard_map/return/all_to_all | solution.py:29
  152.5 2.9 %split_terms.1 = (f32[128,512]{1,0:T(8,128)S(1)}, bf16[128,512]{1,0:T(8,128)(2,1)}, bf16[128,512]{1,0:T(8,128)(2,1)}, bf16[128,512]{1,0:T(8,128)(2,1)}) custom-call(s32[1]{0:T(128)} %bitcast.30.place_ref, bf16[256,1024]{1,0:T(8,128)(2,1)S(1)} %copy-done, bf16[256,1024]{1,0:T(8,128)(2,1)} %collective-permute-done.4.refs_1_, ...), custom_call_target="tpu_custom_call" | custom-call | flops 1 | bytes 1 | tf_op jit(solution)/shard_map/value_third/split_terms/pallas_call | solution.py:265
  156.3 2.7 %collective-permute-start.10 = (bf16[128,512]{1,0:T(8,128)(2,1)}, bf16[128,512]{1,0:T(8,128)(2,1)}, u32[]{:S(2)}, u32[]{:S(2)}) collective-permute-start(bf16[128,512]{1,0:T(8,128)(2,1)} %get-tuple-element.56), channel_id=1, source_target_pairs={{0,2},{1,3},{2,0},{3,1},{4,6},{5,7},{6,4},{7,5},{8,10},{9,11},{10,... | collective-permute-start | bytes 393224 | tf_op jit(solution)/shard_map/value_third/ppermute | solution.py:286
  159.1 1.4 collective-permute-start.11
  160.5 1.7 slice_bitcast_fusion
  162.1 3.5 %collective-permute-start.8 = (bf16[256,512]{1,0:T(8,128)(2,1)}, bf16[256,512]{1,0:T(8,128)(2,1)}, u32[]{:S(2)}, u32[]{:S(2)}) collective-permute-start(bf16[256,512]{1,0:T(8,128)(2,1)} %slice_bitcast_fusion), channel_id=1, source_target_pairs={{0,48},{16,0},{32,16},{48,32},{1,49},{17,1},{33,17},{49,33},{2,50}... | collective-permute-start | bytes 786440 | tf_op jit(solution)/shard_map/value_third/ppermute | solution.py:286
  165.6 1.7 slice_bitcast_fusion.1
  167.3 13.4 %slot_grads.2 = bf16[1024,3072]{1,0:T(8,128)(2,1)} custom-call(bf16[1024,1536]{1,0:T(8,128)(2,1)S(1)} %get-tuple-element.46.hidden_ref, bf16[4096,768]{1,0:T(8,128)(2,1)} %bitcast.82, bf16[4096,768]{1,0:T(8,128)(2,1)} %bitcast.84), custom_call_target="tpu_custom_call" | custom-call | flops 9663676416 | bytes 18874368 | tf_op jit(solution)/shard_map/experts/slot_grads/pallas_call | solution.py:174
  180.7 3.4 %all-to-all-done.2 = bf16[128,8,1152]{2,1,0:T(8,128)(2,1)} async-done(((bf16[128,8,1152]{2,1,0:T(8,128)(2,1)}), bf16[128,8,1152]{2,1,0:T(8,128)(2,1)}, u32[]{:S(2)}, u32[]{:S(2)}) %all-to-all-start.2) | async-done | bytes 2359328 | tf_op jit(solution)/shard_map/return/all_to_all | solution.py:29
  184.1 5.9 %all-to-all-start.1 = ((bf16[128,8,3072]{2,1,0:T(8,128)(2,1)}), bf16[128,8,3072]{2,1,0:T(8,128)(2,1)}, u32[]{:S(2)}, u32[]{:S(2)}) async-start(bf16[128,8,3072]{2,1,0:T(8,128)(2,1)} %bitcast.78), calls=%async_computation.1 | async-start | bytes 12582912 | tf_op jit(solution)/shard_map/return/all_to_all | solution.py:29
  190.1 2.8 %combine.2.refs_0_ = bf16[128,4096]{1,0:T(8,128)(2,1)} custom-call(bf16[128,1024]{1,0:T(8,128)(2,1)S(1)} %copy-done.1, bf16[1024,1152]{1,0:T(8,128)(2,1)} %bitcast.27.rows_ref), custom_call_target="tpu_custom_call" | custom-call | flops 999999995904 | bytes 2359296 | tf_op jit(solution)/shard_map/return/combine/pallas_call | solution.py:223
  194.0 1.5 pad_maximum_fusion
  195.7 1.1 convert_reduce_fusion
  198.1 1.1 convert_add_fusion
  199.3 2.9 %collective-permute-start.14 = (f32[32,512]{1,0:T(8,128)S(1)}, f32[32,512]{1,0:T(8,128)S(1)}, u32[]{:S(2)}, u32[]{:S(2)}) collective-permute-start(f32[32,512]{1,0:T(8,128)S(1)} %get-tuple-element.98), channel_id=1, source_target_pairs={{0,48},{16,0},{32,16},{48,32},{1,49},{17,1},{33,17},{49,33},{2,50}... | collective-permute-start | bytes 196616 | tf_op jit(solution)/shard_map/value_last/ppermute | solution.py:286
  202.5 1.1 collective-permute-start.12
  204.3 2.3 fusion.1
  207.3 1.3 copy.112
  208.6 56.4 %all-to-all-done.1 = bf16[128,8,3072]{2,1,0:T(8,128)(2,1)} async-done(((bf16[128,8,3072]{2,1,0:T(8,128)(2,1)}), bf16[128,8,3072]{2,1,0:T(8,128)(2,1)}, u32[]{:S(2)}, u32[]{:S(2)}) %all-to-all-start.1) | async-done | bytes 6291488 | tf_op jit(solution)/shard_map/return/all_to_all | solution.py:29
  265.0 5.0 %combine.3 = bf16[128,4096]{1,0:T(8,128)(2,1)} custom-call(bf16[128,1024]{1,0:T(8,128)(2,1)S(1)} %copy-done.1, bf16[1024,3072]{1,0:T(8,128)(2,1)} %bitcast.25.rows_ref, bf16[128,4096]{1,0:T(8,128)(2,1)} %combine.2.refs_0_), custom_call_target="tpu_custom_call", output_to_operand_aliasing={{}: (2, {})} | custom-call | flops 805306368 | bytes 7077888 | tf_op jit(solution)/shard_map/return/combine/pallas_call | solution.py:223
  (82 shorter events, 14.7 us)
Async XLA Ops:
  0.6 8.8 %collective-permute-start = (bf16[256,512]{1,0:T(8,128)(2,1)}, bf16[256,512]{1,0:T(8,128)(2,1)S(1)}, u32[]{:S(2)}, u32[]{:S(2)}) collective-permute-start(bf16[256,512]{1,0:T(8,128)(2,1)} %param.15), channel_id=1, source_target_pairs={{0,64},{64,0},{1,65},{65,1},{2,66},{66,2},{3,67},{67,3},{4,68},{68... | collective-permute-start | bytes 786440 | tf_op jit(solution)/shard_map/value_first/ppermute | solution.py:286
  9.5 11.3 %copy-start.7 = (bf16[128,4096]{1,0:T(8,128)(2,1)S(1)}, bf16[128,4096]{1,0:T(8,128)(2,1)}, u32[]{:S(2)}) copy-start(bf16[128,4096]{1,0:T(8,128)(2,1)} %param.13) | copy-start | bytes 3145732
  9.5 109.3 %all-to-all-start = ((bf16[128,8,4096]{2,1,0:T(8,128)(2,1)}), bf16[128,8,4096]{2,1,0:T(8,128)(2,1)}, u32[]{:S(2)}, u32[]{:S(2)}) async-start(bf16[128,8,4096]{2,1,0:T(8,128)(2,1)} %bitcast.75), calls=%async_computation | async-start | bytes 16777216 | tf_op jit(solution)/shard_map/dispatch/all_to_all | solution.py:29
  21.4 0.9 copy-start.3
  21.5 1.8 copy-start.10
  21.5 1.9 copy-start.12
  21.5 2.9 %copy-start.9 = (bf16[256,512]{1,0:T(8,128)(2,1)S(1)}, bf16[256,512]{1,0:T(8,128)(2,1)}, u32[]{:S(2)}) copy-start(bf16[256,512]{1,0:T(8,128)(2,1)} %param.15) | copy-start | bytes 786436
  23.2 5.2 %collective-permute-start.1 = (bf16[128,2560]{1,0:T(8,128)(2,1)}, bf16[128,2560]{1,0:T(8,128)(2,1)S(1)}, u32[]{:S(2)}, u32[]{:S(2)}) collective-permute-start(bf16[128,2560]{1,0:T(8,128)(2,1)} %pad_maximum_fusion.1), channel_id=1, source_target_pairs={{0,8},{8,0},{1,9},{9,1},{2,10},{10,2},{3,11},{11,3},{4,12},{12,4},... | collective-permute-start | bytes 1966088 | tf_op jit(solution)/shard_map/value_second/ppermute | solution.py:286
  25.5 111.2 %collective-permute-start.3 = (bf16[2,256,512]{2,1,0:T(8,128)(2,1)}, bf16[2,256,512]{2,1,0:T(8,128)(2,1)}, u32[]{:S(2)}, u32[]{:S(2)}) collective-permute-start(bf16[2,256,512]{2,1,0:T(8,128)(2,1)} %get-tuple-element.95), channel_id=1, source_target_pairs={{0,48},{16,0},{32,16},{48,32},{1,49},{17,1},{33,17},{49,33},{2,50}... | collective-permute-start | bytes 1572872 | tf_op jit(solution)/shard_map/value_second/ppermute | solution.py:286
  28.4 108.3 %collective-permute-start.2 = (bf16[2,256,512]{2,1,0:T(8,128)(2,1)}, bf16[2,256,512]{2,1,0:T(8,128)(2,1)}, u32[]{:S(2)}, u32[]{:S(2)}) collective-permute-start(bf16[2,256,512]{2,1,0:T(8,128)(2,1)} %get-tuple-element.95), channel_id=1, source_target_pairs={{0,16},{16,32},{32,48},{48,0},{1,17},{17,33},{33,49},{49,1},{2,18}... | collective-permute-start | bytes 1572872 | tf_op jit(solution)/shard_map/value_second/ppermute | solution.py:286
  29.4 5.8 %copy-start.11 = (s32[128,8]{0,1:T(8,128)S(1)}, s32[128,8]{0,1:T(8,128)}, u32[]{:S(2)}) copy-start(s32[128,8]{0,1:T(8,128)} %param.18) | copy-start | bytes 12292
  29.5 8.9 %copy-start.5 = (bf16[1,128,8,768]{3,2,1,0:T(8,128)(2,1)S(1)}, bf16[1,128,8,768]{3,2,1,0:T(8,128)(2,1)}, u32[]{:S(2)}) copy-start(bf16[1,128,8,768]{3,2,1,0:T(8,128)(2,1)} %param.21) | copy-start | bytes 4718596
  31.0 8.8 %copy-start.6 = (bf16[1,128,8,768]{3,2,1,0:T(8,128)(2,1)S(1)}, bf16[1,128,8,768]{3,2,1,0:T(8,128)(2,1)}, u32[]{:S(2)}) copy-start(bf16[1,128,8,768]{3,2,1,0:T(8,128)(2,1)} %param.22) | copy-start | bytes 4718596
  31.0 105.7 %collective-permute-start.6 = (bf16[256,1024]{1,0:T(8,128)(2,1)}, bf16[256,1024]{1,0:T(8,128)(2,1)}, u32[]{:S(2)}, u32[]{:S(2)}) collective-permute-start(bf16[256,1024]{1,0:T(8,128)(2,1)} %get-tuple-element.102), channel_id=1, source_target_pairs={{0,68},{4,64},{64,4},{68,0},{1,69},{5,65},{65,5},{69,1},{2,70},{6,... | collective-permute-start | bytes 1572872 | tf_op jit(solution)/shard_map/value_second/ppermute | solution.py:286
  33.8 103.0 %collective-permute-start.4 = (bf16[256,1024]{1,0:T(8,128)(2,1)}, bf16[256,1024]{1,0:T(8,128)(2,1)}, u32[]{:S(2)}, u32[]{:S(2)}) collective-permute-start(bf16[256,1024]{1,0:T(8,128)(2,1)} %get-tuple-element.103), channel_id=1, source_target_pairs={{0,4},{4,0},{64,68},{68,64},{1,5},{5,1},{65,69},{69,65},{2,6},{6,2... | collective-permute-start | bytes 1572872 | tf_op jit(solution)/shard_map/value_second/ppermute | solution.py:286
  34.6 102.2 %collective-permute-start.5 = (bf16[256,1024]{1,0:T(8,128)(2,1)}, bf16[256,1024]{1,0:T(8,128)(2,1)}, u32[]{:S(2)}, u32[]{:S(2)}) collective-permute-start(bf16[256,1024]{1,0:T(8,128)(2,1)} %get-tuple-element.104), channel_id=1, source_target_pairs={{0,64},{4,68},{64,0},{68,4},{1,65},{5,69},{65,1},{69,5},{2,66},{6,... | collective-permute-start | bytes 1572872 | tf_op jit(solution)/shard_map/value_second/ppermute | solution.py:286
  136.8 47.3 %all-to-all-start.2 = ((bf16[128,8,1152]{2,1,0:T(8,128)(2,1)}), bf16[128,8,1152]{2,1,0:T(8,128)(2,1)}, u32[]{:S(2)}, u32[]{:S(2)}) async-start(bf16[128,8,1152]{2,1,0:T(8,128)(2,1)} %bitcast.76), calls=%async_computation.2 | async-start | bytes 4718592 | tf_op jit(solution)/shard_map/return/all_to_all | solution.py:29
  151.5 1.0 copy-start
  155.4 37.4 %collective-permute-start.9 = (bf16[128,512]{1,0:T(8,128)(2,1)}, bf16[128,512]{1,0:T(8,128)(2,1)}, u32[]{:S(2)}, u32[]{:S(2)}) collective-permute-start(bf16[128,512]{1,0:T(8,128)(2,1)} %get-tuple-element.55), channel_id=1, source_target_pairs={{0,1},{1,2},{2,3},{3,0},{4,5},{5,6},{6,7},{7,4},{8,9},{9,10},{10,1... | collective-permute-start | bytes 393224 | tf_op jit(solution)/shard_map/value_third/ppermute | solution.py:286
  156.3 36.5 %collective-permute-start.10 = (bf16[128,512]{1,0:T(8,128)(2,1)}, bf16[128,512]{1,0:T(8,128)(2,1)}, u32[]{:S(2)}, u32[]{:S(2)}) collective-permute-start(bf16[128,512]{1,0:T(8,128)(2,1)} %get-tuple-element.56), channel_id=1, source_target_pairs={{0,2},{1,3},{2,0},{3,1},{4,6},{5,7},{6,4},{7,5},{8,10},{9,11},{10,... | collective-permute-start | bytes 393224 | tf_op jit(solution)/shard_map/value_third/ppermute | solution.py:286
  159.1 33.8 %collective-permute-start.11 = (bf16[128,512]{1,0:T(8,128)(2,1)}, bf16[128,512]{1,0:T(8,128)(2,1)}, u32[]{:S(2)}, u32[]{:S(2)}) collective-permute-start(bf16[128,512]{1,0:T(8,128)(2,1)} %get-tuple-element.57), channel_id=1, source_target_pairs={{0,3},{1,0},{2,1},{3,2},{4,7},{5,4},{6,5},{7,6},{8,11},{9,8},{10,9... | collective-permute-start | bytes 393224 | tf_op jit(solution)/shard_map/value_third/ppermute | solution.py:286
  162.1 30.7 %collective-permute-start.8 = (bf16[256,512]{1,0:T(8,128)(2,1)}, bf16[256,512]{1,0:T(8,128)(2,1)}, u32[]{:S(2)}, u32[]{:S(2)}) collective-permute-start(bf16[256,512]{1,0:T(8,128)(2,1)} %slice_bitcast_fusion), channel_id=1, source_target_pairs={{0,48},{16,0},{32,16},{48,32},{1,49},{17,1},{33,17},{49,33},{2,50}... | collective-permute-start | bytes 786440 | tf_op jit(solution)/shard_map/value_third/ppermute | solution.py:286
  167.3 25.6 %collective-permute-start.7 = (bf16[256,512]{1,0:T(8,128)(2,1)}, bf16[256,512]{1,0:T(8,128)(2,1)}, u32[]{:S(2)}, u32[]{:S(2)}) collective-permute-start(bf16[256,512]{1,0:T(8,128)(2,1)} %slice_bitcast_fusion.1), channel_id=1, source_target_pairs={{0,16},{16,32},{32,48},{48,0},{1,17},{17,33},{33,49},{49,1},{2,18}... | collective-permute-start | bytes 786440 | tf_op jit(solution)/shard_map/value_third/ppermute | solution.py:286
  184.1 6.0 %copy-start.1 = (bf16[128,1024]{1,0:T(8,128)(2,1)S(1)}, bf16[128,1024]{1,0:T(8,128)(2,1)}, u32[]{:S(2)}) copy-start(bf16[128,1024]{1,0:T(8,128)(2,1)} %mix_weights.1.mix_ref) | copy-start | bytes 786436
  184.1 80.9 %all-to-all-start.1 = ((bf16[128,8,3072]{2,1,0:T(8,128)(2,1)}), bf16[128,8,3072]{2,1,0:T(8,128)(2,1)}, u32[]{:S(2)}, u32[]{:S(2)}) async-start(bf16[128,8,3072]{2,1,0:T(8,128)(2,1)} %bitcast.78), calls=%async_computation.1 | async-start | bytes 12582912 | tf_op jit(solution)/shard_map/return/all_to_all | solution.py:29
  190.1 3.9 %copy-start.2 = (bf16[1,2,256,512]{3,2,1,0:T(8,128)(2,1)S(1)}, bf16[1,2,256,512]{3,2,1,0:T(8,128)(2,1)}, u32[]{:S(2)}) copy-start(bf16[1,2,256,512]{3,2,1,0:T(8,128)(2,1)} %get-tuple-element.94) | copy-start | bytes 1572868
  194.0 2.8 %copy-start.8 = (s32[128,8]{1,0:T(8,128)S(1)}, s32[128,8]{1,0:T(8,128)}, u32[]{:S(2)}) copy-start(s32[128,8]{1,0:T(8,128)} %broadcast_select_fusion.2.slot_ref) | copy-start | bytes 12292
  194.0 9.6 %copy-start.4 = (bf16[128,512]{1,0:T(8,128)(2,1)S(1)}, bf16[128,512]{1,0:T(8,128)(2,1)}, u32[]{:S(2)}) copy-start(bf16[128,512]{1,0:T(8,128)(2,1)} %param.14) | copy-start | bytes 393220
  195.5 8.8 %collective-permute-start.15 = (bf16[4,2,256,512]{3,2,1,0:T(8,128)(2,1)S(1)}, bf16[4,2,256,512]{3,2,1,0:T(8,128)(2,1)}, u32[]{:S(2)}, u32[]{:S(2)}) collective-permute-start(bf16[4,2,256,512]{3,2,1,0:T(8,128)(2,1)S(1)} %pad_maximum_fusion), channel_id=1, source_target_pairs={{0,8},{8,0},{1,9},{9,1},{2,10},{10,2},{3,11},{11,3},{4,12},{12,4},... | collective-permute-start | bytes 6291464 | tf_op jit(solution)/shard_map/value_last/ppermute | solution.py:286
  199.3 70.8 %collective-permute-start.14 = (f32[32,512]{1,0:T(8,128)S(1)}, f32[32,512]{1,0:T(8,128)S(1)}, u32[]{:S(2)}, u32[]{:S(2)}) collective-permute-start(f32[32,512]{1,0:T(8,128)S(1)} %get-tuple-element.98), channel_id=1, source_target_pairs={{0,48},{16,0},{32,16},{48,32},{1,49},{17,1},{33,17},{49,33},{2,50}... | collective-permute-start | bytes 196616 | tf_op jit(solution)/shard_map/value_last/ppermute | solution.py:286
  202.2 67.9 %collective-permute-start.13 = (f32[32,512]{1,0:T(8,128)S(1)}, f32[32,512]{1,0:T(8,128)S(1)}, u32[]{:S(2)}, u32[]{:S(2)}) collective-permute-start(f32[32,512]{1,0:T(8,128)S(1)} %get-tuple-element.99), channel_id=1, source_target_pairs={{0,32},{16,48},{32,0},{48,16},{1,33},{17,49},{33,1},{49,17},{2,34}... | collective-permute-start | bytes 196616 | tf_op jit(solution)/shard_map/value_last/ppermute | solution.py:286
  202.5 67.5 %collective-permute-start.12 = (f32[32,512]{1,0:T(8,128)S(1)}, f32[32,512]{1,0:T(8,128)S(1)}, u32[]{:S(2)}, u32[]{:S(2)}) collective-permute-start(f32[32,512]{1,0:T(8,128)S(1)} %get-tuple-element.100), channel_id=1, source_target_pairs={{0,16},{16,32},{32,48},{48,0},{1,17},{17,33},{33,49},{49,1},{2,18}... | collective-permute-start | bytes 196616 | tf_op jit(solution)/shard_map/value_last/ppermute | solution.py:286
